TPU v7x, 32 devices: a whole 2x2x4 slice. The times are simulated.
32 devices in a mesh: gx: 8 (over y, x, core), gy: 4 (over z).
Axes of the slice: x: 2, y: 2, z: 4, core: 2. Of those that a mesh axis runs over, the one named last changes fastest.
Arguments:
- state_in: float32 [4, 8192, 16, 128], P(None, ('gx', 'gy')), may hold values from -6 to 6
- stiffness: float32 [16, 16, 8192], P(None, None, ('gx', 'gy')), may hold values from -1.5 to 1.5
- elem_cell: int32 [8192], P(('gx', 'gy')), may hold values from 0 to 8191, as said below
- group_column: int32 [32768], P(('gx', 'gy')), may hold values from 0 to 32767, as said below
- group_inverse: bfloat16 [2048, 128, 128], P(('gx', 'gy')), may hold values from 0 to 0.875
Outputs:
- state_out: float32 [4, 8192, 16, 128], P(None, ('gx', 'gy'))
Inputs may be any that keep to these rules, and one draw needn't show every extreme that they name: `elem_cell`: device i * 4 + j (index i along gx, j along gy) holds in its 256 slots, in some order, exactly the cells with x from i * 16 to (i + 1) * 16 - 1 and y from j * 16 to (j + 1) * 16 - 1; every cell is held once. `group_column`: every column is named once. Column c lies on device c // 1024, slot p on device p // 1024; the 1024 slots of each device name exactly 32 columns of each device.
All inputs are finite; a program needn't handle non-finite values.
Results may differ from a plain program's by a relative error of at most 0.0031.
Values may be sent and summed in bfloat16 or wider, within the bound.
No kernel may reach another device: no remote copies, remote signals or barrier semaphores. Data moves between devices by JAX's collectives and lax.ppermute only.
A program may use at most 128 MiB of HBM per device.

v0:
```python
import functools
import math

import jax
import jax.numpy as jnp
import numpy as np
from jax import lax
from jax.experimental import pallas as pl
from jax.experimental.pallas import tpu as pltpu
from jax.sharding import PartitionSpec as P

GROUP_COLS = 16
EXD = 16
EYD = 16
NP = 16
F32 = jnp.float32
BF16 = jnp.bfloat16
I32 = jnp.int32
MB = 1024 * 1024


def lagrange_value(node_index, position, gll_nodes):
    running = 1.0
    for other_index in range(4):
        if other_index != node_index:
            running = (
                running
                * (position - gll_nodes[other_index])
                / (gll_nodes[node_index] - gll_nodes[other_index])
            )
    return running


def half_tables():
    gll_nodes = [-1.0, -1.0 / math.sqrt(5.0), 1.0 / math.sqrt(5.0), 1.0]
    halves = np.zeros((2, 4))
    for half_index, (lower_end, upper_end) in enumerate(((-1.0, 0.0), (0.0, 1.0))):
        centre = 0.5 * (lower_end + upper_end)
        offset = 0.5 * (upper_end - lower_end) / math.sqrt(3.0)
        for node in range(4):
            first = lagrange_value(node, centre - offset, gll_nodes)
            second = lagrange_value(node, centre + offset, gll_nodes)
            halves[half_index, node] = 0.5 * (upper_end - lower_end) * (first + second)
    product = halves @ halves.T
    determinant = product[0, 0] * product[1, 1] - product[0, 1] * product[1, 0]
    inverse = (
        np.array([[product[1, 1], -product[0, 1]], [-product[1, 0], product[0, 0]]]) / determinant
    )
    spread = halves.T @ inverse
    return halves.astype(np.float32), spread.astype(np.float32)


HALVES, SPREAD = half_tables()
ONE_D = np.array([0.5, 1.0, 1.0, 0.5])


def shift_down(n):
    return np.eye(n, k=-1)


def local_pass(n):
    table = np.einsum("ab,xy->axby", np.eye(4), np.eye(n))
    table[0, :, 3, :] += shift_down(n)
    table[3, :, 0, :] += shift_down(n).T
    return table


def constant_tables():
    h = HALVES.astype(np.float64)
    s = SPREAD.astype(np.float64)
    w = ONE_D
    eye = np.eye(EXD)
    line = local_pass(EYD)
    col_x = []
    for a in (0, 3):
        col_x.append(
            np.einsum("i,jb,b,byez->ijyez", h[:, a] * w[a], h, w, line).reshape(4 * EYD, 4 * EYD)
        )
    col_y = np.zeros((EXD, 2, 2, EYD, 2, 4, EXD))
    for side, (b, y) in enumerate(((0, 0), (3, EYD - 1))):
        col_y[:, :, :, y, side] = np.einsum("ia,j,xz->xijaz", h * w, h[:, b] * w[b], eye)
    col_y = col_y.reshape(EXD * 4 * EYD, 2 * 4 * EXD)
    nodes = np.einsum("ai,bj,yz->abyijz", s, s, np.eye(EYD))
    across = np.zeros((4, 4, EYD, 3, 2, 2, EYD))
    across[:, :, :, 1] = nodes
    across[0, :, :, 0] = nodes[3]
    across[3, :, :, 2] = nodes[0]
    full = np.einsum("byez,aezdijt->abydijt", line, across)
    full = full * w[:, None, None, None, None, None, None] * w[:, None, None, None, None, None]
    final = full.reshape(NP * EYD, 3 * 4 * EYD)
    along = local_pass(EXD)
    lines = np.zeros((2, 4, EXD, EXD, 2, 2, EYD))
    corner_col = np.zeros((2, 4, EXD, 2, 2, 2, EYD))
    corner_pt = np.zeros((2, 4, EXD, 2, 4, EYD))
    for side, (b, y) in enumerate(((0, 0), (3, EYD - 1))):
        lines[side, :, :, :, :, :, y] = np.einsum("axcz,ci,j->axzij", along, s, s[b])
        corner_col[side, 0, 0, 0, :, :, y] = np.outer(s[3], s[b])
        corner_col[side, 3, EXD - 1, 1, :, :, y] = np.outer(s[0], s[b])
        corner_pt[side, 0, 0, 0, b, y] = 1.0
        corner_pt[side, 3, EXD - 1, 1, b, y] = 1.0
    lines = lines.reshape(2 * 4 * EXD, EXD * 4 * EYD)
    corner_col = corner_col.reshape(2 * 4 * EXD, 2 * 4 * EYD)
    corner_pt = corner_pt.reshape(2 * 4 * EXD, 2 * 4 * EYD)
    border = np.zeros((4, EYD, NP, 128))
    order = full.transpose(2, 0, 1, 3, 4, 5, 6).reshape(EYD, NP, 3, 4 * EYD)
    west, east = hi_lo_arrays(order[:, :, 0]), hi_lo_arrays(order[:, :, 2])
    border[0] = np.concatenate(west, axis=-1)
    border[1] = np.concatenate(east, axis=-1)
    for side, b in enumerate((0, 3)):
        for a in range(4):
            for x in range(EXD):
                border[2 + side, x, 4 * a + b, 16 * a + x] = w[a] * w[b]
    return dict(
        col_x=np.concatenate(col_x, axis=0),
        col_y=col_y,
        final=order.reshape(EYD * NP, 3 * 4 * EYD),
        lines=lines,
        corner_col=corner_col,
        corner_pt=corner_pt,
        border=border.reshape(4 * EYD * NP, 128),
    )


def hi_lo_arrays(table):
    hi = np.asarray(table, np.float32).astype(jnp.bfloat16)
    lo = (np.asarray(table, np.float32) - hi.astype(np.float32)).astype(jnp.bfloat16)
    return hi, lo


def hi_lo(table):
    return jnp.asarray(np.concatenate(hi_lo_arrays(table), axis=1))


TABLES = constant_tables()


def dot(left, right):
    return jnp.dot(left, right, preferred_element_type=F32)


def dot_nt(left, right):
    return lax.dot_general(left, right, (((1,), (1,)), ((), ())), preferred_element_type=F32)


def dot_twice(table, right):
    return dot(table, jnp.concatenate([right, right], axis=0))


def split(values):
    hi = values.astype(BF16)
    return hi, (values - hi.astype(F32)).astype(BF16)


def iota(shape, dim):
    return lax.broadcasted_iota(I32, shape, dim)


def one_hot(condition):
    return jnp.where(condition, 1.0, 0.0).astype(BF16)


def as_columns(row, start):
    piece = row[:, start : start + 128].astype(F32)
    return jnp.transpose(jnp.broadcast_to(piece, (128, 128))).astype(I32)


def tile_number(cell, span_y):
    shift = span_y.bit_length() - 1
    assert span_y == 1 << shift
    return ((cell >> shift) & (EXD - 1)) * EYD + (cell & (EYD - 1))


VMEM = pl.BlockSpec(memory_space=pltpu.VMEM)
SMEM = pl.BlockSpec(memory_space=pltpu.SMEM)
ANY = pl.BlockSpec(memory_space=pl.ANY)


def params(mib):
    return pltpu.CompilerParams(vmem_limit_bytes=mib * MB)


def cost(flops, moved):
    return pl.CostEstimate(flops=int(flops), bytes_accessed=int(moved), transcendentals=0)


def request_kernel(devices, per_peer, group_ref, wanted_ref, q_ref):
    columns_dev = devices * per_peer
    shift = columns_dev.bit_length() - 1
    group = group_ref[...]
    source = group >> shift
    local = group & (columns_dev - 1)
    of_source = source == iota((devices, columns_dev), 0)
    marks = one_hot(of_source)
    upper = one_hot(iota((128, 128), 0) <= iota((128, 128), 1))
    before = jnp.zeros((devices, 1), F32)
    ranks = []
    for start in range(0, columns_dev, 128):
        piece = marks[:, start : start + 128]
        counts = dot(piece, upper) + before
        ranks.append(counts)
        before = counts[:, 127:128]
    counts = jnp.concatenate(ranks, axis=1)
    rank = jnp.sum(jnp.where(of_source, counts, 0.0), axis=0, keepdims=True).astype(I32) - 1
    q_ref[...] = source * per_peer + rank
    of_rank = one_hot(rank == iota((128, columns_dev), 0))
    high = jnp.where(of_source, (local >> 5).astype(F32), 0.0).astype(BF16)
    low = jnp.where(of_source, (local & 31).astype(F32), 0.0).astype(BF16)
    wanted = (dot_nt(high, of_rank) * 32.0 + dot_nt(low, of_rank)).astype(I32)
    wanted_ref[...] = jnp.broadcast_to(wanted[:, None, :], (devices, 8, 128))


def requests(group, devices):
    columns_dev = group.shape[1]
    return pl.pallas_call(
        functools.partial(request_kernel, devices, columns_dev // devices),
        out_shape=(
            jax.ShapeDtypeStruct((devices, 8, 128), I32),
            jax.ShapeDtypeStruct((1, columns_dev), I32),
        ),
        in_specs=[VMEM],
        out_specs=(VMEM,) * 2,
        compiler_params=params(16),
        cost_estimate=cost(2e7, 2e5),
        name="requests",
    )(group)


def operator_masks(rows):
    row, col = iota((rows, 256), 0), iota((rows, 256), 1)
    same_elem = one_hot((row & 15) == (col >> 4))
    row, col = iota((256, 256), 0), iota((256, 256), 1)
    tiling = one_hot((row & 15) == (col & 15))
    return tiling, same_elem


def operator_block(ktt, nodes, tiling, same_elem):
    parts = []
    column = iota((16, 256), 1) >> 4
    for part in split(ktt):
        part = part.astype(F32)
        stacked = jnp.concatenate(
            [jnp.where(column == n, part, 0.0).astype(BF16) for n in nodes], axis=0
        )
        parts.append(dot(stacked, tiling).astype(BF16) * same_elem)
    return parts


def apply_operator(operator, hi, lo):
    k_hi, k_lo = operator
    return dot(k_hi, hi) + dot(k_lo, hi) + dot(k_hi, lo)


def shifted(values, step):
    rows = values.shape[0]
    moved = pltpu.roll(values, step % rows, 0)
    free = 0 if step > 0 else rows - 1
    return jnp.where(iota(values.shape, 0) == free, 0.0, moved)


CHUNKS = 8


def front_kernel(
    fields,
    span_y,
    cell_smem,
    cell_ref,
    stiff_ref,
    state_ref,
    hi_ref,
    lo_ref,
    ktt_ref,
    slot_ref,
    west_ref,
    east_ref,
    south_ref,
    north_ref,
    buffer,
    sems,
):
    elements = cell_ref.shape[1]
    levels = state_ref.shape[3]
    per = elements // CHUNKS

    def copy(chunk):
        return pltpu.make_async_copy(
            state_ref.at[:, pl.ds(chunk * per, per)], buffer.at[chunk], sems.at[chunk]
        )

    for chunk in range(CHUNKS):
        copy(chunk).start()

    tile = tile_number(cell_ref[...], span_y)
    marks = one_hot(tile == iota((elements, elements), 0))
    pick = iota((64, elements), 0)
    kind = pick >> 4
    place = pick & 15
    edge_tile = jnp.where(
        kind == 0,
        place,
        jnp.where(
            kind == 1,
            place + (EXD - 1) * EYD,
            jnp.where(kind == 2, place * EYD, place * EYD + EYD - 1),
        ),
    )
    marks = jnp.concatenate([marks, one_hot(tile == edge_tile)], axis=0)
    stiff = stiff_ref[...]
    row = iota(stiff.shape, 0)
    stiff = stiff + jnp.where((row >> 4) == (row & 15), 1.0, 0.0)
    k_hi, k_lo = split(stiff)
    ktt = dot_nt(marks, k_hi) + dot_nt(marks, k_lo)
    ktt_ref[...] = ktt[0:elements]
    tiling, same_elem = operator_masks(64)
    nodes = ((0, 1, 2, 3), (12, 13, 14, 15), (0, 4, 8, 12), (3, 7, 11, 15))
    operators = [
        operator_block(
            ktt[elements + 16 * k : elements + 16 * k + 16], nodes[k], tiling, same_elem
        )
        for k in range(4)
    ]

    for chunk in range(CHUNKS):
        copy(chunk).wait()

        def place_slots(i, _, chunk=chunk):
            for u in range(4):
                k = i * 4 + u
                slot = chunk * per + k
                where = tile_number(cell_smem[slot], span_y)
                slot_ref[0, where] = slot
                for f in range(fields):
                    hi, lo = split(buffer[chunk, f, k])
                    hi_ref[where, :, f * levels : (f + 1) * levels] = hi
                    lo_ref[where, :, f * levels : (f + 1) * levels] = lo
            return 0

        lax.fori_loop(0, per // 4, place_slots, 0)

    for kind in range(4):
        if kind < 2:
            first = (0, (EXD - 1) * EYD)[kind]
            hi, lo = (
                part[first : first + EYD].reshape(EYD * NP, fields * levels)
                for part in (hi_ref, lo_ref)
            )
        else:
            y = (0, EYD - 1)[kind - 2]
            hi, lo = (
                jnp.concatenate([part[x * EYD + y] for x in range(EXD)], axis=0)
                for part in (hi_ref, lo_ref)
            )
        line = apply_operator(operators[kind], hi, lo)
        if kind == 0:
            west_ref[...] = line.astype(BF16)
        elif kind == 1:
            east_ref[...] = line.astype(BF16)
        else:
            first, last = line[0:16], line[48:64]
            out = (south_ref, north_ref)[kind - 2]
            out[0:16] = first + shifted(last, 1)
            out[16:48] = line[16:48]
            out[48:64] = last + shifted(first, -1)


def front(cell, stiff, state, span_y):
    fields, elements, _, levels = state.shape
    width = fields * levels
    return pl.pallas_call(
        functools.partial(front_kernel, fields, span_y),
        out_shape=(
            jax.ShapeDtypeStruct((elements, NP, width), BF16),
            jax.ShapeDtypeStruct((elements, NP, width), BF16),
            jax.ShapeDtypeStruct((elements, 256), F32),
            jax.ShapeDtypeStruct((1, elements), I32),
            jax.ShapeDtypeStruct((64, width), BF16),
            jax.ShapeDtypeStruct((64, width), BF16),
            jax.ShapeDtypeStruct((64, width), F32),
            jax.ShapeDtypeStruct((64, width), F32),
        ),
        in_specs=[SMEM, VMEM, VMEM, ANY],
        out_specs=(VMEM, VMEM, VMEM, SMEM, VMEM, VMEM, VMEM, VMEM),
        scratch_shapes=[
            pltpu.VMEM((CHUNKS, fields, elements // CHUNKS, NP, levels), F32),
            pltpu.SemaphoreType.DMA((CHUNKS,)),
        ],
        compiler_params=params(FRONT_LIMIT),
        cost_estimate=cost(8e8, 2e7),
        name="front",
    )(cell, cell.reshape(1, elements), stiff, state)


FRONT_LIMIT = 48


def row_kernel(emit_columns, *refs):
    ktt_ref, hi_ref, lo_ref = refs[:3]
    refs = refs[3:]
    if not emit_columns:
        hx_west, hx_east, hy_south, hy_north = refs[:4]
        refs = refs[4:]
    out_ref, held, before = refs[:3]
    width = held.shape[1]
    if not emit_columns:
        turned = refs[3]
        levels = turned.shape[2]
        fields = width // levels
    tiling, same_elem = operator_masks(256)

    def emit(row, next_first):
        nodes = [held[16 * n : 16 * n + 16] for n in range(NP)]
        for b in range(4):
            nodes[b] = nodes[b] + before[16 * b : 16 * b + 16]
            if next_first is not None:
                nodes[12 + b] = nodes[12 + b] + next_first[b]
        if emit_columns:
            along = [
                [
                    sum(float(HALVES[i, a] * ONE_D[a]) * nodes[4 * a + b] for a in range(4))
                    for b in range(4)
                ]
                for i in range(2)
            ]
            for i in range(2):
                for j in range(2):
                    out_ref[pl.ds(pl.multiple_of(row * 64 + (2 * i + j) * 16, 16), 16)] = sum(
                        float(HALVES[j, b] * ONE_D[b]) * along[i][b] for b in range(4)
                    )
        else:
            for a in range(4):
                at_row = pl.ds(16 * a + row, 1)
                for b in range(4):
                    n = 4 * a + b
                    values = nodes[n]
                    if b == 0:
                        values = values + jnp.where(
                            iota(values.shape, 0) == 0, hy_south[at_row], 0.0
                        )
                    if b == 3:
                        values = values + jnp.where(
                            iota(values.shape, 0) == 15, hy_north[at_row], 0.0
                        )
                    values = values * float(ONE_D[a] * ONE_D[b])
                    for f in range(fields):
                        turned[f, 16 * n : 16 * n + 16] = values[:, f * levels : (f + 1) * levels]
            for y in range(EYD):
                for f in range(fields):
                    out_ref[row * EYD + y, :, f * levels : (f + 1) * levels] = turned[
                        f, pl.ds(y, NP, stride=16)
                    ]

    before[...] = jnp.zeros_like(before)

    def one_row(row, _):
        operator = operator_block(
            ktt_ref[pl.ds(pl.multiple_of(row * 16, 16), 16)], range(NP), tiling, same_elem
        )
        at = pl.ds(pl.multiple_of(row * EYD, EYD), EYD)
        points = apply_operator(
            operator,
            hi_ref[at].reshape(EYD * NP, width),
            lo_ref[at].reshape(EYD * NP, width),
        )
        nodes = [points[16 * n : 16 * n + 16] for n in range(NP)]
        if not emit_columns:
            low = jnp.where(row == 0, 1.0, 0.0)
            high = jnp.where(row == EXD - 1, 1.0, 0.0)
            for b in range(4):
                rows = slice(16 * b, 16 * b + 16)
                nodes[b] = nodes[b] + hx_west[rows].astype(F32) * low
                nodes[12 + b] = nodes[12 + b] + hx_east[rows].astype(F32) * high
        for a in range(4):
            first, last = nodes[4 * a], nodes[4 * a + 3]
            nodes[4 * a] = first + shifted(last, 1)
            nodes[4 * a + 3] = last + shifted(first, -1)

        @pl.when(row > 0)
        def _():
            emit(row - 1, nodes[0:4])
            before[...] = held[192:256]

        for n in range(NP):
            held[16 * n : 16 * n + 16] = nodes[n]
        return 0

    lax.fori_loop(0, EXD, one_row, 0)
    emit(EXD - 1, None)


def rows_call(emit_columns, ktt, hi, lo, levels, halos=()):
    elements, _, width = hi.shape
    out = (
        jax.ShapeDtypeStruct((4 * elements, width), F32)
        if emit_columns
        else jax.ShapeDtypeStruct((elements, NP, width), F32)
    )
    scratch = [pltpu.VMEM((256, width), F32), pltpu.VMEM((64, width), F32)]
    if not emit_columns:
        scratch.append(pltpu.VMEM((width // levels, 256, levels), F32))
    return pl.pallas_call(
        functools.partial(row_kernel, emit_columns),
        out_shape=out,
        in_specs=[VMEM] * (3 + len(halos)),
        out_specs=VMEM,
        scratch_shapes=scratch,
        compiler_params=params(16),
        cost_estimate=cost(4e9, 2e7),
        name="column_rows" if emit_columns else "dynamics_rows",
    )(ktt, hi, lo, *halos)


def message_kernel(twice, west_ref, east_ref, south_ref, north_ref, table, to_south, to_north):
    both = jnp.concatenate([west_ref[...], east_ref[...]], axis=0)
    add = dot_twice(table[...], both) if twice else dot(table[...], both)
    to_south[...] = (south_ref[...] + add[0:64]).astype(BF16)
    to_north[...] = (north_ref[...] + add[64:128]).astype(BF16)


def messages(west, east, south, north, table):
    width = west.shape[1]
    return pl.pallas_call(
        functools.partial(message_kernel, table.shape[1] > 128),
        out_shape=(jax.ShapeDtypeStruct((64, width), BF16),) * 2,
        in_specs=[VMEM] * 5,
        out_specs=(VMEM,) * 2,
        compiler_params=params(16),
        cost_estimate=cost(4e7, 6e5),
        name="line_messages",
    )(west, east, south, north, table)


def ring(axis, step):
    count = lax.axis_size(axis)
    return [(i, (i + step) % count) for i in range(count)]


def exchange(axis, to_low, to_high):
    from_low = lax.ppermute(to_high, axis, ring(axis, 1))
    from_high = lax.ppermute(to_low, axis, ring(axis, -1))
    return from_low, from_high


def send_kernel(
    devices,
    span_y,
    columns_ref,
    west_ref,
    east_ref,
    south_ref,
    north_ref,
    table_ref,
    requested_ref,
    cell_ref,
    out_ref,
    place_ref,
    rounded,
):
    count = columns_ref.shape[0]
    per_peer = count // devices
    requested = requested_ref[:, 0, :]
    spread_out = one_hot((iota((128, count), 1) & (per_peer - 1)) == iota((128, count), 0))
    own = (iota((devices, count), 1) // per_peer) == iota((devices, count), 0)
    wide = dot((requested >> 5).astype(F32).astype(BF16), spread_out) * 32.0 + dot(
        (requested & 31).astype(F32).astype(BF16), spread_out
    )
    requested = jnp.sum(jnp.where(own, wide, 0.0), axis=0, keepdims=True).astype(I32)
    elements = cell_ref.shape[1]
    marks = one_hot((requested >> 2) == iota((elements, count), 0))
    tile_row = tile_number(cell_ref[...], span_y).astype(F32)
    tile_row = jnp.broadcast_to(tile_row, (8, elements)).astype(BF16)
    tile = dot(tile_row, marks)[0:1].astype(I32)
    place = (tile >> 4) * 64 + (requested & 3) * 16 + (tile & 15)
    place_ref[...] = place

    lines = jnp.concatenate([south_ref[...], north_ref[...]], axis=0)
    west = dot_twice(table_ref[count : count + 64, 0:128], west_ref[...])
    east = dot_twice(table_ref[count + 64 : count + 128, 0:128], east_ref[...])
    for start in range(0, count, 128):
        rows = slice(start, start + 128)
        values = columns_ref[rows] + dot_twice(table_ref[rows], lines)
        if start == 0:
            values = values + jnp.concatenate([west, jnp.zeros_like(west)], axis=0)
        if start == count - 128:
            values = values + jnp.concatenate([jnp.zeros_like(east), east], axis=0)
        rounded[rows] = values.astype(BF16)
    for start in range(0, count, 128):
        column = as_columns(place, start)
        pick = jnp.concatenate(
            [one_hot(column == iota((128, 128), 1) + other) for other in range(0, count, 128)],
            axis=1,
        )
        out_ref[start : start + 128] = dot(pick, rounded[...]).astype(BF16)


def send_columns(columns, halos, requested, cell, devices, span_y):
    count, width = columns.shape
    extra = np.concatenate(hi_lo_arrays(TABLES["col_x"]), axis=1)
    table = np.concatenate(hi_lo_arrays(TABLES["col_y"]), axis=1)
    table = np.concatenate([table, np.pad(extra, ((0, 0), (0, 128)))], axis=0)
    return pl.pallas_call(
        functools.partial(send_kernel, devices, span_y),
        out_shape=(
            jax.ShapeDtypeStruct((count, width), BF16),
            jax.ShapeDtypeStruct((1, count), I32),
        ),
        in_specs=[VMEM] * 8,
        out_specs=(VMEM,) * 2,
        scratch_shapes=[pltpu.VMEM((count, width), BF16)],
        compiler_params=params(16),
        cost_estimate=cost(2e9, 5e6),
        name="send_columns",
    )(columns, *halos, jnp.asarray(table), requested, cell)


def physics_kernel(fields, incoming_ref, q_ref, inverse_ref, out_ref, tendency):
    count, width = incoming_ref.shape
    levels = width // fields
    q = q_ref[...]
    for start in range(0, count, 128):
        column = as_columns(q, start)
        pick = jnp.concatenate(
            [one_hot(column == iota((128, 128), 1) + other) for other in range(0, count, 128)],
            axis=1,
        )
        physics = dot(pick, incoming_ref[...])
        for group in range(128 // GROUP_COLS):
            rows = physics[group * GROUP_COLS : (group + 1) * GROUP_COLS]
            stacked = jnp.concatenate(
                [rows[:, f * levels : (f + 1) * levels] for f in range(fields)], axis=0
            )
            inverse = inverse_ref[start // GROUP_COLS + group]
            result = dot_nt(stacked.astype(BF16), inverse) - stacked
            where = start + group * GROUP_COLS
            tendency[where : where + GROUP_COLS] = jnp.concatenate(
                [result[f * GROUP_COLS : (f + 1) * GROUP_COLS] for f in range(fields)], axis=1
            ).astype(BF16)
    for start in range(0, count, 128):
        pick = one_hot(q == iota((128, count), 0) + start)
        out_ref[start : start + 128] = dot(pick, tendency[...]).astype(BF16)


def physics_step(incoming, q, inverse, fields):
    count, width = incoming.shape
    return pl.pallas_call(
        functools.partial(physics_kernel, fields),
        out_shape=jax.ShapeDtypeStruct((count, width), BF16),
        in_specs=[VMEM] * 3,
        out_specs=VMEM,
        scratch_shapes=[pltpu.VMEM((count, width), BF16)],
        compiler_params=params(16),
        cost_estimate=cost(3e9, 5e6),
        name="physics",
    )(incoming, q, inverse)


def unpack_kernel(
    received_ref, place_ref, lines_table, back_ref, west_ref, east_ref, south_ref, north_ref
):
    count = received_ref.shape[0]
    place = place_ref[...]
    for start in range(0, count, 128):
        pick = one_hot(place == iota((128, count), 0) + start)
        back_ref[start : start + 128] = dot(pick, received_ref[...]).astype(BF16)
    west_ref[...] = back_ref[0:64]
    east_ref[...] = back_ref[count - 64 : count]
    lines = dot(lines_table[:, 0:count], back_ref[...]) + dot(
        lines_table[:, count : 2 * count], back_ref[...]
    )
    south_ref[...] = lines[0:64]
    north_ref[...] = lines[64:128]


def unpack(received, place):
    count, width = received.shape
    return pl.pallas_call(
        unpack_kernel,
        out_shape=(
            jax.ShapeDtypeStruct((count, width), BF16),
            jax.ShapeDtypeStruct((64, width), BF16),
            jax.ShapeDtypeStruct((64, width), BF16),
            jax.ShapeDtypeStruct((64, width), F32),
            jax.ShapeDtypeStruct((64, width), F32),
        ),
        in_specs=[VMEM] * 3,
        out_specs=(VMEM,) * 5,
        compiler_params=params(16),
        cost_estimate=cost(2e9, 4e6),
        name="unpack",
    )(received, place, hi_lo(TABLES["lines"]))


def inner_kernel(
    fields, span_y, cell_smem, dynamics_ref, back_ref, table_ref, out_ref, border_ref, total, buffer, sems
):
    elements, _, width = dynamics_ref.shape
    levels = width // fields
    count = back_ref.shape[0]
    depth = 192

    def near_sum(row, first, rows, skip):
        near = back_ref[pl.ds(first, rows)]
        sums = dot(table_ref[:, skip : skip + rows], near)
        sums = sums + dot(table_ref[:, depth + skip : depth + skip + rows], near)
        at = pl.ds(row * EYD, EYD)
        total[at] = dynamics_ref[at] + sums.reshape(EYD, NP, width)

    near_sum(0, 0, 128, 64)
    near_sum(EXD - 1, count - 128, 128, 0)

    def middle(row, _):
        near_sum(row, pl.multiple_of(row * 64 - 64, 64), 192, 0)
        return 0

    lax.fori_loop(1, EXD - 1, middle, 0)
    for kind in range(4):
        for k in range(16):
            tile = (k, (EXD - 1) * EYD + k, k * EYD, k * EYD + EYD - 1)[kind]
            for f in range(fields):
                border_ref[kind, f, k] = total[tile, :, f * levels : (f + 1) * levels]
    per = elements // CHUNKS

    def copy(chunk):
        return pltpu.make_async_copy(
            buffer.at[chunk], out_ref.at[:, pl.ds(chunk * per, per)], sems.at[chunk]
        )

    for chunk in range(CHUNKS):

        def take_slots(i, _, chunk=chunk):
            for u in range(4):
                k = i * 4 + u
                tile = tile_number(cell_smem[chunk * per + k], span_y)
                for f in range(fields):
                    buffer[chunk, f, k] = total[tile, :, f * levels : (f + 1) * levels]
            return 0

        lax.fori_loop(0, per // 4, take_slots, 0)
        copy(chunk).start()
    for chunk in range(CHUNKS):
        copy(chunk).wait()


def inner_sum(cell, dynamics, back, fields, span_y):
    elements, _, width = dynamics.shape
    levels = width // fields
    return pl.pallas_call(
        functools.partial(inner_kernel, fields, span_y),
        out_shape=(
            jax.ShapeDtypeStruct((fields, elements, NP, levels), F32),
            jax.ShapeDtypeStruct((4, fields, 16, NP, levels), F32),
        ),
        in_specs=[SMEM, VMEM, VMEM, VMEM],
        out_specs=(ANY, VMEM),
        scratch_shapes=[
            pltpu.VMEM((elements, NP, width), F32),
            pltpu.VMEM((CHUNKS, fields, elements // CHUNKS, NP, levels), F32),
            pltpu.SemaphoreType.DMA((CHUNKS,)),
        ],
        compiler_params=params(32),
        cost_estimate=cost(2e9, 2e7),
        name="inner_sum",
    )(cell, dynamics, back, hi_lo(TABLES["final"]))


def border_kernel(
    fields, slot_ref, west_ref, east_ref, south_ref, north_ref, border_ref, table_ref, _, out_ref, buffer, sem
):
    width = west_ref.shape[1]
    levels = width // fields
    adds = []
    for kind, ref in enumerate((west_ref, east_ref, south_ref, north_ref)):
        table = table_ref[kind * 256 : kind * 256 + 256]
        if kind < 2:
            add = dot_twice(table, ref[...])
        else:
            add = dot(table[:, 0:64], ref[...])
        adds.append(add.reshape(16, NP, width))
    for kind in range(4):
        for k in range(16):
            if kind >= 2 and k in (0, 15):
                continue
            add = adds[kind][k]
            if kind < 2 and k in (0, 15):
                add = add + adds[2 if k == 0 else 3][0 if kind == 0 else 15]
            for f in range(fields):
                buffer[kind, f, k] = border_ref[kind, f, k] + add[:, f * levels : (f + 1) * levels]
            tile = (k, (EXD - 1) * EYD + k, k * EYD, k * EYD + EYD - 1)[kind]
            pltpu.make_async_copy(
                buffer.at[kind, :, k], out_ref.at[:, slot_ref[0, tile]], sem.at[kind]
            ).start()
    for kind in range(4):
        part = buffer.at[kind] if kind < 2 else buffer.at[kind, :, 1:15]
        pltpu.make_async_copy(part, part, sem.at[kind]).wait()


def border_sum(slot, halos, border, out):
    fields, levels = out.shape[0], out.shape[3]
    table = jnp.asarray(TABLES["border"].astype(np.float32).astype(jnp.bfloat16))
    return pl.pallas_call(
        functools.partial(border_kernel, fields),
        out_shape=jax.ShapeDtypeStruct(out.shape, F32),
        in_specs=[SMEM] + [VMEM] * 6 + [ANY],
        out_specs=ANY,
        scratch_shapes=[
            pltpu.VMEM((4, fields, 16, NP, levels), F32),
            pltpu.SemaphoreType.DMA((4,)),
        ],
        input_output_aliases={7: 0},
        compiler_params=params(16),
        cost_estimate=cost(2e8, 4e6),
        name="border_sum",
    )(slot, *halos, border, table, out)


def regroup(blocks):
    return lax.all_to_all(blocks, ("gx", "gy"), split_axis=0, concat_axis=0, tiled=True)


def per_device(state_in, stiffness, elem_cell, group_column, group_inverse):
    fields, elements, _, levels = state_in.shape
    devices = lax.axis_size("gx") * lax.axis_size("gy")
    columns_dev = 4 * elements
    span_y = EYD * lax.axis_size("gy")

    wanted, q = requests(group_column.reshape(1, columns_dev), devices)
    requested = regroup(wanted)
    hi, lo, ktt, slot, to_west, to_east, south, north = front(
        elem_cell, stiffness.reshape(NP * NP, elements), state_in, span_y
    )
    hx = exchange("gx", to_west, to_east)
    columns = rows_call(True, ktt, hi, lo, levels)
    corner = jnp.asarray(TABLES["corner_pt"].astype(np.float32).astype(jnp.bfloat16))
    hy = exchange("gy", *messages(*hx, south, north, corner))

    outgoing, place = send_columns(
        columns, (*hx, *hy), requested, elem_cell.reshape(1, elements), devices, span_y
    )
    incoming = regroup(outgoing)
    halos = (*hx, hy[0].astype(F32), hy[1].astype(F32))
    dynamics = rows_call(False, ktt, hi, lo, levels, halos)
    incoming, dynamics = lax.optimization_barrier((incoming, dynamics))
    received = regroup(physics_step(incoming, q, group_inverse, fields))

    back, west, east, south, north = unpack(received, place)
    bx = exchange("gx", west, east)
    by = exchange("gy", *messages(*bx, south, north, hi_lo(TABLES["corner_col"])))
    inner, border = inner_sum(elem_cell, dynamics, back, fields, span_y)
    return border_sum(slot, (*bx, *by), border, inner)


def solution(mesh):
    placed = (
        P(None, ("gx", "gy"), None, None),
        P(None, None, ("gx", "gy")),
        P(("gx", "gy")),
        P(("gx", "gy")),
        P(("gx", "gy"), None, None),
    )
    return jax.shard_map(
        per_device,
        mesh=mesh,
        in_specs=placed,
        out_specs=P(None, ("gx", "gy"), None, None),
        check_vma=False,
    )
```

profile of v0, /device:TPU:0, one launch (start us, length us, event | category | flops | bytes accessed | tf_op | source)
XLA Modules:
  0.0 132.4 jit_solution(7231747689070072001)
XLA Ops:
  1.6 6.6 %front.1 = (bf16[256,16,512]{2,1,0:T(8,128)(2,1)S(1)}, bf16[256,16,512]{2,1,0:T(8,128)(2,1)}, f32[256,256]{1,0:T(8,128)S(1)}, s32[1,256]{1,0:T(1,128)S(1)}, bf16...) custom-call(s32[256]{0:T(256)S(1)} %copy-done.12, ...), custom_call_target="tpu_custom_call" | custom-call | flops 800000000 | bytes 20000000 | tf_op jit(solution)/shard_map/front/pallas_call | solution.py:369
  8.3 2.0 %copy-done.2 = bf16[256,16,512]{2,1,0:T(8,128)(2,1)} copy-done((bf16[256,16,512]{2,1,0:T(8,128)(2,1)}, bf16[256,16,512]{2,1,0:T(8,128)(2,1)S(1)}, u32[]{:S(2)}) %copy-start.2) | copy-done | bytes 4194328
  10.7 2.9 %collective-permute-start.1 = (bf16[64,512]{1,0:T(8,128)(2,1)S(1)}, bf16[64,512]{1,0:T(8,128)(2,1)S(1)}, u32[]{:S(2)}, u32[]{:S(2)}) collective-permute-start(bf16[64,512]{1,0:T(8,128)(2,1)S(1)} %get-tuple-element.35), channel_id=1, source_target_pairs={{0,28},{4,0},{8,4},{12,8},{16,12},{20,16},{24,20},{28,24},{1,29},{... | collective-permute-start | bytes 196616 | tf_op jit(solution)/shard_map/ppermute | solution.py:539
  15.0 5.7 %all-to-all-start = ((s32[32,8,128]{2,1,0:T(8,128)}), s32[32,8,128]{2,1,0:T(8,128)S(1)}, u32[]{:S(2)}, u32[]{:S(2)}) async-start(s32[32,8,128]{2,1,0:T(8,128)} %get-tuple-element.40), calls=%async_computation | async-start | bytes 262144 | tf_op jit(solution)/shard_map/all_to_all | solution.py:816
  20.9 1.8 %collective-permute-start.2 = (bf16[64,512]{1,0:T(8,128)(2,1)S(1)}, bf16[64,512]{1,0:T(8,128)(2,1)S(1)}, u32[]{:S(2)}, u32[]{:S(2)}) collective-permute-start(bf16[64,512]{1,0:T(8,128)(2,1)S(1)} %get-tuple-element.38), channel_id=1, source_target_pairs={{0,1},{1,2},{2,3},{3,0},{4,5},{5,6},{6,7},{7,4},{8,9},{9,10},{10,1... | collective-permute-start | bytes 196616 | tf_op jit(solution)/shard_map/ppermute | solution.py:538
  22.8 2.1 %collective-permute-start.3 = (bf16[64,512]{1,0:T(8,128)(2,1)S(1)}, bf16[64,512]{1,0:T(8,128)(2,1)S(1)}, u32[]{:S(2)}, u32[]{:S(2)}) collective-permute-start(bf16[64,512]{1,0:T(8,128)(2,1)S(1)} %get-tuple-element.39), channel_id=1, source_target_pairs={{0,3},{1,0},{2,1},{3,2},{4,7},{5,4},{6,5},{7,6},{8,11},{9,8},{10,9... | collective-permute-start | bytes 196616 | tf_op jit(solution)/shard_map/ppermute | solution.py:539
  24.8 2.2 %copy-done.3 = bf16[256,16,512]{2,1,0:T(8,128)(2,1)S(1)} copy-done((bf16[256,16,512]{2,1,0:T(8,128)(2,1)S(1)}, bf16[256,16,512]{2,1,0:T(8,128)(2,1)}, u32[]{:S(2)}) %copy-start.3) | copy-done | bytes 4194328
  27.0 2.2 %copy-done.5 = bf16[256,16,512]{2,1,0:T(8,128)(2,1)S(1)} copy-done((bf16[256,16,512]{2,1,0:T(8,128)(2,1)S(1)}, bf16[256,16,512]{2,1,0:T(8,128)(2,1)}, u32[]{:S(2)}) %copy-start.5) | copy-done | bytes 4194328
  29.2 10.7 %column_rows.1.columns_ref = f32[1024,512]{1,0:T(8,128)S(1)} custom-call(f32[256,256]{1,0:T(8,128)S(1)} %get-tuple-element.31.refs_0_, bf16[256,16,512]{2,1,0:T(8,128)(2,1)S(1)} %copy-done.3, bf16[256,16,512]{2,1,0:T(8,128)(2,1)S(1)} %copy-done.5), custom_call_target="tpu_custom_call" | custom-call | flops 4000000000 | bytes 20000000 | tf_op jit(solution)/shard_map/column_rows/pallas_call | solution.py:500
  42.9 3.0 %send_columns.1 = (bf16[1024,512]{1,0:T(8,128)(2,1)}, s32[1,1024]{1,0:T(1,128)S(1)}) custom-call(f32[1024,512]{1,0:T(8,128)S(1)} %copy-done.19, bf16[64,512]{1,0:T(8,128)(2,1)S(1)} %collective-permute-done.west_ref.refs_3_, bf16[64,512]{1,0:T(8,128)(2,1)S(1)} %collective-permute-done.1.east_ref.refs_4_, ...), custom_call_target="tpu_custom_call" | custom-call | flops 2000000000 | bytes 5000000 | tf_op jit(solution)/shard_map/send_columns/pallas_call | solution.py:600
  45.9 4.0 %all-to-all-start.1 = ((bf16[32,32,512]{2,1,0:T(8,128)(2,1)}), bf16[32,32,512]{2,1,0:T(8,128)(2,1)S(1)}, u32[]{:S(2)}, u32[]{:S(2)}) async-start(bf16[32,32,512]{2,1,0:T(8,128)(2,1)} %bitcast.3), calls=%async_computation.1 | async-start | bytes 2097152 | tf_op jit(solution)/shard_map/all_to_all | solution.py:816
  49.9 2.2 %copy-done.4 = bf16[256,16,512]{2,1,0:T(8,128)(2,1)S(1)} copy-done((bf16[256,16,512]{2,1,0:T(8,128)(2,1)S(1)}, bf16[256,16,512]{2,1,0:T(8,128)(2,1)}, u32[]{:S(2)}) %copy-start.4) | copy-done | bytes 4194328
  52.1 2.2 %copy-done.6 = bf16[256,16,512]{2,1,0:T(8,128)(2,1)S(1)} copy-done((bf16[256,16,512]{2,1,0:T(8,128)(2,1)S(1)}, bf16[256,16,512]{2,1,0:T(8,128)(2,1)}, u32[]{:S(2)}) %copy-start.6) | copy-done | bytes 4194328
  54.3 12.4 %dynamics_rows.1.dynamics_ref = f32[256,16,512]{2,1,0:T(8,128)S(1)} custom-call(f32[256,256]{1,0:T(8,128)S(1)} %get-tuple-element.31.refs_0_, bf16[256,16,512]{2,1,0:T(8,128)(2,1)S(1)} %copy-done.4, bf16[256,16,512]{2,1,0:T(8,128)(2,1)S(1)} %copy-done.6, bf16[64,512]{1,0:T(8,128)(2,1)S(1)} %collective-permute-done.west_ref.refs_3_, ...), custom_call_target="tpu_custom_call" | custom-call | flops 4000000000 | bytes 20000000 | tf_op jit(solution)/shard_map/dynamics_rows/pallas_call | solution.py:500
  66.7 3.4 %copy-done = f32[256,16,512]{2,1,0:T(8,128)} copy-done((f32[256,16,512]{2,1,0:T(8,128)}, f32[256,16,512]{2,1,0:T(8,128)S(1)}, u32[]{:S(2)}) %copy-start) | copy-done | bytes 8388632
  70.1 4.8 %all-to-all-done.1 = bf16[32,32,512]{2,1,0:T(8,128)(2,1)S(1)} async-done(((bf16[32,32,512]{2,1,0:T(8,128)(2,1)}), bf16[32,32,512]{2,1,0:T(8,128)(2,1)S(1)}, u32[]{:S(2)}, u32[]{:S(2)}) %all-to-all-start.1) | async-done | bytes 1048608 | tf_op jit(solution)/shard_map/all_to_all | solution.py:816
  75.0 1.6 %copy-done.14 = bf16[64,128,128]{2,1,0:T(8,128)(2,1)S(1)} copy-done((bf16[64,128,128]{2,1,0:T(8,128)(2,1)S(1)}, bf16[64,128,128]{2,1,0:T(8,128)(2,1)}, u32[]{:S(2)}) %copy-start.14) | copy-done | bytes 2097176
  76.5 4.7 %physics.1 = bf16[1024,512]{1,0:T(8,128)(2,1)S(1)} custom-call(bf16[1024,512]{1,0:T(8,128)(2,1)S(1)} %bitcast.7, s32[1,1024]{1,0:T(1,128)S(1)} %get-tuple-element.43.q_ref, bf16[64,128,128]{2,1,0:T(8,128)(2,1)S(1)} %copy-done.14), custom_call_target="tpu_custom_call" | custom-call | flops 3000000000 | bytes 5000000 | tf_op jit(solution)/shard_map/physics/pallas_call | solution.py:644
  81.2 29.3 %all_to_all.28 = bf16[32,32,512]{2,1,0:T(8,128)(2,1)S(1)} all-to-all(bf16[32,32,512]{2,1,0:T(8,128)(2,1)S(1)} %bitcast.9), channel_id=1, replica_groups=mesh['gx'=8,'gy'=4] {'gx','gy'}, dimensions={0} | all-to-all | bytes 2097152 | tf_op jit(solution)/shard_map/all_to_all | solution.py:816
  112.2 1.6 %collective-permute-start.4 = (bf16[64,512]{1,0:T(8,128)(2,1)S(1)}, bf16[64,512]{1,0:T(8,128)(2,1)S(1)}, u32[]{:S(2)}, u32[]{:S(2)}) collective-permute-start(bf16[64,512]{1,0:T(8,128)(2,1)S(1)} %get-tuple-element.45), channel_id=1, source_target_pairs={{0,4},{4,8},{8,12},{12,16},{16,20},{20,24},{24,28},{28,0},{1,5},{5... | collective-permute-start | bytes 196616 | tf_op jit(solution)/shard_map/ppermute | solution.py:538
  114.9 1.9 %collective-permute-done.4.west_ref = bf16[64,512]{1,0:T(8,128)(2,1)S(1)} collective-permute-done((bf16[64,512]{1,0:T(8,128)(2,1)S(1)}, bf16[64,512]{1,0:T(8,128)(2,1)S(1)}, u32[]{:S(2)}, u32[]{:S(2)}) %collective-permute-start.4) | collective-permute-done | bytes 65568 | tf_op jit(solution)/shard_map/ppermute | solution.py:538
  117.0 3.8 %collective-permute-start.6 = (bf16[64,512]{1,0:T(8,128)(2,1)S(1)}, bf16[64,512]{1,0:T(8,128)(2,1)S(1)}, u32[]{:S(2)}, u32[]{:S(2)}) collective-permute-start(bf16[64,512]{1,0:T(8,128)(2,1)S(1)} %get-tuple-element.49), channel_id=1, source_target_pairs={{0,1},{1,2},{2,3},{3,0},{4,5},{5,6},{6,7},{7,4},{8,9},{9,10},{10,1... | collective-permute-start | bytes 196616 | tf_op jit(solution)/shard_map/ppermute | solution.py:538
  120.9 9.3 %inner_sum.1 = (f32[4,256,16,128]{3,2,1,0:T(8,128)}, f32[4,4,16,16,128]{4,3,2,1,0:T(8,128)S(1)}) custom-call(s32[256]{0:T(256)S(1)} %copy-done.13, f32[256,16,512]{2,1,0:T(8,128)S(1)} %copy-done.1, bf16[1024,512]{1,0:T(8,128)(2,1)S(1)} %get-tuple-element.52.back_ref, bf16[256,384]{1,0:T(8,128)(2,1)S(1)} %copy-done.9), custom_call_target="tpu_custom_call" | custom-call | flops 2000000000 | bytes 20000000 | tf_op jit(solution)/shard_map/inner_sum/pallas_call | solution.py:746
  130.3 2.1 %border_sum.1 = f32[4,256,16,128]{3,2,1,0:T(8,128)} custom-call(s32[1,256]{1,0:T(1,128)S(1)} %get-tuple-element.30.slot_ref, bf16[64,512]{1,0:T(8,128)(2,1)S(1)} %collective-permute-done.4.west_ref, bf16[64,512]{1,0:T(8,128)(2,1)S(1)} %collective-permute-done.5.east_ref, ...), custom_call_target="tpu_custom_call", output_to_operand_aliasing={{}: (7, {})} | custom-call | flops 200000000 | bytes 4000000 | tf_op jit(solution)/shard_map/border_sum/pallas_call | solution.py:799
  (50 shorter events, 9.7 us)
Async XLA Ops:
  1.6 11.9 %copy-start.15 = (s32[1024]{0:T(1024)S(1)}, s32[1024]{0:T(1024)}, u32[]{:S(2)}) copy-start(s32[1024]{0:T(1024)} %param.14) | copy-start | bytes 12292
  1.6 19.1 %copy-start.11 = (bf16[128,128]{1,0:T(8,128)(2,1)S(1)}, bf16[128,128]{1,0:T(8,128)(2,1)}, u32[]{:S(2)}) copy-start(bf16[128,128]{1,0:T(8,128)(2,1)} %constant.12.clone.table) | copy-start | bytes 98308
  10.2 10.5 %collective-permute-start = (bf16[64,512]{1,0:T(8,128)(2,1)S(1)}, bf16[64,512]{1,0:T(8,128)(2,1)S(1)}, u32[]{:S(2)}, u32[]{:S(2)}) collective-permute-start(bf16[64,512]{1,0:T(8,128)(2,1)S(1)} %get-tuple-element.34), channel_id=1, source_target_pairs={{0,4},{4,8},{8,12},{12,16},{16,20},{20,24},{24,28},{28,0},{1,5},{5... | collective-permute-start | bytes 196616 | tf_op jit(solution)/shard_map/ppermute | solution.py:538
  10.7 10.1 %collective-permute-start.1 = (bf16[64,512]{1,0:T(8,128)(2,1)S(1)}, bf16[64,512]{1,0:T(8,128)(2,1)S(1)}, u32[]{:S(2)}, u32[]{:S(2)}) collective-permute-start(bf16[64,512]{1,0:T(8,128)(2,1)S(1)} %get-tuple-element.35), channel_id=1, source_target_pairs={{0,28},{4,0},{8,4},{12,8},{16,12},{20,16},{24,20},{28,24},{1,29},{... | collective-permute-start | bytes 196616 | tf_op jit(solution)/shard_map/ppermute | solution.py:539
  15.0 26.3 %all-to-all-start = ((s32[32,8,128]{2,1,0:T(8,128)}), s32[32,8,128]{2,1,0:T(8,128)S(1)}, u32[]{:S(2)}, u32[]{:S(2)}) async-start(s32[32,8,128]{2,1,0:T(8,128)} %get-tuple-element.40), calls=%async_computation | async-start | bytes 262144 | tf_op jit(solution)/shard_map/all_to_all | solution.py:816
  20.9 20.3 %collective-permute-start.2 = (bf16[64,512]{1,0:T(8,128)(2,1)S(1)}, bf16[64,512]{1,0:T(8,128)(2,1)S(1)}, u32[]{:S(2)}, u32[]{:S(2)}) collective-permute-start(bf16[64,512]{1,0:T(8,128)(2,1)S(1)} %get-tuple-element.38), channel_id=1, source_target_pairs={{0,1},{1,2},{2,3},{3,0},{4,5},{5,6},{6,7},{7,4},{8,9},{9,10},{10,1... | collective-permute-start | bytes 196616 | tf_op jit(solution)/shard_map/ppermute | solution.py:538
  22.8 18.5 %collective-permute-start.3 = (bf16[64,512]{1,0:T(8,128)(2,1)S(1)}, bf16[64,512]{1,0:T(8,128)(2,1)S(1)}, u32[]{:S(2)}, u32[]{:S(2)}) collective-permute-start(bf16[64,512]{1,0:T(8,128)(2,1)S(1)} %get-tuple-element.39), channel_id=1, source_target_pairs={{0,3},{1,0},{2,1},{3,2},{4,7},{5,4},{6,5},{7,6},{8,11},{9,8},{10,9... | collective-permute-start | bytes 196616 | tf_op jit(solution)/shard_map/ppermute | solution.py:539
  24.8 2.2 %copy-start.3 = (bf16[256,16,512]{2,1,0:T(8,128)(2,1)S(1)}, bf16[256,16,512]{2,1,0:T(8,128)(2,1)}, u32[]{:S(2)}) copy-start(bf16[256,16,512]{2,1,0:T(8,128)(2,1)} %copy-done.2) | copy-start | bytes 12582916
  27.0 2.2 %copy-start.5 = (bf16[256,16,512]{2,1,0:T(8,128)(2,1)S(1)}, bf16[256,16,512]{2,1,0:T(8,128)(2,1)}, u32[]{:S(2)}) copy-start(bf16[256,16,512]{2,1,0:T(8,128)(2,1)} %get-tuple-element.33.refs_2_) | copy-start | bytes 12582916
  29.2 12.1 %copy-start.13 = (s32[256]{0:T(256)S(1)}, s32[256]{0:T(256)}, u32[]{:S(2)}) copy-start(s32[256]{0:T(256)} %cell_smem.3) | copy-start | bytes 3076
  29.2 12.1 %copy-start.16 = (bf16[1152,256]{1,0:T(8,128)(2,1)S(1)}, bf16[1152,256]{1,0:T(8,128)(2,1)}, u32[]{:S(2)}) copy-start(bf16[1152,256]{1,0:T(8,128)(2,1)} %constant.13.clone.table_ref) | copy-start | bytes 1769476
  45.9 29.1 %all-to-all-start.1 = ((bf16[32,32,512]{2,1,0:T(8,128)(2,1)}), bf16[32,32,512]{2,1,0:T(8,128)(2,1)S(1)}, u32[]{:S(2)}, u32[]{:S(2)}) async-start(bf16[32,32,512]{2,1,0:T(8,128)(2,1)} %bitcast.3), calls=%async_computation.1 | async-start | bytes 2097152 | tf_op jit(solution)/shard_map/all_to_all | solution.py:816
  49.9 2.2 %copy-start.4 = (bf16[256,16,512]{2,1,0:T(8,128)(2,1)S(1)}, bf16[256,16,512]{2,1,0:T(8,128)(2,1)}, u32[]{:S(2)}) copy-start(bf16[256,16,512]{2,1,0:T(8,128)(2,1)} %copy-done.2) | copy-start | bytes 12582916
  52.1 2.2 %copy-start.6 = (bf16[256,16,512]{2,1,0:T(8,128)(2,1)S(1)}, bf16[256,16,512]{2,1,0:T(8,128)(2,1)}, u32[]{:S(2)}) copy-start(bf16[256,16,512]{2,1,0:T(8,128)(2,1)} %get-tuple-element.33.refs_2_) | copy-start | bytes 12582916
  66.7 3.4 %copy-start = (f32[256,16,512]{2,1,0:T(8,128)}, f32[256,16,512]{2,1,0:T(8,128)S(1)}, u32[]{:S(2)}) copy-start(f32[256,16,512]{2,1,0:T(8,128)S(1)} %dynamics_rows.1.dynamics_ref) | copy-start | bytes 25165828
  76.5 34.0 %copy-start.17 = (bf16[128,2048]{1,0:T(8,128)(2,1)S(1)}, bf16[128,2048]{1,0:T(8,128)(2,1)}, u32[]{:S(2)}) copy-start(bf16[128,2048]{1,0:T(8,128)(2,1)} %constant.14.clone.lines_table) | copy-start | bytes 1572868
  81.2 39.7 %copy-start.1 = (f32[256,16,512]{2,1,0:T(8,128)S(1)}, f32[256,16,512]{2,1,0:T(8,128)}, u32[]{:S(2)}) copy-start(f32[256,16,512]{2,1,0:T(8,128)} %copy-done) | copy-start | bytes 25165828
  110.6 6.2 %copy-start.10 = (bf16[128,256]{1,0:T(8,128)(2,1)S(1)}, bf16[128,256]{1,0:T(8,128)(2,1)}, u32[]{:S(2)}) copy-start(bf16[128,256]{1,0:T(8,128)(2,1)} %constant.15.clone.table) | copy-start | bytes 196612
  110.6 10.3 %copy-start.9 = (bf16[256,384]{1,0:T(8,128)(2,1)S(1)}, bf16[256,384]{1,0:T(8,128)(2,1)}, u32[]{:S(2)}) copy-start(bf16[256,384]{1,0:T(8,128)(2,1)} %constant.16.clone.table_ref) | copy-start | bytes 589828
  112.2 4.6 %collective-permute-start.4 = (bf16[64,512]{1,0:T(8,128)(2,1)S(1)}, bf16[64,512]{1,0:T(8,128)(2,1)S(1)}, u32[]{:S(2)}, u32[]{:S(2)}) collective-permute-start(bf16[64,512]{1,0:T(8,128)(2,1)S(1)} %get-tuple-element.45), channel_id=1, source_target_pairs={{0,4},{4,8},{8,12},{12,16},{16,20},{20,24},{24,28},{28,0},{1,5},{5... | collective-permute-start | bytes 196616 | tf_op jit(solution)/shard_map/ppermute | solution.py:538
  113.8 3.0 %collective-permute-start.5 = (bf16[64,512]{1,0:T(8,128)(2,1)S(1)}, bf16[64,512]{1,0:T(8,128)(2,1)S(1)}, u32[]{:S(2)}, u32[]{:S(2)}) collective-permute-start(bf16[64,512]{1,0:T(8,128)(2,1)S(1)} %get-tuple-element.46), channel_id=1, source_target_pairs={{0,28},{4,0},{8,4},{12,8},{16,12},{20,16},{24,20},{28,24},{1,29},{... | collective-permute-start | bytes 196616 | tf_op jit(solution)/shard_map/ppermute | solution.py:539
  117.0 13.2 %collective-permute-start.6 = (bf16[64,512]{1,0:T(8,128)(2,1)S(1)}, bf16[64,512]{1,0:T(8,128)(2,1)S(1)}, u32[]{:S(2)}, u32[]{:S(2)}) collective-permute-start(bf16[64,512]{1,0:T(8,128)(2,1)S(1)} %get-tuple-element.49), channel_id=1, source_target_pairs={{0,1},{1,2},{2,3},{3,0},{4,5},{5,6},{6,7},{7,4},{8,9},{9,10},{10,1... | collective-permute-start | bytes 196616 | tf_op jit(solution)/shard_map/ppermute | solution.py:538
  120.8 9.4 %collective-permute-start.7 = (bf16[64,512]{1,0:T(8,128)(2,1)S(1)}, bf16[64,512]{1,0:T(8,128)(2,1)S(1)}, u32[]{:S(2)}, u32[]{:S(2)}) collective-permute-start(bf16[64,512]{1,0:T(8,128)(2,1)S(1)} %get-tuple-element.50), channel_id=1, source_target_pairs={{0,3},{1,0},{2,1},{3,2},{4,7},{5,4},{6,5},{7,6},{8,11},{9,8},{10,9... | collective-permute-start | bytes 196616 | tf_op jit(solution)/shard_map/ppermute | solution.py:539
  120.9 9.4 %copy-start.7 = (bf16[1024,128]{1,0:T(8,128)(2,1)S(1)}, bf16[1024,128]{1,0:T(8,128)(2,1)}, u32[]{:S(2)}) copy-start(bf16[1024,128]{1,0:T(8,128)(2,1)} %constant.17.clone.table_ref) | copy-start | bytes 786436
  (6 other events, 8.2 us)
where the time goes:
time: 133 us; the launch traced here: 132 us
  Pallas kernels  52.2 us (39%)
  blocking collectives  29.3 us (22%)
  starting transfers between devices  23.6 us (18%)
  local copies, waits for them, and re-layouts  20.3 us (15%)
  waiting for transfers between devices  6.76 us (5%)
    all_to_all x1, blocking collectives, regroup(): lax.all_to_all(blocks, ('gx', 'gy'), split_axis=0, concat_axis=0, tiled=T...  29.3 us
    pallas_call x2, Pallas kernels, rows_call(): pl.pallas_call(functools.partial(row_kernel, emit_columns), out_shape=out...  23.1 us
    unnamed x40, local copies, waits for them, and re-layouts  20.3 us
    all_to_all x2, starting transfers between devices, regroup(): lax.all_to_all(blocks, ('gx', 'gy'), split_axis=0, concat_axis=0, tiled=T...  9.75 us
    pallas_call x1, Pallas kernels, inner_sum(): pl.pallas_call(functools.partial(inner_kernel, fields, span_y), out_shape...  9.32 us
    ppermute x4, starting transfers between devices, exchange(): from_low = lax.ppermute(to_high, axis, ring(axis, 1))  7.66 us
    pallas_call x1, Pallas kernels, front(): pl.pallas_call(functools.partial(front_kernel, fields, span_y), out_shape...  6.6 us
    ppermute x4, starting transfers between devices, exchange(): from_high = lax.ppermute(to_low, axis, ring(axis, -1))  6.15 us
  transfers between devices with their start and end apart: 10, of which 2 were waited for; matrix products, arithmetic and copies ran while one was open for 0% of the time, Pallas kernels for 26%

commit v1 on v0

v1 whole, which is shorter than its diff:
```python
import functools
import math

import jax
import jax.numpy as jnp
import numpy as np
from jax import lax
from jax.experimental import pallas as pl
from jax.experimental.pallas import tpu as pltpu
from jax.sharding import PartitionSpec as P

GROUP_COLS = 16
EXD = 16
EYD = 16
NP = 16
F32 = jnp.float32
BF16 = jnp.bfloat16
I32 = jnp.int32
MB = 1024 * 1024


def lagrange_value(node_index, position, gll_nodes):
    running = 1.0
    for other_index in range(4):
        if other_index != node_index:
            running = (
                running
                * (position - gll_nodes[other_index])
                / (gll_nodes[node_index] - gll_nodes[other_index])
            )
    return running


def half_tables():
    gll_nodes = [-1.0, -1.0 / math.sqrt(5.0), 1.0 / math.sqrt(5.0), 1.0]
    halves = np.zeros((2, 4))
    for half_index, (lower_end, upper_end) in enumerate(((-1.0, 0.0), (0.0, 1.0))):
        centre = 0.5 * (lower_end + upper_end)
        offset = 0.5 * (upper_end - lower_end) / math.sqrt(3.0)
        for node in range(4):
            first = lagrange_value(node, centre - offset, gll_nodes)
            second = lagrange_value(node, centre + offset, gll_nodes)
            halves[half_index, node] = 0.5 * (upper_end - lower_end) * (first + second)
    product = halves @ halves.T
    determinant = product[0, 0] * product[1, 1] - product[0, 1] * product[1, 0]
    inverse = (
        np.array([[product[1, 1], -product[0, 1]], [-product[1, 0], product[0, 0]]]) / determinant
    )
    spread = halves.T @ inverse
    return halves.astype(np.float32), spread.astype(np.float32)


HALVES, SPREAD = half_tables()
ONE_D = np.array([0.5, 1.0, 1.0, 0.5])


def shift_down(n):
    return np.eye(n, k=-1)


def local_pass(n):
    table = np.einsum("ab,xy->axby", np.eye(4), np.eye(n))
    table[0, :, 3, :] += shift_down(n)
    table[3, :, 0, :] += shift_down(n).T
    return table


def constant_tables():
    h = HALVES.astype(np.float64)
    s = SPREAD.astype(np.float64)
    w = ONE_D
    eye = np.eye(EXD)
    line = local_pass(EYD)
    col_x = []
    for a in (0, 3):
        col_x.append(
            np.einsum("i,jb,b,byez->ijyez", h[:, a] * w[a], h, w, line).reshape(4 * EYD, 4 * EYD)
        )
    col_y = np.zeros((EXD, 2, 2, EYD, 2, 4, EXD))
    for side, (b, y) in enumerate(((0, 0), (3, EYD - 1))):
        col_y[:, :, :, y, side] = np.einsum("ia,j,xz->xijaz", h * w, h[:, b] * w[b], eye)
    col_y = col_y.reshape(EXD * 4 * EYD, 2 * 4 * EXD)
    nodes = np.einsum("ai,bj,yz->abyijz", s, s, np.eye(EYD))
    across = np.zeros((4, 4, EYD, 3, 2, 2, EYD))
    across[:, :, :, 1] = nodes
    across[0, :, :, 0] = nodes[3]
    across[3, :, :, 2] = nodes[0]
    full = np.einsum("byez,aezdijt->abydijt", line, across)
    full = full * w[:, None, None, None, None, None, None] * w[:, None, None, None, None, None]
    final = full.reshape(NP * EYD, 3 * 4 * EYD)
    along = local_pass(EXD)
    lines = np.zeros((2, 4, EXD, EXD, 2, 2, EYD))
    corner_col = np.zeros((2, 4, EXD, 2, 2, 2, EYD))
    corner_pt = np.zeros((2, 4, EXD, 2, 4, EYD))
    for side, (b, y) in enumerate(((0, 0), (3, EYD - 1))):
        lines[side, :, :, :, :, :, y] = np.einsum("axcz,ci,j->axzij", along, s, s[b])
        corner_col[side, 0, 0, 0, :, :, y] = np.outer(s[3], s[b])
        corner_col[side, 3, EXD - 1, 1, :, :, y] = np.outer(s[0], s[b])
        corner_pt[side, 0, 0, 0, b, y] = 1.0
        corner_pt[side, 3, EXD - 1, 1, b, y] = 1.0
    lines = lines.reshape(2 * 4 * EXD, EXD * 4 * EYD)
    corner_col = corner_col.reshape(2 * 4 * EXD, 2 * 4 * EYD)
    corner_pt = corner_pt.reshape(2 * 4 * EXD, 2 * 4 * EYD)
    border = np.zeros((4, EYD, NP, 128))
    order = full.transpose(2, 0, 1, 3, 4, 5, 6).reshape(EYD, NP, 3, 4 * EYD)
    west, east = hi_lo_arrays(order[:, :, 0]), hi_lo_arrays(order[:, :, 2])
    border[0] = np.concatenate(west, axis=-1)
    border[1] = np.concatenate(east, axis=-1)
    for side, b in enumerate((0, 3)):
        for a in range(4):
            for x in range(EXD):
                border[2 + side, x, 4 * a + b, 16 * a + x] = w[a] * w[b]
    return dict(
        col_x=np.concatenate(col_x, axis=0),
        col_y=col_y,
        final=order.reshape(EYD * NP, 3 * 4 * EYD),
        lines=lines,
        corner_col=corner_col,
        corner_pt=corner_pt,
        border=border.reshape(4 * EYD * NP, 128),
    )


def hi_lo_arrays(table):
    hi = np.asarray(table, np.float32).astype(jnp.bfloat16)
    lo = (np.asarray(table, np.float32) - hi.astype(np.float32)).astype(jnp.bfloat16)
    return hi, lo


def hi_lo(table):
    return jnp.asarray(np.concatenate(hi_lo_arrays(table), axis=1))


TABLES = constant_tables()


def dot(left, right):
    return jnp.dot(left, right, preferred_element_type=F32)


def dot_nt(left, right):
    return lax.dot_general(left, right, (((1,), (1,)), ((), ())), preferred_element_type=F32)


def dot_twice(table, right):
    return dot(table, jnp.concatenate([right, right], axis=0))


def split(values):
    hi = values.astype(BF16)
    return hi, (values - hi.astype(F32)).astype(BF16)


def iota(shape, dim):
    return lax.broadcasted_iota(I32, shape, dim)


def one_hot(condition):
    return jnp.where(condition, 1.0, 0.0).astype(BF16)


def as_columns(row, start):
    piece = row[:, start : start + 128].astype(F32)
    return jnp.transpose(jnp.broadcast_to(piece, (128, 128))).astype(I32)


def tile_number(cell, span_y):
    shift = span_y.bit_length() - 1
    assert span_y == 1 << shift
    return ((cell >> shift) & (EXD - 1)) * EYD + (cell & (EYD - 1))


VMEM = pl.BlockSpec(memory_space=pltpu.VMEM)
SMEM = pl.BlockSpec(memory_space=pltpu.SMEM)
ANY = pl.BlockSpec(memory_space=pl.ANY)


def params(mib):
    return pltpu.CompilerParams(vmem_limit_bytes=mib * MB)


def cost(flops, moved):
    return pl.CostEstimate(flops=int(flops), bytes_accessed=int(moved), transcendentals=0)


def column_requests(devices, per_peer, group):
    columns_dev = devices * per_peer
    shift = columns_dev.bit_length() - 1
    source = group >> shift
    local = group & (columns_dev - 1)
    of_source = source == iota((devices, columns_dev), 0)
    marks = one_hot(of_source)
    upper = one_hot(iota((128, 128), 0) <= iota((128, 128), 1))
    before = jnp.zeros((devices, 1), F32)
    ranks = []
    for start in range(0, columns_dev, 128):
        piece = marks[:, start : start + 128]
        counts = dot(piece, upper) + before
        ranks.append(counts)
        before = counts[:, 127:128]
    counts = jnp.concatenate(ranks, axis=1)
    rank = jnp.sum(jnp.where(of_source, counts, 0.0), axis=0, keepdims=True).astype(I32) - 1
    of_rank = one_hot(rank == iota((128, columns_dev), 0))
    high = jnp.where(of_source, (local >> 5).astype(F32), 0.0).astype(BF16)
    low = jnp.where(of_source, (local & 31).astype(F32), 0.0).astype(BF16)
    wanted = dot_nt(high, of_rank) * 32.0 + dot_nt(low, of_rank)
    return wanted, source * per_peer + rank


def diagonal(sizes, step_x, step_y):
    count_x, count_y = sizes
    x = lax.rem(lax.axis_index("gx") + step_x + count_x, count_x)
    y = lax.rem(lax.axis_index("gy") + step_y + count_y, count_y)
    return x * count_y + y


CHUNKS = 8


def state_copy(state_ref, raw, sems, chunk):
    per = raw.shape[2]
    return pltpu.make_async_copy(
        state_ref.at[:, pl.ds(chunk * per, per)], raw.at[chunk], sems.at[chunk]
    )


def tile_operators(span_y, cell, stiff):
    elements = cell.shape[1]
    marks = one_hot(tile_number(cell, span_y) == iota((elements, elements), 0))
    row = iota(stiff.shape, 0)
    stiff = stiff + jnp.where((row >> 4) == (row & 15), 1.0, 0.0)
    hi, lo = split(stiff)
    return dot_nt(marks, hi), dot_nt(marks, lo)


def place_operators(parts, operators):
    row, col = iota((256, 256), 0), iota((256, 256), 1)
    same_elem = one_hot((row & 15) == (col >> 4))
    tiling = one_hot((row & 15) == (col & 15))
    column = iota((EYD, 256), 1) >> 4
    for x in range(EXD):
        stacked = jnp.concatenate(
            [
                jnp.where(column == n, part[x * EYD : (x + 1) * EYD], 0.0).astype(BF16)
                for part in parts
                for n in range(NP)
            ],
            axis=0,
        )
        placed = dot(stacked, tiling).astype(BF16)
        operators[x, 0:256] = placed[0:256] * same_elem
        operators[x, 256:512] = placed[256:512] * same_elem


def place_states(span_y, cell_smem, state_ref, raw, sems, hi_ref, lo_ref):
    fields, per, _, levels = raw.shape[1:]
    for chunk in range(CHUNKS):
        state_copy(state_ref, raw, sems, chunk).wait()

        def place_slots(i, _, chunk=chunk):
            for u in range(4):
                k = i * 4 + u
                where = tile_number(cell_smem[chunk * per + k], span_y)
                for f in range(fields):
                    hi, lo = split(raw[chunk, f, k])
                    hi_ref[where, :, f * levels : (f + 1) * levels] = hi
                    lo_ref[where, :, f * levels : (f + 1) * levels] = lo
            return 0

        lax.fori_loop(0, per // 4, place_slots, 0)


def row_points(row, operators, hi_ref, lo_ref):
    width = hi_ref.shape[2]
    at = pl.ds(pl.multiple_of(row * EYD, EYD), EYD)
    hi = hi_ref[at].reshape(EYD * NP, width)
    lo = lo_ref[at].reshape(EYD * NP, width)
    both = dot(operators[row], hi)
    return both[0:256] + both[256:512] + dot(operators[row, 0:256], lo)


def shifted(values, step):
    rows = values.shape[0]
    moved = pltpu.roll(values, step % rows, 0)
    free = 0 if step > 0 else rows - 1
    return jnp.where(iota(values.shape, 0) == free, 0.0, moved)


def sum_along_y(nodes):
    for a in range(4):
        first, last = nodes[4 * a], nodes[4 * a + 3]
        nodes[4 * a] = first + shifted(last, 1)
        nodes[4 * a + 3] = last + shifted(first, -1)


def held_nodes(held, before, next_first):
    nodes = [held[16 * n : 16 * n + 16] for n in range(NP)]
    for b in range(4):
        nodes[b] = nodes[b] + before[16 * b : 16 * b + 16]
        if next_first is not None:
            nodes[12 + b] = nodes[12 + b] + next_first[b]
    return nodes


def front_kernel(
    sizes,
    span_y,
    cell_smem,
    cell_ref,
    group_ref,
    stiff_ref,
    state_ref,
    columns_out,
    blocks_ref,
    q_ref,
    x_one,
    x_two,
    y_one,
    y_two,
    raw,
    sems,
    hi_ref,
    lo_ref,
    operators,
    held,
    before,
    lines,
    ends,
    columns,
    out_sem,
):
    devices = sizes[0] * sizes[1]
    width = held.shape[1]
    for chunk in range(CHUNKS):
        state_copy(state_ref, raw, sems, chunk).start()
    place_operators(tile_operators(span_y, cell_ref[...], stiff_ref[...]), operators)
    wanted, q_ref[...] = column_requests(
        devices, group_ref.shape[1] // devices, group_ref[...]
    )
    blocks_ref[...] = jnp.broadcast_to(wanted[:, None, :], (devices, 8, 128))
    place_states(span_y, cell_smem, state_ref, raw, sems, hi_ref, lo_ref)
    before[...] = jnp.zeros_like(before)
    held[...] = jnp.zeros_like(held)

    def emit(row, next_first):
        nodes = held_nodes(held, before, next_first)
        along = [
            [
                sum(float(HALVES[i, a] * ONE_D[a]) * nodes[4 * a + b] for a in range(4))
                for b in range(4)
            ]
            for i in range(2)
        ]
        for i in range(2):
            for j in range(2):
                columns[pl.ds(pl.multiple_of(row * 64 + (2 * i + j) * 16, 16), 16)] = sum(
                    float(HALVES[j, b] * ONE_D[b]) * along[i][b] for b in range(4)
                )

    def one_row(row, _):
        points = row_points(row, operators, hi_ref, lo_ref)

        ends[0, jnp.minimum(row, 1)] = points[0:64]
        ends[1, jnp.maximum(row - EXD + 2, 0)] = points[192:256]
        nodes = [points[16 * n : 16 * n + 16] for n in range(NP)]
        for a in range(4):
            lines[0, pl.ds(16 * a + row, 1)] = nodes[4 * a][0:1]
            lines[1, pl.ds(16 * a + row, 1)] = nodes[4 * a + 3][15:16]
        sum_along_y(nodes)
        emit(jnp.maximum(row - 1, 0), nodes[0:4])
        before[...] = held[192:256]
        for n in range(NP):
            held[16 * n : 16 * n + 16] = nodes[n]
        return 0

    def send(part):
        rows = pl.ds(part * (columns.shape[0] // 2), columns.shape[0] // 2)
        return pltpu.make_async_copy(columns.at[rows], columns_out.at[rows], out_sem.at[part])

    lax.fori_loop(0, EXD // 2 + 2, one_row, 0, unroll=2)
    send(0).start()
    lax.fori_loop(EXD // 2 + 2, EXD, one_row, 0, unroll=2)
    emit(EXD - 1, None)
    send(1).start()
    whole = []
    for side in range(2):
        first, last = lines[side, 0:16], lines[side, 48:64]
        whole.append(
            jnp.concatenate(
                [first + shifted(last, 1), lines[side, 16:48], last + shifted(first, -1)], axis=0
            )
        )
    for axis, low, high, one, two in (
        ("gx", ends[0, 0], ends[1, 1], x_one, x_two),
        ("gy", whole[0], whole[1], y_one, y_two),
    ):
        first, second = by_parity(axis, low, high)
        one[...] = first.astype(BF16)
        two[...] = second.astype(BF16)
    for step_x, row in ((-1, 0), (1, 3 * 16 + 15)):
        for step_y, side in ((-1, 0), (1, 1)):
            block = diagonal(sizes, step_x, step_y)
            point = lines[side, row : row + 1]
            for f in range(width // 128):
                blocks_ref[block, 1 + f : 2 + f] = point[:, f * 128 : (f + 1) * 128]
    send(0).wait()
    send(1).wait()


def state_scratch(fields, elements, levels):
    width = fields * levels
    return [
        pltpu.VMEM((CHUNKS, fields, elements // CHUNKS, NP, levels), F32),
        pltpu.SemaphoreType.DMA((CHUNKS,)),
        pltpu.VMEM((elements, NP, width), BF16),
        pltpu.VMEM((elements, NP, width), BF16),
        pltpu.VMEM((EXD, 512, 256), BF16),
        pltpu.VMEM((256, width), F32),
        pltpu.VMEM((64, width), F32),
    ]


FRONT_LIMIT = 56


def front(cell, group, stiff, state, sizes):
    fields, elements, _, levels = state.shape
    width = fields * levels
    devices = sizes[0] * sizes[1]
    line = jax.ShapeDtypeStruct((64, width), BF16)
    return pl.pallas_call(
        functools.partial(front_kernel, sizes, EYD * sizes[1]),
        out_shape=(
            jax.ShapeDtypeStruct((4 * elements, width), F32),
            jax.ShapeDtypeStruct((devices, 8, 128), F32),
            jax.ShapeDtypeStruct((1, 4 * elements), I32),
            line,
            line,
            line,
            line,
        ),
        in_specs=[SMEM, VMEM, VMEM, VMEM, ANY],
        out_specs=(ANY,) + (VMEM,) * 6,
        scratch_shapes=state_scratch(fields, elements, levels)
        + [
            pltpu.VMEM((2, 64, width), F32),
            pltpu.VMEM((2, 2, 64, width), F32),
            pltpu.VMEM((4 * elements, width), F32),
            pltpu.SemaphoreType.DMA((2,)),
        ],
        compiler_params=params(FRONT_LIMIT),
        cost_estimate=cost(4e9, 2e7),
        name="front",
    )(cell, cell.reshape(1, elements), group, stiff, state)


def dynamics_kernel(
    span_y,
    cell_smem,
    cell_ref,
    stiff_ref,
    state_ref,
    hx_one,
    hx_two,
    hy_south,
    hy_north,
    out_ref,
    raw,
    sems,
    hi_ref,
    lo_ref,
    operators,
    held,
    before,
    turned,
    hx,
    rows_out,
    out_sems,
):
    hx[0], hx[1] = from_neighbours("gx", hx_one[...].astype(F32), hx_two[...].astype(F32))
    fields, _, levels = turned.shape
    for chunk in range(CHUNKS):
        state_copy(state_ref, raw, sems, chunk).start()
    place_operators(tile_operators(span_y, cell_ref[...], stiff_ref[...]), operators)
    place_states(span_y, cell_smem, state_ref, raw, sems, hi_ref, lo_ref)
    before[...] = jnp.zeros_like(before)
    held[...] = jnp.zeros_like(held)

    def emit(row, next_first):
        nodes = held_nodes(held, before, next_first)
        for a in range(4):
            at_row = pl.ds(16 * a + row, 1)
            for b in range(4):
                n = 4 * a + b
                values = nodes[n]
                if b == 0:
                    values = values + jnp.where(iota(values.shape, 0) == 0, hy_south[at_row], 0.0)
                if b == 3:
                    values = values + jnp.where(iota(values.shape, 0) == 15, hy_north[at_row], 0.0)
                values = values * float(ONE_D[a] * ONE_D[b])
                for f in range(fields):
                    turned[f, 16 * n : 16 * n + 16] = values[:, f * levels : (f + 1) * levels]
        slot = row & 1
        for y in range(EYD):
            for f in range(fields):
                rows_out[slot, y, :, f * levels : (f + 1) * levels] = turned[
                    f, pl.ds(y, NP, stride=16)
                ]

    def copy_out(row):
        slot = row & 1
        return pltpu.make_async_copy(
            rows_out.at[slot], out_ref.at[pl.ds(row * EYD, EYD)], out_sems.at[slot]
        )

    def one_row(row, _):
        points = row_points(row, operators, hi_ref, lo_ref)
        nodes = [points[16 * n : 16 * n + 16] for n in range(NP)]
        low = jnp.where(row == 0, 1.0, 0.0)
        high = jnp.where(row == EXD - 1, 1.0, 0.0)
        for b in range(4):
            rows = slice(16 * b, 16 * b + 16)
            nodes[b] = nodes[b] + hx[0, rows] * low
            nodes[12 + b] = nodes[12 + b] + hx[1, rows] * high
        sum_along_y(nodes)

        @pl.when(row >= 3)
        def _():
            copy_out(row - 3).wait()

        @pl.when(row >= 1)
        def _():
            emit(row - 1, nodes[0:4])
            copy_out(row - 1).start()

        before[...] = held[192:256]
        for n in range(NP):
            held[16 * n : 16 * n + 16] = nodes[n]
        return 0

    lax.fori_loop(0, EXD, one_row, 0)
    copy_out(EXD - 3).wait()
    emit(EXD - 1, None)
    copy_out(EXD - 1).start()
    copy_out(EXD - 2).wait()
    copy_out(EXD - 1).wait()


def dynamics_rows(cell, stiff, state, span_y, halos):
    fields, elements, _, levels = state.shape
    width = fields * levels
    return pl.pallas_call(
        functools.partial(dynamics_kernel, span_y),
        out_shape=jax.ShapeDtypeStruct((elements, NP, width), F32),
        in_specs=[SMEM, VMEM, VMEM, ANY] + [VMEM] * 4,
        out_specs=ANY,
        scratch_shapes=state_scratch(fields, elements, levels)
        + [
            pltpu.VMEM((fields, 256, levels), F32),
            pltpu.VMEM((2, 64, width), F32),
            pltpu.VMEM((2, EYD, NP, width), F32),
            pltpu.SemaphoreType.DMA((2,)),
        ],
        compiler_params=params(DYN_LIMIT),
        cost_estimate=cost(4e9, 2e7),
        name="dynamics_rows",
    )(cell, cell.reshape(1, elements), stiff, state, *halos)


def message_kernel(x_one, x_two, south_ref, north_ref, table, y_one, y_two):
    both = jnp.concatenate(from_neighbours("gx", x_one[...], x_two[...]), axis=0)
    add = dot_twice(table[...], both)
    one, two = by_parity("gy", south_ref[...] + add[0:64], north_ref[...] + add[64:128])
    y_one[...] = one.astype(BF16)
    y_two[...] = two.astype(BF16)


def messages(one, two, south, north, table):
    width = one.shape[1]
    return pl.pallas_call(
        message_kernel,
        out_shape=(jax.ShapeDtypeStruct((64, width), BF16),) * 2,
        in_specs=[VMEM] * 5,
        out_specs=(VMEM,) * 2,
        compiler_params=params(16),
        cost_estimate=cost(4e7, 6e5),
        name="line_messages",
    )(one, two, south, north, table)


def pairs(axis, first):
    count = lax.axis_size(axis)
    low = range(0 if first else 1, count, 2)
    return [(i, (i + 1) % count) for i in low] + [((i + 1) % count, i) for i in low]


def exchange(axis, one, two):
    return (
        lax.ppermute(one, axis, pairs(axis, True)),
        lax.ppermute(two, axis, pairs(axis, False)),
    )


def by_parity(axis, to_low, to_high):
    even = (lax.axis_index(axis) & 1) == 0
    return jnp.where(even, to_high, to_low), jnp.where(even, to_low, to_high)


def from_neighbours(axis, one, two):
    even = (lax.axis_index(axis) & 1) == 0
    return jnp.where(even, two, one), jnp.where(even, one, two)


def send_kernel(
    sizes,
    span_y,
    columns_hbm,
    table_hbm,
    x_one,
    x_two,
    y_one,
    y_two,
    blocks_ref,
    cell_ref,
    out_ref,
    place_ref,
    whole_south,
    whole_north,
    columns_ref,
    table_ref,
    rounded,
    pick,
    sems,
):
    count, width = columns_ref.shape
    devices = sizes[0] * sizes[1]
    per_peer = count // devices
    table_copy = pltpu.make_async_copy(table_hbm, table_ref, sems.at[0])
    table_copy.start()
    copy = pltpu.make_async_copy(columns_hbm, columns_ref, sems.at[1])
    copy.start()
    requested = blocks_ref[:, 0, :].astype(I32)
    spread_out = one_hot((iota((128, count), 1) & (per_peer - 1)) == iota((128, count), 0))
    shift = per_peer.bit_length() - 1
    own = (iota((devices, count), 1) >> shift) == iota((devices, count), 0)
    wide = dot((requested >> 5).astype(F32).astype(BF16), spread_out) * 32.0 + dot(
        (requested & 31).astype(F32).astype(BF16), spread_out
    )
    requested = jnp.sum(jnp.where(own, wide, 0.0), axis=0, keepdims=True).astype(I32)
    elements = cell_ref.shape[1]
    marks = one_hot((requested >> 2) == iota((elements, count), 0))
    tile_row = tile_number(cell_ref[...], span_y).astype(F32)
    tile_row = jnp.broadcast_to(tile_row, (8, elements)).astype(BF16)
    tile = dot(tile_row, marks)[0:1].astype(I32)
    place = (tile >> 4) * 64 + (requested & 3) * 16 + (tile & 15)
    place_ref[...] = place
    for start in range(0, count, 128):
        column = as_columns(place, start)
        for other in range(0, count, 128):
            pick[start : start + 128, other : other + 128] = one_hot(
                column == iota((128, 128), 1) + other
            )

    south, north = from_neighbours("gy", y_one[...].astype(F32), y_two[...].astype(F32))
    for ref, line, step_y in ((whole_south, south, -1), (whole_north, north, 1)):
        ref[...] = line
        for step_x, row in ((-1, 0), (1, 63)):
            block = diagonal(sizes, step_x, step_y)
            for f in range(width // 128):
                ref[row : row + 1, f * 128 : (f + 1) * 128] += blocks_ref[block, 1 + f : 2 + f]
    lines = jnp.concatenate([whole_south[...], whole_north[...]], axis=0).astype(BF16)
    west, east = from_neighbours("gx", x_one[...], x_two[...])
    table_copy.wait()
    west = dot_twice(table_ref[count : count + 64, 0:128], west)
    east = dot_twice(table_ref[count + 64 : count + 128, 0:128], east)
    add = dot_twice(table_ref[0:count], lines)
    copy.wait()
    rounded[...] = (columns_ref[...] + add).astype(BF16)
    rounded[0:64] = (columns_ref[0:64] + add[0:64] + west).astype(BF16)
    rounded[count - 64 : count] = (
        columns_ref[count - 64 : count] + add[count - 64 : count] + east
    ).astype(BF16)
    out_ref[...] = dot(pick[...], rounded[...]).astype(BF16)


def send_columns(columns, halos, blocks, cell, sizes):
    count, width = columns.shape
    extra = np.concatenate(hi_lo_arrays(TABLES["col_x"]), axis=1)
    table = np.concatenate(hi_lo_arrays(TABLES["col_y"]), axis=1)
    table = np.concatenate([table, np.pad(extra, ((0, 0), (0, 128)))], axis=0)
    return pl.pallas_call(
        functools.partial(send_kernel, sizes, EYD * sizes[1]),
        out_shape=(
            jax.ShapeDtypeStruct((count, width), BF16),
            jax.ShapeDtypeStruct((1, count), I32),
            jax.ShapeDtypeStruct((64, width), F32),
            jax.ShapeDtypeStruct((64, width), F32),
        ),
        in_specs=[ANY, ANY] + [VMEM] * 6,
        out_specs=(VMEM,) * 4,
        scratch_shapes=[
            pltpu.VMEM((count, width), F32),
            pltpu.VMEM(table.shape, BF16),
            pltpu.VMEM((count, width), BF16),
            pltpu.VMEM((count, count), BF16),
            pltpu.SemaphoreType.DMA((2,)),
        ],
        compiler_params=params(SEND_LIMIT),
        cost_estimate=cost(2e9, 5e6),
        name="send_columns",
    )(columns, jnp.asarray(table), *halos, blocks, cell)


SEND_LIMIT = 60
DYN_LIMIT = 56


def physics_kernel(
    fields, incoming_ref, q_ref, inverse_hbm, out_ref, inverse, pick, physics, tendency, sem
):
    count, width = incoming_ref.shape
    levels = width // fields
    copy = pltpu.make_async_copy(inverse_hbm, inverse, sem)
    copy.start()
    q = q_ref[...]
    for start in range(0, count, 128):
        column = as_columns(q, start)
        for other in range(0, count, 128):
            pick[start : start + 128, other : other + 128] = one_hot(
                column == iota((128, 128), 1) + other
            )
    physics[...] = dot(pick[...], incoming_ref[...])
    copy.wait()
    for start in range(0, count, 128):
        pick[start : start + 128] = one_hot(q == iota((128, count), 0) + start)
    for group in range(count // GROUP_COLS):
        at = slice(group * GROUP_COLS, (group + 1) * GROUP_COLS)
        stacked = jnp.concatenate(
            [physics[at, f * levels : (f + 1) * levels] for f in range(fields)], axis=0
        )
        result = dot_nt(stacked.astype(BF16), inverse[group]) - stacked
        tendency[at] = jnp.concatenate(
            [result[f * GROUP_COLS : (f + 1) * GROUP_COLS] for f in range(fields)], axis=1
        ).astype(BF16)
    out_ref[...] = dot(pick[...], tendency[...]).astype(BF16)


def physics_step(incoming, q, inverse, fields):
    count, width = incoming.shape
    return pl.pallas_call(
        functools.partial(physics_kernel, fields),
        out_shape=jax.ShapeDtypeStruct((count, width), BF16),
        in_specs=[VMEM, VMEM, ANY],
        out_specs=VMEM,
        scratch_shapes=[
            pltpu.VMEM(inverse.shape, BF16),
            pltpu.VMEM((count, count), BF16),
            pltpu.VMEM((count, width), F32),
            pltpu.VMEM((count, width), BF16),
            pltpu.SemaphoreType.DMA,
        ],
        compiler_params=params(PHYSICS_LIMIT),
        cost_estimate=cost(3e9, 5e6),
        name="physics",
    )(incoming, q, inverse)


PHYSICS_LIMIT = 16


def unpack_kernel(
    received_ref,
    place_ref,
    lines_table,
    back_ref,
    x_one,
    x_two,
    south_ref,
    north_ref,
    pick,
):
    count = received_ref.shape[0]
    place = place_ref[...]
    for start in range(0, count, 128):
        pick[start : start + 128] = one_hot(place == iota((128, count), 0) + start)
    back_ref[...] = dot(pick[...], received_ref[...]).astype(BF16)
    x_one[...], x_two[...] = by_parity("gx", back_ref[0:64], back_ref[count - 64 : count])
    lines = dot(lines_table[...], back_ref[...])
    south_ref[...] = lines[0:64] + lines[128:192]
    north_ref[...] = lines[64:128] + lines[192:256]


def unpack(received, place):
    count, width = received.shape
    table = jnp.asarray(np.concatenate(hi_lo_arrays(TABLES["lines"]), axis=0))
    return pl.pallas_call(
        unpack_kernel,
        out_shape=(
            jax.ShapeDtypeStruct((count, width), BF16),
            jax.ShapeDtypeStruct((64, width), BF16),
            jax.ShapeDtypeStruct((64, width), BF16),
            jax.ShapeDtypeStruct((64, width), F32),
            jax.ShapeDtypeStruct((64, width), F32),
        ),
        in_specs=[VMEM] * 3,
        out_specs=(VMEM,) * 5,
        scratch_shapes=[pltpu.VMEM((count, count), BF16)],
        compiler_params=params(16),
        cost_estimate=cost(2e9, 4e6),
        name="unpack",
    )(received, place, table)


def inner_kernel(
    span_y,
    cell_smem,
    dynamics_ref,
    back_ref,
    table_ref,
    out_ref,
    border_ref,
    slot_ref,
    total,
    buffer,
    sems,
):
    elements, _, width = total.shape
    fields, levels = buffer.shape[1], buffer.shape[4]
    count = back_ref.shape[0]

    def near_sum(row, first, rows, skip):
        near = back_ref[pl.ds(first, rows)]
        both = dot(table_ref[:, skip : skip + rows], near)
        at = pl.ds(row * EYD, 2 * EYD)
        sums = both[0:512] + both[512:1024]
        total[at] = dynamics_ref[at] + sums.reshape(2 * EYD, NP, width)

    near_sum(0, 0, 192, 64)
    near_sum(EXD - 2, count - 192, 192, 0)

    def middle(pair, _):
        near_sum(pair * 2, pl.multiple_of(pair * 128 - 64, 64), 256, 0)
        return 0

    lax.fori_loop(1, EXD // 2 - 1, middle, 0, unroll=2)
    for kind in range(4):
        for k in range(16):
            tile = (k, (EXD - 1) * EYD + k, k * EYD, k * EYD + EYD - 1)[kind]
            for f in range(fields):
                border_ref[kind, f, k] = total[tile, :, f * levels : (f + 1) * levels]
    per = elements // CHUNKS

    def copy(chunk):
        return pltpu.make_async_copy(
            buffer.at[chunk], out_ref.at[:, pl.ds(chunk * per, per)], sems.at[chunk]
        )

    for chunk in range(CHUNKS):

        def take_slots(i, _, chunk=chunk):
            for u in range(4):
                k = i * 4 + u
                tile = tile_number(cell_smem[chunk * per + k], span_y)
                slot_ref[0, tile] = chunk * per + k
                for f in range(fields):
                    buffer[chunk, f, k] = total[tile, :, f * levels : (f + 1) * levels]
            return 0

        lax.fori_loop(0, per // 4, take_slots, 0)
        copy(chunk).start()
    for chunk in range(CHUNKS):
        copy(chunk).wait()


def inner_sum(cell, dynamics, back, fields, span_y):
    elements, _, width = dynamics.shape
    levels = width // fields
    one = TABLES["final"].reshape(EYD * NP, 3, 64)
    two = np.zeros((2, EYD * NP, 4, 64))
    two[0, :, 0:3] = one
    two[1, :, 1:4] = one
    table = np.concatenate(hi_lo_arrays(two.reshape(2 * EYD * NP, 256)), axis=0)
    return pl.pallas_call(
        functools.partial(inner_kernel, span_y),
        out_shape=(
            jax.ShapeDtypeStruct((fields, elements, NP, levels), F32),
            jax.ShapeDtypeStruct((4, fields, 16, NP, levels), F32),
            jax.ShapeDtypeStruct((1, elements), I32),
        ),
        in_specs=[SMEM, VMEM, VMEM, VMEM],
        out_specs=(ANY, VMEM, SMEM),
        scratch_shapes=[
            pltpu.VMEM((elements, NP, width), F32),
            pltpu.VMEM((CHUNKS, fields, elements // CHUNKS, NP, levels), F32),
            pltpu.SemaphoreType.DMA((CHUNKS,)),
        ],
        compiler_params=params(32),
        cost_estimate=cost(2e9, 2e7),
        name="inner_sum",
    )(cell, dynamics, back, jnp.asarray(table))


def border_kernel(
    fields, slot_ref, x_one, x_two, y_one, y_two, border_ref, table_ref, _, out_ref, buffer, sem
):
    width = x_one.shape[1]
    levels = width // fields
    adds = []
    halos = from_neighbours("gx", x_one[...], x_two[...])
    halos = halos + from_neighbours("gy", y_one[...], y_two[...])
    for kind, halo in enumerate(halos):
        table = table_ref[kind * 256 : kind * 256 + 256]
        if kind < 2:
            add = dot_twice(table, halo)
        else:
            add = dot(table[:, 0:64], halo)
        adds.append(add.reshape(16, NP, width))
    for kind in range(4):
        for k in range(16):
            if kind >= 2 and k in (0, 15):
                continue
            add = adds[kind][k]
            if kind < 2 and k in (0, 15):
                add = add + adds[2 if k == 0 else 3][0 if kind == 0 else 15]
            for f in range(fields):
                buffer[kind, f, k] = border_ref[kind, f, k] + add[:, f * levels : (f + 1) * levels]
            tile = (k, (EXD - 1) * EYD + k, k * EYD, k * EYD + EYD - 1)[kind]
            pltpu.make_async_copy(
                buffer.at[kind, :, k], out_ref.at[:, slot_ref[0, tile]], sem.at[kind]
            ).start()
    for kind in range(4):
        part = buffer.at[kind] if kind < 2 else buffer.at[kind, :, 1:15]
        pltpu.make_async_copy(part, part, sem.at[kind]).wait()


def border_sum(slot, halos, border, out):
    fields, levels = out.shape[0], out.shape[3]
    table = jnp.asarray(TABLES["border"].astype(np.float32).astype(jnp.bfloat16))
    return pl.pallas_call(
        functools.partial(border_kernel, fields),
        out_shape=jax.ShapeDtypeStruct(out.shape, F32),
        in_specs=[SMEM] + [VMEM] * 6 + [ANY],
        out_specs=ANY,
        scratch_shapes=[
            pltpu.VMEM((4, fields, 16, NP, levels), F32),
            pltpu.SemaphoreType.DMA((4,)),
        ],
        input_output_aliases={7: 0},
        compiler_params=params(16),
        cost_estimate=cost(2e8, 4e6),
        name="border_sum",
    )(slot, *halos, border, table, out)


def regroup(blocks):
    return lax.all_to_all(blocks, ("gx", "gy"), split_axis=0, concat_axis=0, tiled=True)


def per_device(state_in, stiffness, elem_cell, group_column, group_inverse):
    fields, elements = state_in.shape[:2]
    sizes = (lax.axis_size("gx"), lax.axis_size("gy"))
    columns_dev = 4 * elements
    span_y = EYD * sizes[1]
    stiff = stiffness.reshape(NP * NP, elements)

    columns, blocks, q, x_one, x_two, y_one, y_two = front(
        elem_cell, group_column.reshape(1, columns_dev), stiff, state_in, sizes
    )
    hx = exchange("gx", x_one, x_two)
    hy = exchange("gy", y_one, y_two)
    blocks = regroup(blocks)

    outgoing, place, south, north = send_columns(
        columns, (*hx, *hy), blocks, elem_cell.reshape(1, elements), sizes
    )
    incoming = regroup(outgoing)
    dynamics = dynamics_rows(elem_cell, stiff, state_in, span_y, (*hx, south, north))
    incoming, dynamics = lax.optimization_barrier((incoming, dynamics))
    received = regroup(physics_step(incoming, q, group_inverse, fields))

    back, x_one, x_two, south, north = unpack(received, place)
    bx = exchange("gx", x_one, x_two)
    by = exchange("gy", *messages(*bx, south, north, hi_lo(TABLES["corner_col"])))
    inner, border, slot = inner_sum(elem_cell, dynamics, back, fields, span_y)
    return border_sum(slot, (*bx, *by), border, inner)


def solution(mesh):
    placed = (
        P(None, ("gx", "gy"), None, None),
        P(None, None, ("gx", "gy")),
        P(("gx", "gy")),
        P(("gx", "gy")),
        P(("gx", "gy"), None, None),
    )
    return jax.shard_map(
        per_device,
        mesh=mesh,
        in_specs=placed,
        out_specs=P(None, ("gx", "gy"), None, None),
        check_vma=False,
    )
```

time: 133 us -> 119 us (0.89)
  local copies, waits for them, and re-layouts: 20.3 us -> 0.7 us
  waiting for transfers between devices: 6.76 us -> 16.6 us
  Pallas kernels: 52.2 us -> 49.3 us
  starting transfers between devices: 23.6 us -> 22.1 us
    unnamed x40 -> x30, local copies, waits for them, and re-layouts: 20.3 us -> 0.7 us
    ppermute x8, waiting for transfers between devices: 1.93 us -> 7.72 us  [the longest x4 7.03 us: exchange(): lax.ppermute(two, axis, pairs(axis, False))]
    all_to_all x2, waiting for transfers between devices: 4.82 us -> 8.91 us  [regroup(): lax.all_to_all(blocks, ('gx', 'gy'), split_axis=0, concat_axis=0, tiled=T...]
    pallas_call x8 -> x5, Pallas kernels: 43.8 us -> 41.2 us  [the longest x1 16.1 us: dynamics_rows(): pl.pallas_call(functools.partial(dynamics_kernel, span_y), out_shape=jax....]
    ppermute x8, starting transfers between devices: 13.8 us -> 12 us  [the longest x4 6.97 us: exchange(): lax.ppermute(two, axis, pairs(axis, False))]
  transfers between devices with their start and end apart: 10 -> 10, of which waited for: 2 -> 4; matrix products, arithmetic and copies ran while one was open for 0% -> 0% of each run, Pallas kernels for 26% -> 20%
where the time goes in v1:
time: 119 us; the launch traced here: 118 us
  Pallas kernels  49.3 us (41%)
  blocking collectives  29.3 us (25%)
  starting transfers between devices  22.1 us (19%)
  waiting for transfers between devices  16.6 us (14%)
    all_to_all x1, blocking collectives, regroup(): lax.all_to_all(blocks, ('gx', 'gy'), split_axis=0, concat_axis=0, tiled=T...  29.3 us
    pallas_call x1, Pallas kernels, dynamics_rows(): pl.pallas_call(functools.partial(dynamics_kernel, span_y), out_shape=jax....  16.1 us
    pallas_call x1, Pallas kernels, front(): pl.pallas_call(functools.partial(front_kernel, sizes, EYD * sizes[1]), ou...  12.1 us
    all_to_all x2, starting transfers between devices, regroup(): lax.all_to_all(blocks, ('gx', 'gy'), split_axis=0, concat_axis=0, tiled=T...  10.1 us
    all_to_all x2, waiting for transfers between devices, regroup(): lax.all_to_all(blocks, ('gx', 'gy'), split_axis=0, concat_axis=0, tiled=T...  8.91 us
    pallas_call x1, Pallas kernels, inner_sum(): pl.pallas_call(functools.partial(inner_kernel, span_y), out_shape=(jax.Sh...  7.66 us
    ppermute x4, waiting for transfers between devices, exchange(): lax.ppermute(two, axis, pairs(axis, False))  7.03 us
    ppermute x4, starting transfers between devices, exchange(): lax.ppermute(two, axis, pairs(axis, False))  6.97 us
  transfers between devices with their start and end apart: 10, of which 4 were waited for; matrix products, arithmetic and copies ran while one was open for 0% of the time, Pallas kernels for 20%

profile of v1, /device:TPU:0, one launch (start us, length us, event | category | flops | bytes accessed | tf_op | source)
XLA Modules:
  0.0 118.4 jit_solution(3562196063074570365)
XLA Ops:
  0.0 12.1 %front.1 = (f32[1024,512]{1,0:T(8,128)}, f32[32,8,128]{2,1,0:T(8,128)}, s32[1,1024]{1,0:T(1,128)}, bf16[64,512]{1,0:T(8,128)(2,1)}, bf16[64,512]{1,0:T(8,128)(2,...) custom-call(s32[256]{0:T(256)} %cell_smem.5, s32[1,256]{1,0:T(1,128)} %bitcast.12, s32[1,1024]{1,0:T(1,128)} %bitcast.18, ...), custom_call_target="tpu_custom_call" | custom-call | flops 4000000000 | bytes 20000000 | tf_op jit(solution)/shard_map/front/pallas_call | solution.py:431
  12.1 7.3 %all-to-all-start = ((f32[32,8,128]{2,1,0:T(8,128)}), f32[32,8,128]{2,1,0:T(8,128)S(1)}, u32[]{:S(2)}, u32[]{:S(2)}) async-start(f32[32,8,128]{2,1,0:T(8,128)} %get-tuple-element.33), calls=%async_computation | async-start | bytes 262144 | tf_op jit(solution)/shard_map/all_to_all | solution.py:956
  19.4 0.3 collective-permute-start
  19.7 2.5 %collective-permute-start.1 = (bf16[64,512]{1,0:T(8,128)(2,1)}, bf16[64,512]{1,0:T(8,128)(2,1)S(1)}, u32[]{:S(2)}, u32[]{:S(2)}) collective-permute-start(bf16[64,512]{1,0:T(8,128)(2,1)} %get-tuple-element.30), channel_id=1, source_target_pairs={{4,8},{12,16},{20,24},{28,0},{8,4},{16,12},{24,20},{0,28},{5,9},{1... | collective-permute-start | bytes 196616 | tf_op jit(solution)/shard_map/ppermute | solution.py:600
  22.3 1.5 %collective-permute-start.2 = (bf16[64,512]{1,0:T(8,128)(2,1)}, bf16[64,512]{1,0:T(8,128)(2,1)S(1)}, u32[]{:S(2)}, u32[]{:S(2)}) collective-permute-start(bf16[64,512]{1,0:T(8,128)(2,1)} %get-tuple-element.31), channel_id=1, source_target_pairs={{0,1},{2,3},{1,0},{3,2},{4,5},{6,7},{5,4},{7,6},{8,9},{10,11},{9,8... | collective-permute-start | bytes 196616 | tf_op jit(solution)/shard_map/ppermute | solution.py:599
  23.7 2.4 %collective-permute-start.3 = (bf16[64,512]{1,0:T(8,128)(2,1)}, bf16[64,512]{1,0:T(8,128)(2,1)S(1)}, u32[]{:S(2)}, u32[]{:S(2)}) collective-permute-start(bf16[64,512]{1,0:T(8,128)(2,1)} %get-tuple-element.32), channel_id=1, source_target_pairs={{1,2},{3,0},{2,1},{0,3},{5,6},{7,4},{6,5},{4,7},{9,10},{11,8},{10,... | collective-permute-start | bytes 196616 | tf_op jit(solution)/shard_map/ppermute | solution.py:600
  26.1 0.7 collective-permute-done.2.y_one
  26.8 3.2 %collective-permute-done.3.y_two = bf16[64,512]{1,0:T(8,128)(2,1)S(1)} collective-permute-done((bf16[64,512]{1,0:T(8,128)(2,1)}, bf16[64,512]{1,0:T(8,128)(2,1)S(1)}, u32[]{:S(2)}, u32[]{:S(2)}) %collective-permute-start.3) | collective-permute-done | bytes 65568 | tf_op jit(solution)/shard_map/ppermute | solution.py:600
  30.0 0.6 copy-done.12
  30.7 5.1 %send_columns.1 = (bf16[1024,512]{1,0:T(8,128)(2,1)}, s32[1,1024]{1,0:T(1,128)}, f32[64,512]{1,0:T(8,128)}, f32[64,512]{1,0:T(8,128)}) custom-call(f32[1024,512]{1,0:T(8,128)} %get-tuple-element.28.columns_hbm, bf16[1152,256]{1,0:T(8,128)(2,1)} %constant.10.clone.table_hbm, bf16[64,512]{1,0:T(8,128)(2,1)} %copy-done.9, bf16[64,512]{1,0:T(8,128)(2,1)} %copy-done.10, ...), custom_call_target="tpu_custom_call" | custom-call | flops 2000000000 | bytes 5000000 | tf_op jit(solution)/shard_map/send_columns/pallas_call | solution.py:691
  35.8 2.8 %all-to-all-start.1 = ((bf16[32,32,512]{2,1,0:T(8,128)(2,1)}), bf16[32,32,512]{2,1,0:T(8,128)(2,1)S(1)}, u32[]{:S(2)}, u32[]{:S(2)}) async-start(bf16[32,32,512]{2,1,0:T(8,128)(2,1)} %bitcast.15), calls=%async_computation.1 | async-start | bytes 2097152 | tf_op jit(solution)/shard_map/all_to_all | solution.py:956
  38.6 16.1 %dynamics_rows.1.dynamics_ref = f32[256,16,512]{2,1,0:T(8,128)} custom-call(s32[256]{0:T(256)} %cell_smem.5, s32[1,256]{1,0:T(1,128)} %bitcast.14, f32[256,256]{1,0:T(8,128)} %bitcast.17, f32[4,256,16,128]{3,2,1,0:T(8,128)} %state_ref.3, bf16[64,512]{1,0:T(8,128)(2,1)} %copy-done.9, bf16[64,512]{1,0:T(8,128)(2,1)} %copy-done.10, ...), custom_call_target="tpu_custom_call" | custom-call | flops 4000000000 | bytes 20000000 | tf_op jit(solution)/shard_map/dynamics_rows/pallas_call | solution.py:552
  54.7 8.9 %all-to-all-done.1 = bf16[32,32,512]{2,1,0:T(8,128)(2,1)S(1)} async-done(((bf16[32,32,512]{2,1,0:T(8,128)(2,1)}), bf16[32,32,512]{2,1,0:T(8,128)(2,1)S(1)}, u32[]{:S(2)}, u32[]{:S(2)}) %all-to-all-start.1) | async-done | bytes 1048608 | tf_op jit(solution)/shard_map/all_to_all | solution.py:956
  63.7 4.5 %physics.1 = bf16[1024,512]{1,0:T(8,128)(2,1)S(1)} custom-call(bf16[1024,512]{1,0:T(8,128)(2,1)S(1)} %bitcast.9, s32[1,1024]{1,0:T(1,128)S(1)} %copy-done.7, bf16[64,128,128]{2,1,0:T(8,128)(2,1)S(1)} %copy-done.4), custom_call_target="tpu_custom_call" | custom-call | flops 3000000000 | bytes 5000000 | tf_op jit(solution)/shard_map/physics/pallas_call | solution.py:750
  68.2 29.3 %all_to_all.28 = bf16[32,32,512]{2,1,0:T(8,128)(2,1)S(1)} all-to-all(bf16[32,32,512]{2,1,0:T(8,128)(2,1)S(1)} %bitcast.11), channel_id=1, replica_groups=mesh['gx'=8,'gy'=4] {'gx','gy'}, dimensions={0} | all-to-all | bytes 2097152 | tf_op jit(solution)/shard_map/all_to_all | solution.py:956
  97.5 1.5 %unpack.1 = (bf16[1024,512]{1,0:T(8,128)(2,1)S(1)}, bf16[64,512]{1,0:T(8,128)(2,1)S(1)}, bf16[64,512]{1,0:T(8,128)(2,1)S(1)}, f32[64,512]{1,0:T(8,128)S(1)}, f32[64,512]{1,0:T(8,128)S(1)}) custom-call(bf16[1024,512]{1,0:T(8,128)(2,1)S(1)} %bitcast.10, s32[1,1024]{1,0:T(1,128)S(1)} %copy-done.6, bf16[256,1024]{1,0:T(8,128)(2,1)S(1)} %copy-done.5), custom_call_target="tpu_custom_call" | custom-call | flops 2000000000 | bytes 4000000 | tf_op jit(solution)/shard_map/unpack/pallas_call | solution.py:796
  99.1 1.6 %collective-permute-start.4 = (bf16[64,512]{1,0:T(8,128)(2,1)S(1)}, bf16[64,512]{1,0:T(8,128)(2,1)S(1)}, u32[]{:S(2)}, u32[]{:S(2)}) collective-permute-start(bf16[64,512]{1,0:T(8,128)(2,1)S(1)} %get-tuple-element.43), channel_id=1, source_target_pairs={{0,4},{8,12},{16,20},{24,28},{4,0},{12,8},{20,16},{28,24},{1,5},{9... | collective-permute-start | bytes 196616 | tf_op jit(solution)/shard_map/ppermute | solution.py:599
  100.7 1.2 collective-permute-start.5
  101.8 3.9 %collective-permute-done.5.x_two = bf16[64,512]{1,0:T(8,128)(2,1)S(1)} collective-permute-done((bf16[64,512]{1,0:T(8,128)(2,1)S(1)}, bf16[64,512]{1,0:T(8,128)(2,1)S(1)}, u32[]{:S(2)}, u32[]{:S(2)}) %collective-permute-start.5) | collective-permute-done | bytes 65568 | tf_op jit(solution)/shard_map/ppermute | solution.py:600
  105.7 0.2 line_messages.1
  105.9 1.7 %collective-permute-start.6 = (bf16[64,512]{1,0:T(8,128)(2,1)S(1)}, bf16[64,512]{1,0:T(8,128)(2,1)S(1)}, u32[]{:S(2)}, u32[]{:S(2)}) collective-permute-start(bf16[64,512]{1,0:T(8,128)(2,1)S(1)} %get-tuple-element.47), channel_id=1, source_target_pairs={{0,1},{2,3},{1,0},{3,2},{4,5},{6,7},{5,4},{7,6},{8,9},{10,11},{9,8... | collective-permute-start | bytes 196616 | tf_op jit(solution)/shard_map/ppermute | solution.py:599
  107.5 0.9 collective-permute-start.7
  108.5 7.7 %inner_sum.1 = (f32[4,256,16,128]{3,2,1,0:T(8,128)}, f32[4,4,16,16,128]{4,3,2,1,0:T(8,128)S(1)}, s32[1,256]{1,0:T(1,128)S(1)}) custom-call(s32[256]{0:T(256)S(1)} %copy-done.3, f32[256,16,512]{2,1,0:T(8,128)S(1)} %bitcast.8, bf16[1024,512]{1,0:T(8,128)(2,1)S(1)} %get-tuple-element.41.back_ref, bf16[1024,256]{1,0:T(8,128)(2,1)S(1)} %copy-done), custom_call_target="tpu_custom_call" | custom-call | flops 2000000000 | bytes 20000000 | tf_op jit(solution)/shard_map/inner_sum/pallas_call | solution.py:883
  116.2 2.1 %border_sum.1 = f32[4,256,16,128]{3,2,1,0:T(8,128)} custom-call(s32[1,256]{1,0:T(1,128)S(1)} %get-tuple-element.42.slot_ref, bf16[64,512]{1,0:T(8,128)(2,1)S(1)} %collective-permute-done.4.x_one, bf16[64,512]{1,0:T(8,128)(2,1)S(1)} %collective-permute-done.5.x_two, bf16[64,512]{1,0:T(8,128)(2,1)S(1)} %collective-permute-done.6.y_one, ...), custom_call_target="tpu_custom_call", output_to_operand_aliasing={{}: (7, {})} | custom-call | flops 200000000 | bytes 4000000 | tf_op jit(solution)/shard_map/border_sum/pallas_call | solution.py:939
  (36 shorter events, 0.1 us)
Async XLA Ops:
  12.1 17.9 %all-to-all-start = ((f32[32,8,128]{2,1,0:T(8,128)}), f32[32,8,128]{2,1,0:T(8,128)S(1)}, u32[]{:S(2)}, u32[]{:S(2)}) async-start(f32[32,8,128]{2,1,0:T(8,128)} %get-tuple-element.33), calls=%async_computation | async-start | bytes 262144 | tf_op jit(solution)/shard_map/all_to_all | solution.py:956
  19.4 6.7 %collective-permute-start = (bf16[64,512]{1,0:T(8,128)(2,1)}, bf16[64,512]{1,0:T(8,128)(2,1)S(1)}, u32[]{:S(2)}, u32[]{:S(2)}) collective-permute-start(bf16[64,512]{1,0:T(8,128)(2,1)} %get-tuple-element.29), channel_id=1, source_target_pairs={{0,4},{8,12},{16,20},{24,28},{4,0},{12,8},{20,16},{28,24},{1,5},{9... | collective-permute-start | bytes 196616 | tf_op jit(solution)/shard_map/ppermute | solution.py:599
  19.7 6.4 %collective-permute-start.1 = (bf16[64,512]{1,0:T(8,128)(2,1)}, bf16[64,512]{1,0:T(8,128)(2,1)S(1)}, u32[]{:S(2)}, u32[]{:S(2)}) collective-permute-start(bf16[64,512]{1,0:T(8,128)(2,1)} %get-tuple-element.30), channel_id=1, source_target_pairs={{4,8},{12,16},{20,24},{28,0},{8,4},{16,12},{24,20},{0,28},{5,9},{1... | collective-permute-start | bytes 196616 | tf_op jit(solution)/shard_map/ppermute | solution.py:600
  22.3 4.6 %collective-permute-start.2 = (bf16[64,512]{1,0:T(8,128)(2,1)}, bf16[64,512]{1,0:T(8,128)(2,1)S(1)}, u32[]{:S(2)}, u32[]{:S(2)}) collective-permute-start(bf16[64,512]{1,0:T(8,128)(2,1)} %get-tuple-element.31), channel_id=1, source_target_pairs={{0,1},{2,3},{1,0},{3,2},{4,5},{6,7},{5,4},{7,6},{8,9},{10,11},{9,8... | collective-permute-start | bytes 196616 | tf_op jit(solution)/shard_map/ppermute | solution.py:599
  23.7 6.3 %collective-permute-start.3 = (bf16[64,512]{1,0:T(8,128)(2,1)}, bf16[64,512]{1,0:T(8,128)(2,1)S(1)}, u32[]{:S(2)}, u32[]{:S(2)}) collective-permute-start(bf16[64,512]{1,0:T(8,128)(2,1)} %get-tuple-element.32), channel_id=1, source_target_pairs={{1,2},{3,0},{2,1},{0,3},{5,6},{7,4},{6,5},{4,7},{9,10},{11,8},{10,... | collective-permute-start | bytes 196616 | tf_op jit(solution)/shard_map/ppermute | solution.py:600
  26.1 3.9 %copy-start.9 = (bf16[64,512]{1,0:T(8,128)(2,1)}, bf16[64,512]{1,0:T(8,128)(2,1)S(1)}, u32[]{:S(2)}) copy-start(bf16[64,512]{1,0:T(8,128)(2,1)S(1)} %collective-permute-done.x_one.hx_one) | copy-start | bytes 196612
  26.1 3.9 %copy-start.10 = (bf16[64,512]{1,0:T(8,128)(2,1)}, bf16[64,512]{1,0:T(8,128)(2,1)S(1)}, u32[]{:S(2)}) copy-start(bf16[64,512]{1,0:T(8,128)(2,1)S(1)} %collective-permute-done.1.x_two.hx_two) | copy-start | bytes 196612
  26.8 3.2 %copy-start.11 = (bf16[64,512]{1,0:T(8,128)(2,1)}, bf16[64,512]{1,0:T(8,128)(2,1)S(1)}, u32[]{:S(2)}) copy-start(bf16[64,512]{1,0:T(8,128)(2,1)S(1)} %collective-permute-done.2.y_one) | copy-start | bytes 196612
  30.0 0.7 copy-start.8
  35.8 27.9 %all-to-all-start.1 = ((bf16[32,32,512]{2,1,0:T(8,128)(2,1)}), bf16[32,32,512]{2,1,0:T(8,128)(2,1)S(1)}, u32[]{:S(2)}, u32[]{:S(2)}) async-start(bf16[32,32,512]{2,1,0:T(8,128)(2,1)} %bitcast.15), calls=%async_computation.1 | async-start | bytes 2097152 | tf_op jit(solution)/shard_map/all_to_all | solution.py:956
  38.6 25.1 %copy-start.4 = (bf16[64,128,128]{2,1,0:T(8,128)(2,1)S(1)}, bf16[64,128,128]{2,1,0:T(8,128)(2,1)}, u32[]{:S(2)}) copy-start(bf16[64,128,128]{2,1,0:T(8,128)(2,1)} %inverse_hbm.1) | copy-start | bytes 6291460
  38.6 25.1 %copy-start.7 = (s32[1,1024]{1,0:T(1,128)S(1)}, s32[1,1024]{1,0:T(1,128)}, u32[]{:S(2)}) copy-start(s32[1,1024]{1,0:T(1,128)} %get-tuple-element.39.q_ref) | copy-start | bytes 12292
  54.7 42.8 %copy-start.6 = (s32[1,1024]{1,0:T(1,128)S(1)}, s32[1,1024]{1,0:T(1,128)}, u32[]{:S(2)}) copy-start(s32[1,1024]{1,0:T(1,128)} %get-tuple-element.40.place_ref) | copy-start | bytes 12292
  63.6 33.9 %copy-start.5 = (bf16[256,1024]{1,0:T(8,128)(2,1)S(1)}, bf16[256,1024]{1,0:T(8,128)(2,1)}, u32[]{:S(2)}) copy-start(bf16[256,1024]{1,0:T(8,128)(2,1)} %constant.11.clone.lines_table) | copy-start | bytes 1572868
  63.7 44.8 %slice-start = ((s8[8388608]{0:T(1024)(128)(4,1)}), s8[4194304]{0:T(1024)(128)(4,1)S(1)}, s32[]{:S(2)}) async-start(s8[8388608]{0:T(1024)(128)(4,1)} %bitcast.7), calls=%async_computation.3 | async-start | bytes 8388608
  63.7 42.0 %copy-start.2 = (bf16[128,256]{1,0:T(8,128)(2,1)S(1)}, bf16[128,256]{1,0:T(8,128)(2,1)}, u32[]{:S(2)}) copy-start(bf16[128,256]{1,0:T(8,128)(2,1)} %constant.12.clone.table) | copy-start | bytes 196612
  63.7 44.8 %slice-start.1 = ((s8[8388608]{0:T(1024)(128)(4,1)}), s8[4194304]{0:T(1024)(128)(4,1)S(1)}, s32[]{:S(2)}) async-start(s8[8388608]{0:T(1024)(128)(4,1)} %bitcast.7), calls=%async_computation.4 | async-start | bytes 8388608
  63.7 44.8 %copy-start = (bf16[1024,256]{1,0:T(8,128)(2,1)S(1)}, bf16[1024,256]{1,0:T(8,128)(2,1)}, u32[]{:S(2)}) copy-start(bf16[1024,256]{1,0:T(8,128)(2,1)} %constant.13.clone.table_ref) | copy-start | bytes 1572868
  63.7 44.7 %copy-start.3 = (s32[256]{0:T(256)S(1)}, s32[256]{0:T(256)}, u32[]{:S(2)}) copy-start(s32[256]{0:T(256)} %cell_smem.5) | copy-start | bytes 3076
  97.5 18.6 %copy-start.1 = (bf16[1024,128]{1,0:T(8,128)(2,1)S(1)}, bf16[1024,128]{1,0:T(8,128)(2,1)}, u32[]{:S(2)}) copy-start(bf16[1024,128]{1,0:T(8,128)(2,1)} %constant.14.clone.table_ref) | copy-start | bytes 786436
  99.1 2.8 %collective-permute-start.4 = (bf16[64,512]{1,0:T(8,128)(2,1)S(1)}, bf16[64,512]{1,0:T(8,128)(2,1)S(1)}, u32[]{:S(2)}, u32[]{:S(2)}) collective-permute-start(bf16[64,512]{1,0:T(8,128)(2,1)S(1)} %get-tuple-element.43), channel_id=1, source_target_pairs={{0,4},{8,12},{16,20},{24,28},{4,0},{12,8},{20,16},{28,24},{1,5},{9... | collective-permute-start | bytes 196616 | tf_op jit(solution)/shard_map/ppermute | solution.py:599
  100.7 5.0 %collective-permute-start.5 = (bf16[64,512]{1,0:T(8,128)(2,1)S(1)}, bf16[64,512]{1,0:T(8,128)(2,1)S(1)}, u32[]{:S(2)}, u32[]{:S(2)}) collective-permute-start(bf16[64,512]{1,0:T(8,128)(2,1)S(1)} %get-tuple-element.44), channel_id=1, source_target_pairs={{4,8},{12,16},{20,24},{28,0},{8,4},{16,12},{24,20},{0,28},{5,9},{1... | collective-permute-start | bytes 196616 | tf_op jit(solution)/shard_map/ppermute | solution.py:600
  105.9 10.2 %collective-permute-start.6 = (bf16[64,512]{1,0:T(8,128)(2,1)S(1)}, bf16[64,512]{1,0:T(8,128)(2,1)S(1)}, u32[]{:S(2)}, u32[]{:S(2)}) collective-permute-start(bf16[64,512]{1,0:T(8,128)(2,1)S(1)} %get-tuple-element.47), channel_id=1, source_target_pairs={{0,1},{2,3},{1,0},{3,2},{4,5},{6,7},{5,4},{7,6},{8,9},{10,11},{9,8... | collective-permute-start | bytes 196616 | tf_op jit(solution)/shard_map/ppermute | solution.py:599
  107.5 8.6 %collective-permute-start.7 = (bf16[64,512]{1,0:T(8,128)(2,1)S(1)}, bf16[64,512]{1,0:T(8,128)(2,1)S(1)}, u32[]{:S(2)}, u32[]{:S(2)}) collective-permute-start(bf16[64,512]{1,0:T(8,128)(2,1)S(1)} %get-tuple-element.48), channel_id=1, source_target_pairs={{1,2},{3,0},{2,1},{0,3},{5,6},{7,4},{6,5},{4,7},{9,10},{11,8},{10,... | collective-permute-start | bytes 196616 | tf_op jit(solution)/shard_map/ppermute | solution.py:600
  (1 other events, 0.6 us)

commit v2 on v1

--- a/solution.py
+++ b/solution.py
@@ -716,33 +716,43 @@
 
 
 def physics_kernel(
-    fields, incoming_ref, q_ref, inverse_hbm, out_ref, inverse, pick, physics, tendency, sem
+    fields, incoming_ref, q_ref, inverse_hbm, out_ref, inverse, tendency, sem
 ):
     count, width = incoming_ref.shape
     levels = width // fields
     copy = pltpu.make_async_copy(inverse_hbm, inverse, sem)
     copy.start()
     q = q_ref[...]
-    for start in range(0, count, 128):
-        column = as_columns(q, start)
-        for other in range(0, count, 128):
-            pick[start : start + 128, other : other + 128] = one_hot(
-                column == iota((128, 128), 1) + other
+    size = count // PARTS
+    for part in range(PARTS):
+        pick = []
+        for start in range(part * size, (part + 1) * size, 128):
+            column = as_columns(q, start)
+            pick.append(
+                jnp.concatenate(
+                    [
+                        one_hot(column == iota((128, 128), 1) + other)
+                        for other in range(0, count, 128)
+                    ],
+                    axis=1,
+                )
             )
-    physics[...] = dot(pick[...], incoming_ref[...])
-    copy.wait()
-    for start in range(0, count, 128):
-        pick[start : start + 128] = one_hot(q == iota((128, count), 0) + start)
-    for group in range(count // GROUP_COLS):
-        at = slice(group * GROUP_COLS, (group + 1) * GROUP_COLS)
-        stacked = jnp.concatenate(
-            [physics[at, f * levels : (f + 1) * levels] for f in range(fields)], axis=0
-        )
-        result = dot_nt(stacked.astype(BF16), inverse[group]) - stacked
-        tendency[at] = jnp.concatenate(
-            [result[f * GROUP_COLS : (f + 1) * GROUP_COLS] for f in range(fields)], axis=1
-        ).astype(BF16)
-    out_ref[...] = dot(pick[...], tendency[...]).astype(BF16)
+        physics = dot(jnp.concatenate(pick, axis=0), incoming_ref[...])
+        if part == 0:
+            copy.wait()
+        for group in range(size // GROUP_COLS):
+            rows = physics[group * GROUP_COLS : (group + 1) * GROUP_COLS]
+            stacked = jnp.concatenate(
+                [rows[:, f * levels : (f + 1) * levels] for f in range(fields)], axis=0
+            )
+            whole = part * (size // GROUP_COLS) + group
+            result = dot_nt(stacked.astype(BF16), inverse[whole]) - stacked
+            tendency[whole * GROUP_COLS : (whole + 1) * GROUP_COLS] = jnp.concatenate(
+                [result[f * GROUP_COLS : (f + 1) * GROUP_COLS] for f in range(fields)], axis=1
+            ).astype(BF16)
+    for start in range(0, count, size):
+        pick = one_hot(q == iota((size, count), 0) + start)
+        out_ref[start : start + size] = dot(pick, tendency[...]).astype(BF16)
 
 
 def physics_step(incoming, q, inverse, fields):
@@ -754,8 +764,6 @@
         out_specs=VMEM,
         scratch_shapes=[
             pltpu.VMEM(inverse.shape, BF16),
-            pltpu.VMEM((count, count), BF16),
-            pltpu.VMEM((count, width), F32),
             pltpu.VMEM((count, width), BF16),
             pltpu.SemaphoreType.DMA,
         ],
@@ -766,6 +774,7 @@
 
 
 PHYSICS_LIMIT = 16
+PARTS = 2
 
 
 def unpack_kernel(
@@ -811,21 +820,8 @@
     )(received, place, table)
 
 
-def inner_kernel(
-    span_y,
-    cell_smem,
-    dynamics_ref,
-    back_ref,
-    table_ref,
-    out_ref,
-    border_ref,
-    slot_ref,
-    total,
-    buffer,
-    sems,
-):
-    elements, _, width = total.shape
-    fields, levels = buffer.shape[1], buffer.shape[4]
+def inner_kernel(dynamics_ref, back_ref, table_ref, total):
+    width = total.shape[2]
     count = back_ref.shape[0]
 
     def near_sum(row, first, rows, skip):
@@ -843,11 +839,29 @@
         return 0
 
     lax.fori_loop(1, EXD // 2 - 1, middle, 0, unroll=2)
-    for kind in range(4):
-        for k in range(16):
-            tile = (k, (EXD - 1) * EYD + k, k * EYD, k * EYD + EYD - 1)[kind]
-            for f in range(fields):
-                border_ref[kind, f, k] = total[tile, :, f * levels : (f + 1) * levels]
+
+
+def inner_sum(dynamics, back):
+    one = TABLES["final"].reshape(EYD * NP, 3, 64)
+    two = np.zeros((2, EYD * NP, 4, 64))
+    two[0, :, 0:3] = one
+    two[1, :, 1:4] = one
+    table = np.concatenate(hi_lo_arrays(two.reshape(2 * EYD * NP, 256)), axis=0)
+    return pl.pallas_call(
+        inner_kernel,
+        out_shape=jax.ShapeDtypeStruct(dynamics.shape, F32),
+        in_specs=[VMEM] * 3,
+        out_specs=VMEM,
+        input_output_aliases={0: 0},
+        compiler_params=params(16),
+        cost_estimate=cost(4e9, 2e7),
+        name="inner_sum",
+    )(dynamics, back, jnp.asarray(table))
+
+
+def to_slots_kernel(span_y, cell_smem, total, out_ref, slot_ref, buffer, sems):
+    elements, _, width = total.shape
+    fields, levels = buffer.shape[1], buffer.shape[4]
     per = elements // CHUNKS
 
     def copy(chunk):
@@ -872,42 +886,35 @@
         copy(chunk).wait()
 
 
-def inner_sum(cell, dynamics, back, fields, span_y):
-    elements, _, width = dynamics.shape
+def to_slots(cell, total, fields, span_y):
+    elements, _, width = total.shape
     levels = width // fields
-    one = TABLES["final"].reshape(EYD * NP, 3, 64)
-    two = np.zeros((2, EYD * NP, 4, 64))
-    two[0, :, 0:3] = one
-    two[1, :, 1:4] = one
-    table = np.concatenate(hi_lo_arrays(two.reshape(2 * EYD * NP, 256)), axis=0)
     return pl.pallas_call(
-        functools.partial(inner_kernel, span_y),
+        functools.partial(to_slots_kernel, span_y),
         out_shape=(
             jax.ShapeDtypeStruct((fields, elements, NP, levels), F32),
-            jax.ShapeDtypeStruct((4, fields, 16, NP, levels), F32),
             jax.ShapeDtypeStruct((1, elements), I32),
         ),
-        in_specs=[SMEM, VMEM, VMEM, VMEM],
-        out_specs=(ANY, VMEM, SMEM),
+        in_specs=[SMEM, VMEM],
+        out_specs=(ANY, SMEM),
         scratch_shapes=[
-            pltpu.VMEM((elements, NP, width), F32),
             pltpu.VMEM((CHUNKS, fields, elements // CHUNKS, NP, levels), F32),
             pltpu.SemaphoreType.DMA((CHUNKS,)),
         ],
-        compiler_params=params(32),
-        cost_estimate=cost(2e9, 2e7),
-        name="inner_sum",
-    )(cell, dynamics, back, jnp.asarray(table))
+        compiler_params=params(16),
+        cost_estimate=cost(4e9, 2e7),
+        name="to_slots",
+    )(cell, total)
 
 
 def border_kernel(
-    fields, slot_ref, x_one, x_two, y_one, y_two, border_ref, table_ref, _, out_ref, buffer, sem
+    fields, slot_ref, x_one, x_two, y_one, y_two, total_ref, table_ref, _, out_ref, buffer, sem
 ):
     width = x_one.shape[1]
     levels = width // fields
-    adds = []
     halos = from_neighbours("gx", x_one[...], x_two[...])
     halos = halos + from_neighbours("gy", y_one[...], y_two[...])
+    adds = []
     for kind, halo in enumerate(halos):
         table = table_ref[kind * 256 : kind * 256 + 256]
         if kind < 2:
@@ -919,12 +926,12 @@
         for k in range(16):
             if kind >= 2 and k in (0, 15):
                 continue
-            add = adds[kind][k]
+            tile = (k, (EXD - 1) * EYD + k, k * EYD, k * EYD + EYD - 1)[kind]
+            whole = total_ref[tile] + adds[kind][k]
             if kind < 2 and k in (0, 15):
-                add = add + adds[2 if k == 0 else 3][0 if kind == 0 else 15]
+                whole = whole + adds[2 if k == 0 else 3][0 if kind == 0 else 15]
             for f in range(fields):
-                buffer[kind, f, k] = border_ref[kind, f, k] + add[:, f * levels : (f + 1) * levels]
-            tile = (k, (EXD - 1) * EYD + k, k * EYD, k * EYD + EYD - 1)[kind]
+                buffer[kind, f, k] = whole[:, f * levels : (f + 1) * levels]
             pltpu.make_async_copy(
                 buffer.at[kind, :, k], out_ref.at[:, slot_ref[0, tile]], sem.at[kind]
             ).start()
@@ -933,7 +940,7 @@
         pltpu.make_async_copy(part, part, sem.at[kind]).wait()
 
 
-def border_sum(slot, halos, border, out):
+def border_sum(slot, halos, total, out):
     fields, levels = out.shape[0], out.shape[3]
     table = jnp.asarray(TABLES["border"].astype(np.float32).astype(jnp.bfloat16))
     return pl.pallas_call(
@@ -949,7 +956,7 @@
         compiler_params=params(16),
         cost_estimate=cost(2e8, 4e6),
         name="border_sum",
-    )(slot, *halos, border, table, out)
+    )(slot, *halos, total, table, out)
 
 
 def regroup(blocks):
@@ -981,8 +988,9 @@
     back, x_one, x_two, south, north = unpack(received, place)
     bx = exchange("gx", x_one, x_two)
     by = exchange("gy", *messages(*bx, south, north, hi_lo(TABLES["corner_col"])))
-    inner, border, slot = inner_sum(elem_cell, dynamics, back, fields, span_y)
-    return border_sum(slot, (*bx, *by), border, inner)
+    total = inner_sum(dynamics, back)
+    inner, slot = to_slots(elem_cell, total, fields, span_y)
+    return border_sum(slot, (*bx, *by), total, inner)
 
 
 def solution(mesh):

time: 119 us -> 116 us (0.975)
  waiting for transfers between devices: 16.6 us -> 13.8 us
    ppermute x4, waiting for transfers between devices: 7.03 us -> 4.24 us  [exchange(): lax.ppermute(two, axis, pairs(axis, False))]
    pallas_call x1 -> x2, Pallas kernels: 7.66 us -> 7.89 us  [the longest x1 4.65 us: to_slots(): pl.pallas_call(functools.partial(to_slots_kernel, span_y), out_shape=(jax...]
  transfers between devices with their start and end apart: 10 -> 10, of which waited for: 4 -> 5; matrix products, arithmetic and copies ran while one was open for 0% -> 0% of each run, Pallas kernels for 20% -> 21%
where the time goes in v2:
time: 116 us
  Pallas kernels  49.3 us (42%)
  blocking collectives  29.3 us (25%)
  starting transfers between devices  22.1 us (19%)
  waiting for transfers between devices  13.8 us (12%)
    all_to_all x1, blocking collectives, regroup(): lax.all_to_all(blocks, ('gx', 'gy'), split_axis=0, concat_axis=0, tiled=T...  29.3 us
    pallas_call x1, Pallas kernels, dynamics_rows(): pl.pallas_call(functools.partial(dynamics_kernel, span_y), out_shape=jax....  16.1 us
    pallas_call x1, Pallas kernels, front(): pl.pallas_call(functools.partial(front_kernel, sizes, EYD * sizes[1]), ou...  12.1 us
    all_to_all x2, starting transfers between devices, regroup(): lax.all_to_all(blocks, ('gx', 'gy'), split_axis=0, concat_axis=0, tiled=T...  10.1 us
    all_to_all x2, waiting for transfers between devices, regroup(): lax.all_to_all(blocks, ('gx', 'gy'), split_axis=0, concat_axis=0, tiled=T...  8.91 us
    ppermute x4, starting transfers between devices, exchange(): lax.ppermute(two, axis, pairs(axis, False))  6.96 us
    pallas_call x1, Pallas kernels, send_columns(): pl.pallas_call(functools.partial(send_kernel, sizes, EYD * sizes[1]), out...  5.11 us
    ppermute x4, starting transfers between devices, exchange(): lax.ppermute(one, axis, pairs(axis, True))  5.06 us
  transfers between devices with their start and end apart: 10, of which 5 were waited for; matrix products, arithmetic and copies ran while one was open for 0% of the time, Pallas kernels for 21%

profile of v2, /device:TPU:0, one launch (start us, length us, event | category | flops | bytes accessed | tf_op | source)
XLA Modules:
  0.0 115.7 jit_solution(4738252174202327983)
XLA Ops:
  0.0 12.1 %front.1 = (f32[1024,512]{1,0:T(8,128)}, f32[32,8,128]{2,1,0:T(8,128)}, s32[1,1024]{1,0:T(1,128)}, bf16[64,512]{1,0:T(8,128)(2,1)}, bf16[64,512]{1,0:T(8,128)(2,...) custom-call(s32[256]{0:T(256)} %cell_smem.5, s32[1,256]{1,0:T(1,128)} %bitcast.12, s32[1,1024]{1,0:T(1,128)} %bitcast.18, ...), custom_call_target="tpu_custom_call" | custom-call | flops 4000000000 | bytes 20000000 | tf_op jit(solution)/shard_map/front/pallas_call | solution.py:431
  12.1 7.3 %all-to-all-start = ((f32[32,8,128]{2,1,0:T(8,128)}), f32[32,8,128]{2,1,0:T(8,128)S(1)}, u32[]{:S(2)}, u32[]{:S(2)}) async-start(f32[32,8,128]{2,1,0:T(8,128)} %get-tuple-element.32), calls=%async_computation | async-start | bytes 262144 | tf_op jit(solution)/shard_map/all_to_all | solution.py:963
  19.7 2.5 %collective-permute-start.1 = (bf16[64,512]{1,0:T(8,128)(2,1)}, bf16[64,512]{1,0:T(8,128)(2,1)S(1)}, u32[]{:S(2)}, u32[]{:S(2)}) collective-permute-start(bf16[64,512]{1,0:T(8,128)(2,1)} %get-tuple-element.29), channel_id=1, source_target_pairs={{4,8},{12,16},{20,24},{28,0},{8,4},{16,12},{24,20},{0,28},{5,9},{1... | collective-permute-start | bytes 196616 | tf_op jit(solution)/shard_map/ppermute | solution.py:600
  22.3 1.5 %collective-permute-start.2 = (bf16[64,512]{1,0:T(8,128)(2,1)}, bf16[64,512]{1,0:T(8,128)(2,1)S(1)}, u32[]{:S(2)}, u32[]{:S(2)}) collective-permute-start(bf16[64,512]{1,0:T(8,128)(2,1)} %get-tuple-element.30), channel_id=1, source_target_pairs={{0,1},{2,3},{1,0},{3,2},{4,5},{6,7},{5,4},{7,6},{8,9},{10,11},{9,8... | collective-permute-start | bytes 196616 | tf_op jit(solution)/shard_map/ppermute | solution.py:599
  23.7 2.4 %collective-permute-start.3 = (bf16[64,512]{1,0:T(8,128)(2,1)}, bf16[64,512]{1,0:T(8,128)(2,1)S(1)}, u32[]{:S(2)}, u32[]{:S(2)}) collective-permute-start(bf16[64,512]{1,0:T(8,128)(2,1)} %get-tuple-element.31), channel_id=1, source_target_pairs={{1,2},{3,0},{2,1},{0,3},{5,6},{7,4},{6,5},{4,7},{9,10},{11,8},{10,... | collective-permute-start | bytes 196616 | tf_op jit(solution)/shard_map/ppermute | solution.py:600
  26.1 0.7 collective-permute-done.2.y_one
  26.8 3.2 %collective-permute-done.3.y_two = bf16[64,512]{1,0:T(8,128)(2,1)S(1)} collective-permute-done((bf16[64,512]{1,0:T(8,128)(2,1)}, bf16[64,512]{1,0:T(8,128)(2,1)S(1)}, u32[]{:S(2)}, u32[]{:S(2)}) %collective-permute-start.3) | collective-permute-done | bytes 65568 | tf_op jit(solution)/shard_map/ppermute | solution.py:600
  30.0 0.6 copy-done.12
  30.7 5.1 %send_columns.1 = (bf16[1024,512]{1,0:T(8,128)(2,1)}, s32[1,1024]{1,0:T(1,128)}, f32[64,512]{1,0:T(8,128)}, f32[64,512]{1,0:T(8,128)}) custom-call(f32[1024,512]{1,0:T(8,128)} %get-tuple-element.27.columns_hbm, bf16[1152,256]{1,0:T(8,128)(2,1)} %constant.10.clone.table_hbm, bf16[64,512]{1,0:T(8,128)(2,1)} %copy-done.9, bf16[64,512]{1,0:T(8,128)(2,1)} %copy-done.10, ...), custom_call_target="tpu_custom_call" | custom-call | flops 2000000000 | bytes 5000000 | tf_op jit(solution)/shard_map/send_columns/pallas_call | solution.py:691
  35.8 2.8 %all-to-all-start.1 = ((bf16[32,32,512]{2,1,0:T(8,128)(2,1)}), bf16[32,32,512]{2,1,0:T(8,128)(2,1)S(1)}, u32[]{:S(2)}, u32[]{:S(2)}) async-start(bf16[32,32,512]{2,1,0:T(8,128)(2,1)} %bitcast.15), calls=%async_computation.1 | async-start | bytes 2097152 | tf_op jit(solution)/shard_map/all_to_all | solution.py:963
  38.6 16.1 %dynamics_rows.1.dynamics_ref = f32[256,16,512]{2,1,0:T(8,128)} custom-call(s32[256]{0:T(256)} %cell_smem.5, s32[1,256]{1,0:T(1,128)} %bitcast.14, f32[256,256]{1,0:T(8,128)} %bitcast.17, f32[4,256,16,128]{3,2,1,0:T(8,128)} %state_ref.3, bf16[64,512]{1,0:T(8,128)(2,1)} %copy-done.9, bf16[64,512]{1,0:T(8,128)(2,1)} %copy-done.10, ...), custom_call_target="tpu_custom_call" | custom-call | flops 4000000000 | bytes 20000000 | tf_op jit(solution)/shard_map/dynamics_rows/pallas_call | solution.py:552
  54.7 8.9 %all-to-all-done.1 = bf16[32,32,512]{2,1,0:T(8,128)(2,1)S(1)} async-done(((bf16[32,32,512]{2,1,0:T(8,128)(2,1)}), bf16[32,32,512]{2,1,0:T(8,128)(2,1)S(1)}, u32[]{:S(2)}, u32[]{:S(2)}) %all-to-all-start.1) | async-done | bytes 1048608 | tf_op jit(solution)/shard_map/all_to_all | solution.py:963
  63.7 4.3 %physics.1 = bf16[1024,512]{1,0:T(8,128)(2,1)S(1)} custom-call(bf16[1024,512]{1,0:T(8,128)(2,1)S(1)} %bitcast.9, s32[1,1024]{1,0:T(1,128)S(1)} %copy-done.7, bf16[64,128,128]{2,1,0:T(8,128)(2,1)S(1)} %copy-done.4), custom_call_target="tpu_custom_call" | custom-call | flops 3000000000 | bytes 5000000 | tf_op jit(solution)/shard_map/physics/pallas_call | solution.py:760
  68.0 29.3 %all_to_all.28 = bf16[32,32,512]{2,1,0:T(8,128)(2,1)S(1)} all-to-all(bf16[32,32,512]{2,1,0:T(8,128)(2,1)S(1)} %bitcast.11), channel_id=1, replica_groups=mesh['gx'=8,'gy'=4] {'gx','gy'}, dimensions={0} | all-to-all | bytes 2097152 | tf_op jit(solution)/shard_map/all_to_all | solution.py:963
  97.3 1.5 %unpack.1 = (bf16[1024,512]{1,0:T(8,128)(2,1)S(1)}, bf16[64,512]{1,0:T(8,128)(2,1)S(1)}, bf16[64,512]{1,0:T(8,128)(2,1)S(1)}, f32[64,512]{1,0:T(8,128)S(1)}, f32[64,512]{1,0:T(8,128)S(1)}) custom-call(bf16[1024,512]{1,0:T(8,128)(2,1)S(1)} %bitcast.10, s32[1,1024]{1,0:T(1,128)S(1)} %copy-done.6, bf16[256,1024]{1,0:T(8,128)(2,1)S(1)} %copy-done.5), custom_call_target="tpu_custom_call" | custom-call | flops 2000000000 | bytes 4000000 | tf_op jit(solution)/shard_map/unpack/pallas_call | solution.py:805
  98.8 1.6 %collective-permute-start.4 = (bf16[64,512]{1,0:T(8,128)(2,1)S(1)}, bf16[64,512]{1,0:T(8,128)(2,1)S(1)}, u32[]{:S(2)}, u32[]{:S(2)}) collective-permute-start(bf16[64,512]{1,0:T(8,128)(2,1)S(1)} %get-tuple-element.42), channel_id=1, source_target_pairs={{0,4},{8,12},{16,20},{24,28},{4,0},{12,8},{20,16},{28,24},{1,5},{9... | collective-permute-start | bytes 196616 | tf_op jit(solution)/shard_map/ppermute | solution.py:599
  100.4 1.1 collective-permute-start.5
  101.6 3.2 %inner_sum.1.total.total_ref = f32[256,16,512]{2,1,0:T(8,128)S(1)} custom-call(f32[256,16,512]{2,1,0:T(8,128)S(1)} %bitcast.8, bf16[1024,512]{1,0:T(8,128)(2,1)S(1)} %get-tuple-element.40.back_ref, bf16[1024,256]{1,0:T(8,128)(2,1)S(1)} %copy-done), custom_call_target="tpu_custom_call", output_to_operand_aliasing={{}: (0, {})} | custom-call | flops 4000000000 | bytes 20000000 | tf_op jit(solution)/shard_map/inner_sum/pallas_call | solution.py:850
  104.9 0.6 collective-permute-done.5.x_two
  105.7 1.7 %collective-permute-start.6 = (bf16[64,512]{1,0:T(8,128)(2,1)S(1)}, bf16[64,512]{1,0:T(8,128)(2,1)S(1)}, u32[]{:S(2)}, u32[]{:S(2)}) collective-permute-start(bf16[64,512]{1,0:T(8,128)(2,1)S(1)} %get-tuple-element.46), channel_id=1, source_target_pairs={{0,1},{2,3},{1,0},{3,2},{4,5},{6,7},{5,4},{7,6},{8,9},{10,11},{9,8... | collective-permute-start | bytes 196616 | tf_op jit(solution)/shard_map/ppermute | solution.py:599
  107.3 0.9 collective-permute-start.7
  108.2 4.7 %to_slots.1 = (f32[4,256,16,128]{3,2,1,0:T(8,128)}, s32[1,256]{1,0:T(1,128)S(1)}) custom-call(s32[256]{0:T(256)S(1)} %copy-done.3, f32[256,16,512]{2,1,0:T(8,128)S(1)} %inner_sum.1.total.total_ref), custom_call_target="tpu_custom_call" | custom-call | flops 4000000000 | bytes 20000000 | tf_op jit(solution)/shard_map/to_slots/pallas_call | solution.py:892
  112.9 0.5 collective-permute-done.7.y_two
  113.4 2.1 %border_sum.1 = f32[4,256,16,128]{3,2,1,0:T(8,128)} custom-call(s32[1,256]{1,0:T(1,128)S(1)} %get-tuple-element.41.slot_ref, bf16[64,512]{1,0:T(8,128)(2,1)S(1)} %collective-permute-done.4.x_one, bf16[64,512]{1,0:T(8,128)(2,1)S(1)} %collective-permute-done.5.x_two, bf16[64,512]{1,0:T(8,128)(2,1)S(1)} %collective-permute-done.6.y_one, ...), custom_call_target="tpu_custom_call", output_to_operand_aliasing={{}: (7, {})} | custom-call | flops 200000000 | bytes 4000000 | tf_op jit(solution)/shard_map/border_sum/pallas_call | solution.py:946
  (37 shorter events, 0.6 us)
Async XLA Ops:
  12.1 17.9 %all-to-all-start = ((f32[32,8,128]{2,1,0:T(8,128)}), f32[32,8,128]{2,1,0:T(8,128)S(1)}, u32[]{:S(2)}, u32[]{:S(2)}) async-start(f32[32,8,128]{2,1,0:T(8,128)} %get-tuple-element.32), calls=%async_computation | async-start | bytes 262144 | tf_op jit(solution)/shard_map/all_to_all | solution.py:963
  19.4 6.7 %collective-permute-start = (bf16[64,512]{1,0:T(8,128)(2,1)}, bf16[64,512]{1,0:T(8,128)(2,1)S(1)}, u32[]{:S(2)}, u32[]{:S(2)}) collective-permute-start(bf16[64,512]{1,0:T(8,128)(2,1)} %get-tuple-element.28), channel_id=1, source_target_pairs={{0,4},{8,12},{16,20},{24,28},{4,0},{12,8},{20,16},{28,24},{1,5},{9... | collective-permute-start | bytes 196616 | tf_op jit(solution)/shard_map/ppermute | solution.py:599
  19.7 6.4 %collective-permute-start.1 = (bf16[64,512]{1,0:T(8,128)(2,1)}, bf16[64,512]{1,0:T(8,128)(2,1)S(1)}, u32[]{:S(2)}, u32[]{:S(2)}) collective-permute-start(bf16[64,512]{1,0:T(8,128)(2,1)} %get-tuple-element.29), channel_id=1, source_target_pairs={{4,8},{12,16},{20,24},{28,0},{8,4},{16,12},{24,20},{0,28},{5,9},{1... | collective-permute-start | bytes 196616 | tf_op jit(solution)/shard_map/ppermute | solution.py:600
  22.3 4.6 %collective-permute-start.2 = (bf16[64,512]{1,0:T(8,128)(2,1)}, bf16[64,512]{1,0:T(8,128)(2,1)S(1)}, u32[]{:S(2)}, u32[]{:S(2)}) collective-permute-start(bf16[64,512]{1,0:T(8,128)(2,1)} %get-tuple-element.30), channel_id=1, source_target_pairs={{0,1},{2,3},{1,0},{3,2},{4,5},{6,7},{5,4},{7,6},{8,9},{10,11},{9,8... | collective-permute-start | bytes 196616 | tf_op jit(solution)/shard_map/ppermute | solution.py:599
  23.7 6.3 %collective-permute-start.3 = (bf16[64,512]{1,0:T(8,128)(2,1)}, bf16[64,512]{1,0:T(8,128)(2,1)S(1)}, u32[]{:S(2)}, u32[]{:S(2)}) collective-permute-start(bf16[64,512]{1,0:T(8,128)(2,1)} %get-tuple-element.31), channel_id=1, source_target_pairs={{1,2},{3,0},{2,1},{0,3},{5,6},{7,4},{6,5},{4,7},{9,10},{11,8},{10,... | collective-permute-start | bytes 196616 | tf_op jit(solution)/shard_map/ppermute | solution.py:600
  26.1 3.9 %copy-start.9 = (bf16[64,512]{1,0:T(8,128)(2,1)}, bf16[64,512]{1,0:T(8,128)(2,1)S(1)}, u32[]{:S(2)}) copy-start(bf16[64,512]{1,0:T(8,128)(2,1)S(1)} %collective-permute-done.x_one.hx_one) | copy-start | bytes 196612
  26.1 3.9 %copy-start.10 = (bf16[64,512]{1,0:T(8,128)(2,1)}, bf16[64,512]{1,0:T(8,128)(2,1)S(1)}, u32[]{:S(2)}) copy-start(bf16[64,512]{1,0:T(8,128)(2,1)S(1)} %collective-permute-done.1.x_two.hx_two) | copy-start | bytes 196612
  26.8 3.2 %copy-start.11 = (bf16[64,512]{1,0:T(8,128)(2,1)}, bf16[64,512]{1,0:T(8,128)(2,1)S(1)}, u32[]{:S(2)}) copy-start(bf16[64,512]{1,0:T(8,128)(2,1)S(1)} %collective-permute-done.2.y_one) | copy-start | bytes 196612
  30.0 0.7 copy-start.8
  35.8 27.9 %all-to-all-start.1 = ((bf16[32,32,512]{2,1,0:T(8,128)(2,1)}), bf16[32,32,512]{2,1,0:T(8,128)(2,1)S(1)}, u32[]{:S(2)}, u32[]{:S(2)}) async-start(bf16[32,32,512]{2,1,0:T(8,128)(2,1)} %bitcast.15), calls=%async_computation.1 | async-start | bytes 2097152 | tf_op jit(solution)/shard_map/all_to_all | solution.py:963
  38.6 25.1 %copy-start.4 = (bf16[64,128,128]{2,1,0:T(8,128)(2,1)S(1)}, bf16[64,128,128]{2,1,0:T(8,128)(2,1)}, u32[]{:S(2)}) copy-start(bf16[64,128,128]{2,1,0:T(8,128)(2,1)} %inverse_hbm.1) | copy-start | bytes 6291460
  38.6 25.1 %copy-start.7 = (s32[1,1024]{1,0:T(1,128)S(1)}, s32[1,1024]{1,0:T(1,128)}, u32[]{:S(2)}) copy-start(s32[1,1024]{1,0:T(1,128)} %get-tuple-element.38.q_ref) | copy-start | bytes 12292
  54.7 42.6 %copy-start.6 = (s32[1,1024]{1,0:T(1,128)S(1)}, s32[1,1024]{1,0:T(1,128)}, u32[]{:S(2)}) copy-start(s32[1,1024]{1,0:T(1,128)} %get-tuple-element.39.place_ref) | copy-start | bytes 12292
  63.6 33.7 %copy-start.5 = (bf16[256,1024]{1,0:T(8,128)(2,1)S(1)}, bf16[256,1024]{1,0:T(8,128)(2,1)}, u32[]{:S(2)}) copy-start(bf16[256,1024]{1,0:T(8,128)(2,1)} %constant.11.clone.lines_table) | copy-start | bytes 1572868
  63.7 37.9 %slice-start = ((s8[8388608]{0:T(1024)(128)(4,1)}), s8[4194304]{0:T(1024)(128)(4,1)S(1)}, s32[]{:S(2)}) async-start(s8[8388608]{0:T(1024)(128)(4,1)} %bitcast.7), calls=%async_computation.3 | async-start | bytes 8388608
  63.7 37.9 %slice-start.1 = ((s8[8388608]{0:T(1024)(128)(4,1)}), s8[4194304]{0:T(1024)(128)(4,1)S(1)}, s32[]{:S(2)}) async-start(s8[8388608]{0:T(1024)(128)(4,1)} %bitcast.7), calls=%async_computation.4 | async-start | bytes 8388608
  63.7 37.9 %copy-start = (bf16[1024,256]{1,0:T(8,128)(2,1)S(1)}, bf16[1024,256]{1,0:T(8,128)(2,1)}, u32[]{:S(2)}) copy-start(bf16[1024,256]{1,0:T(8,128)(2,1)} %constant.13.clone.table_ref) | copy-start | bytes 1572868
  98.8 6.0 %collective-permute-start.4 = (bf16[64,512]{1,0:T(8,128)(2,1)S(1)}, bf16[64,512]{1,0:T(8,128)(2,1)S(1)}, u32[]{:S(2)}, u32[]{:S(2)}) collective-permute-start(bf16[64,512]{1,0:T(8,128)(2,1)S(1)} %get-tuple-element.42), channel_id=1, source_target_pairs={{0,4},{8,12},{16,20},{24,28},{4,0},{12,8},{20,16},{28,24},{1,5},{9... | collective-permute-start | bytes 196616 | tf_op jit(solution)/shard_map/ppermute | solution.py:599
  100.4 5.0 %collective-permute-start.5 = (bf16[64,512]{1,0:T(8,128)(2,1)S(1)}, bf16[64,512]{1,0:T(8,128)(2,1)S(1)}, u32[]{:S(2)}, u32[]{:S(2)}) collective-permute-start(bf16[64,512]{1,0:T(8,128)(2,1)S(1)} %get-tuple-element.43), channel_id=1, source_target_pairs={{4,8},{12,16},{20,24},{28,0},{8,4},{16,12},{24,20},{0,28},{5,9},{1... | collective-permute-start | bytes 196616 | tf_op jit(solution)/shard_map/ppermute | solution.py:600
  101.6 3.9 %copy-start.2 = (bf16[128,256]{1,0:T(8,128)(2,1)S(1)}, bf16[128,256]{1,0:T(8,128)(2,1)}, u32[]{:S(2)}) copy-start(bf16[128,256]{1,0:T(8,128)(2,1)} %constant.12.clone.table) | copy-start | bytes 196612
  101.6 6.6 %copy-start.3 = (s32[256]{0:T(256)S(1)}, s32[256]{0:T(256)}, u32[]{:S(2)}) copy-start(s32[256]{0:T(256)} %cell_smem.5) | copy-start | bytes 3076
  104.9 8.5 %copy-start.1 = (bf16[1024,128]{1,0:T(8,128)(2,1)S(1)}, bf16[1024,128]{1,0:T(8,128)(2,1)}, u32[]{:S(2)}) copy-start(bf16[1024,128]{1,0:T(8,128)(2,1)} %constant.14.clone.table_ref) | copy-start | bytes 786436
  105.7 7.2 %collective-permute-start.6 = (bf16[64,512]{1,0:T(8,128)(2,1)S(1)}, bf16[64,512]{1,0:T(8,128)(2,1)S(1)}, u32[]{:S(2)}, u32[]{:S(2)}) collective-permute-start(bf16[64,512]{1,0:T(8,128)(2,1)S(1)} %get-tuple-element.46), channel_id=1, source_target_pairs={{0,1},{2,3},{1,0},{3,2},{4,5},{6,7},{5,4},{7,6},{8,9},{10,11},{9,8... | collective-permute-start | bytes 196616 | tf_op jit(solution)/shard_map/ppermute | solution.py:599
  107.3 6.1 %collective-permute-start.7 = (bf16[64,512]{1,0:T(8,128)(2,1)S(1)}, bf16[64,512]{1,0:T(8,128)(2,1)S(1)}, u32[]{:S(2)}, u32[]{:S(2)}) collective-permute-start(bf16[64,512]{1,0:T(8,128)(2,1)S(1)} %get-tuple-element.47), channel_id=1, source_target_pairs={{1,2},{3,0},{2,1},{0,3},{5,6},{7,4},{6,5},{4,7},{9,10},{11,8},{10,... | collective-permute-start | bytes 196616 | tf_op jit(solution)/shard_map/ppermute | solution.py:600
  (1 other events, 0.6 us)

commit v3 on v2

--- a/solution.py
+++ b/solution.py
@@ -71,15 +71,10 @@
     w = ONE_D
     eye = np.eye(EXD)
     line = local_pass(EYD)
-    col_x = []
-    for a in (0, 3):
-        col_x.append(
-            np.einsum("i,jb,b,byez->ijyez", h[:, a] * w[a], h, w, line).reshape(4 * EYD, 4 * EYD)
-        )
-    col_y = np.zeros((EXD, 2, 2, EYD, 2, 4, EXD))
+    col_y = np.zeros((EXD, 2, 2, EYD, 2, 2, EXD))
     for side, (b, y) in enumerate(((0, 0), (3, EYD - 1))):
-        col_y[:, :, :, y, side] = np.einsum("ia,j,xz->xijaz", h * w, h[:, b] * w[b], eye)
-    col_y = col_y.reshape(EXD * 4 * EYD, 2 * 4 * EXD)
+        col_y[:, :, :, y, side] = np.einsum("j,ik,xz->xijkz", h[:, b] * w[b], np.eye(2), eye)
+    col_y = col_y.reshape(EXD * 4 * EYD, 2 * 2 * EXD)
     nodes = np.einsum("ai,bj,yz->abyijz", s, s, np.eye(EYD))
     across = np.zeros((4, 4, EYD, 3, 2, 2, EYD))
     across[:, :, :, 1] = nodes
@@ -90,34 +85,29 @@
     final = full.reshape(NP * EYD, 3 * 4 * EYD)
     along = local_pass(EXD)
     lines = np.zeros((2, 4, EXD, EXD, 2, 2, EYD))
-    corner_col = np.zeros((2, 4, EXD, 2, 2, 2, EYD))
     corner_pt = np.zeros((2, 4, EXD, 2, 4, EYD))
     for side, (b, y) in enumerate(((0, 0), (3, EYD - 1))):
         lines[side, :, :, :, :, :, y] = np.einsum("axcz,ci,j->axzij", along, s, s[b])
-        corner_col[side, 0, 0, 0, :, :, y] = np.outer(s[3], s[b])
-        corner_col[side, 3, EXD - 1, 1, :, :, y] = np.outer(s[0], s[b])
         corner_pt[side, 0, 0, 0, b, y] = 1.0
         corner_pt[side, 3, EXD - 1, 1, b, y] = 1.0
     lines = lines.reshape(2 * 4 * EXD, EXD * 4 * EYD)
-    corner_col = corner_col.reshape(2 * 4 * EXD, 2 * 4 * EYD)
     corner_pt = corner_pt.reshape(2 * 4 * EXD, 2 * 4 * EYD)
-    border = np.zeros((4, EYD, NP, 128))
+    border = np.zeros((4, EYD, NP, 64))
     order = full.transpose(2, 0, 1, 3, 4, 5, 6).reshape(EYD, NP, 3, 4 * EYD)
-    west, east = hi_lo_arrays(order[:, :, 0]), hi_lo_arrays(order[:, :, 2])
-    border[0] = np.concatenate(west, axis=-1)
-    border[1] = np.concatenate(east, axis=-1)
+    for kind, a in enumerate((0, 3)):
+        border[kind, :, 4 * a : 4 * a + 4] = np.einsum("b,byez->ybez", w[a] * w, line).reshape(
+            EYD, 4, 4 * EYD
+        )
     for side, b in enumerate((0, 3)):
         for a in range(4):
             for x in range(EXD):
                 border[2 + side, x, 4 * a + b, 16 * a + x] = w[a] * w[b]
     return dict(
-        col_x=np.concatenate(col_x, axis=0),
         col_y=col_y,
         final=order.reshape(EYD * NP, 3 * 4 * EYD),
         lines=lines,
-        corner_col=corner_col,
         corner_pt=corner_pt,
-        border=border.reshape(4 * EYD * NP, 128),
+        border=border.reshape(4 * EYD * NP, 64),
     )
 
 
@@ -132,6 +122,10 @@
 
 
 TABLES = constant_tables()
+
+
+def bf16_table(name):
+    return jnp.asarray(TABLES[name].astype(np.float32).astype(jnp.bfloat16))
 
 
 def dot(left, right):
@@ -203,8 +197,7 @@
     of_rank = one_hot(rank == iota((128, columns_dev), 0))
     high = jnp.where(of_source, (local >> 5).astype(F32), 0.0).astype(BF16)
     low = jnp.where(of_source, (local & 31).astype(F32), 0.0).astype(BF16)
-    wanted = dot_nt(high, of_rank) * 32.0 + dot_nt(low, of_rank)
-    return wanted, source * per_peer + rank
+    return dot_nt(high, of_rank), dot_nt(low, of_rank), source * per_peer + rank
 
 
 def diagonal(sizes, step_x, step_y):
@@ -293,6 +286,26 @@
         nodes[4 * a + 3] = last + shifted(first, -1)
 
 
+def summed_line(line):
+    first, last = line[0:16], line[48:64]
+    return jnp.concatenate(
+        [first + shifted(last, 1), line[16:48], last + shifted(first, -1)], axis=0
+    )
+
+
+def averaged(line):
+    line = summed_line(line)
+    return jnp.concatenate(
+        [
+            sum(
+                float(HALVES[i, a] * ONE_D[a]) * line[16 * a : 16 * a + 16] for a in range(4)
+            )
+            for i in range(2)
+        ],
+        axis=0,
+    )
+
+
 def held_nodes(held, before, next_first):
     nodes = [held[16 * n : 16 * n + 16] for n in range(NP)]
     for b in range(4):
@@ -311,7 +324,7 @@
     stiff_ref,
     state_ref,
     columns_out,
-    blocks_ref,
+    blocks_out,
     q_ref,
     x_one,
     x_two,
@@ -327,6 +340,7 @@
     lines,
     ends,
     columns,
+    blocks_ref,
     out_sem,
 ):
     devices = sizes[0] * sizes[1]
@@ -334,10 +348,11 @@
     for chunk in range(CHUNKS):
         state_copy(state_ref, raw, sems, chunk).start()
     place_operators(tile_operators(span_y, cell_ref[...], stiff_ref[...]), operators)
-    wanted, q_ref[...] = column_requests(
+    high, low, q_ref[...] = column_requests(
         devices, group_ref.shape[1] // devices, group_ref[...]
     )
-    blocks_ref[...] = jnp.broadcast_to(wanted[:, None, :], (devices, 8, 128))
+    first = iota((devices, 8, 128), 1) == 0
+    blocks_ref[...] = jnp.where(first, high[:, None, :], low[:, None, :])
     place_states(span_y, cell_smem, state_ref, raw, sems, hi_ref, lo_ref)
     before[...] = jnp.zeros_like(before)
     held[...] = jnp.zeros_like(held)
@@ -382,19 +397,11 @@
     lax.fori_loop(EXD // 2 + 2, EXD, one_row, 0, unroll=2)
     emit(EXD - 1, None)
     send(1).start()
-    whole = []
-    for side in range(2):
-        first, last = lines[side, 0:16], lines[side, 48:64]
-        whole.append(
-            jnp.concatenate(
-                [first + shifted(last, 1), lines[side, 16:48], last + shifted(first, -1)], axis=0
-            )
-        )
     for axis, low, high, one, two in (
         ("gx", ends[0, 0], ends[1, 1], x_one, x_two),
-        ("gy", whole[0], whole[1], y_one, y_two),
+        ("gy", lines[0], lines[1], y_one, y_two),
     ):
-        first, second = by_parity(axis, low, high)
+        first, second = by_parity(axis, averaged(low), averaged(high))
         one[...] = first.astype(BF16)
         two[...] = second.astype(BF16)
     for step_x, row in ((-1, 0), (1, 3 * 16 + 15)):
@@ -402,7 +409,8 @@
             block = diagonal(sizes, step_x, step_y)
             point = lines[side, row : row + 1]
             for f in range(width // 128):
-                blocks_ref[block, 1 + f : 2 + f] = point[:, f * 128 : (f + 1) * 128]
+                blocks_ref[block, 2 + f : 3 + f] = point[:, f * 128 : (f + 1) * 128]
+    blocks_out[...] = blocks_ref[...].astype(BF16)
     send(0).wait()
     send(1).wait()
 
@@ -427,12 +435,12 @@
     fields, elements, _, levels = state.shape
     width = fields * levels
     devices = sizes[0] * sizes[1]
-    line = jax.ShapeDtypeStruct((64, width), BF16)
+    line = jax.ShapeDtypeStruct((32, width), BF16)
     return pl.pallas_call(
         functools.partial(front_kernel, sizes, EYD * sizes[1]),
         out_shape=(
             jax.ShapeDtypeStruct((4 * elements, width), F32),
-            jax.ShapeDtypeStruct((devices, 8, 128), F32),
+            jax.ShapeDtypeStruct((devices, 8, 128), BF16),
             jax.ShapeDtypeStruct((1, 4 * elements), I32),
             line,
             line,
@@ -446,6 +454,7 @@
             pltpu.VMEM((2, 64, width), F32),
             pltpu.VMEM((2, 2, 64, width), F32),
             pltpu.VMEM((4 * elements, width), F32),
+            pltpu.VMEM((devices, 8, 128), F32),
             pltpu.SemaphoreType.DMA((2,)),
         ],
         compiler_params=params(FRONT_LIMIT),
@@ -460,11 +469,8 @@
     cell_ref,
     stiff_ref,
     state_ref,
-    hx_one,
-    hx_two,
-    hy_south,
-    hy_north,
     out_ref,
+    lines_ref,
     raw,
     sems,
     hi_ref,
@@ -473,11 +479,10 @@
     held,
     before,
     turned,
-    hx,
+    ends,
     rows_out,
     out_sems,
 ):
-    hx[0], hx[1] = from_neighbours("gx", hx_one[...].astype(F32), hx_two[...].astype(F32))
     fields, _, levels = turned.shape
     for chunk in range(CHUNKS):
         state_copy(state_ref, raw, sems, chunk).start()
@@ -488,18 +493,10 @@
 
     def emit(row, next_first):
         nodes = held_nodes(held, before, next_first)
-        for a in range(4):
-            at_row = pl.ds(16 * a + row, 1)
-            for b in range(4):
-                n = 4 * a + b
-                values = nodes[n]
-                if b == 0:
-                    values = values + jnp.where(iota(values.shape, 0) == 0, hy_south[at_row], 0.0)
-                if b == 3:
-                    values = values + jnp.where(iota(values.shape, 0) == 15, hy_north[at_row], 0.0)
-                values = values * float(ONE_D[a] * ONE_D[b])
-                for f in range(fields):
-                    turned[f, 16 * n : 16 * n + 16] = values[:, f * levels : (f + 1) * levels]
+        for n in range(NP):
+            values = nodes[n] * float(ONE_D[n // 4] * ONE_D[n % 4])
+            for f in range(fields):
+                turned[f, 16 * n : 16 * n + 16] = values[:, f * levels : (f + 1) * levels]
         slot = row & 1
         for y in range(EYD):
             for f in range(fields):
@@ -516,12 +513,11 @@
     def one_row(row, _):
         points = row_points(row, operators, hi_ref, lo_ref)
         nodes = [points[16 * n : 16 * n + 16] for n in range(NP)]
-        low = jnp.where(row == 0, 1.0, 0.0)
-        high = jnp.where(row == EXD - 1, 1.0, 0.0)
-        for b in range(4):
-            rows = slice(16 * b, 16 * b + 16)
-            nodes[b] = nodes[b] + hx[0, rows] * low
-            nodes[12 + b] = nodes[12 + b] + hx[1, rows] * high
+        ends[0, jnp.minimum(row, 1)] = points[0:64]
+        ends[1, jnp.maximum(row - EXD + 2, 0)] = points[192:256]
+        for a in range(4):
+            lines_ref[2, pl.ds(16 * a + row, 1)] = nodes[4 * a][0:1]
+            lines_ref[3, pl.ds(16 * a + row, 1)] = nodes[4 * a + 3][15:16]
         sum_along_y(nodes)
 
         @pl.when(row >= 3)
@@ -542,34 +538,41 @@
     copy_out(EXD - 3).wait()
     emit(EXD - 1, None)
     copy_out(EXD - 1).start()
+    lines_ref[0] = ends[0, 0]
+    lines_ref[1] = ends[1, 1]
+    lines_ref[2] = summed_line(lines_ref[2])
+    lines_ref[3] = summed_line(lines_ref[3])
     copy_out(EXD - 2).wait()
     copy_out(EXD - 1).wait()
 
 
-def dynamics_rows(cell, stiff, state, span_y, halos):
+def dynamics_rows(cell, stiff, state, span_y):
     fields, elements, _, levels = state.shape
     width = fields * levels
     return pl.pallas_call(
         functools.partial(dynamics_kernel, span_y),
-        out_shape=jax.ShapeDtypeStruct((elements, NP, width), F32),
-        in_specs=[SMEM, VMEM, VMEM, ANY] + [VMEM] * 4,
-        out_specs=ANY,
+        out_shape=(
+            jax.ShapeDtypeStruct((elements, NP, width), F32),
+            jax.ShapeDtypeStruct((4, 64, width), F32),
+        ),
+        in_specs=[SMEM, VMEM, VMEM, ANY],
+        out_specs=(ANY, VMEM),
         scratch_shapes=state_scratch(fields, elements, levels)
         + [
             pltpu.VMEM((fields, 256, levels), F32),
-            pltpu.VMEM((2, 64, width), F32),
+            pltpu.VMEM((2, 2, 64, width), F32),
             pltpu.VMEM((2, EYD, NP, width), F32),
             pltpu.SemaphoreType.DMA((2,)),
         ],
         compiler_params=params(DYN_LIMIT),
         cost_estimate=cost(4e9, 2e7),
         name="dynamics_rows",
-    )(cell, cell.reshape(1, elements), stiff, state, *halos)
-
-
-def message_kernel(x_one, x_two, south_ref, north_ref, table, y_one, y_two):
+    )(cell, cell.reshape(1, elements), stiff, state)
+
+
+def message_kernel(x_two, x_one, south_ref, north_ref, table, y_one, y_two):
     both = jnp.concatenate(from_neighbours("gx", x_one[...], x_two[...]), axis=0)
-    add = dot_twice(table[...], both)
+    add = dot(table[...], both)
     one, two = by_parity("gy", south_ref[...] + add[0:64], north_ref[...] + add[64:128])
     y_one[...] = one.astype(BF16)
     y_two[...] = two.astype(BF16)
@@ -585,7 +588,7 @@
         compiler_params=params(16),
         cost_estimate=cost(4e7, 6e5),
         name="line_messages",
-    )(one, two, south, north, table)
+    )(two, one, south, north, table)
 
 
 def pairs(axis, first):
@@ -595,10 +598,8 @@
 
 
 def exchange(axis, one, two):
-    return (
-        lax.ppermute(one, axis, pairs(axis, True)),
-        lax.ppermute(two, axis, pairs(axis, False)),
-    )
+    second = lax.ppermute(two, axis, pairs(axis, False))
+    return lax.ppermute(one, axis, pairs(axis, True)), second
 
 
 def by_parity(axis, to_low, to_high):
@@ -616,18 +617,18 @@
     span_y,
     columns_hbm,
     table_hbm,
-    x_one,
+    y_two,
     x_two,
     y_one,
-    y_two,
-    blocks_ref,
+    x_one,
+    blocks_in,
     cell_ref,
     out_ref,
     place_ref,
-    whole_south,
-    whole_north,
     columns_ref,
     table_ref,
+    lines_ref,
+    blocks_ref,
     rounded,
     pick,
     sems,
@@ -639,12 +640,12 @@
     table_copy.start()
     copy = pltpu.make_async_copy(columns_hbm, columns_ref, sems.at[1])
     copy.start()
-    requested = blocks_ref[:, 0, :].astype(I32)
+    blocks_ref[...] = blocks_in[...].astype(F32)
     spread_out = one_hot((iota((128, count), 1) & (per_peer - 1)) == iota((128, count), 0))
     shift = per_peer.bit_length() - 1
     own = (iota((devices, count), 1) >> shift) == iota((devices, count), 0)
-    wide = dot((requested >> 5).astype(F32).astype(BF16), spread_out) * 32.0 + dot(
-        (requested & 31).astype(F32).astype(BF16), spread_out
+    wide = dot(blocks_ref[:, 0, :].astype(BF16), spread_out) * 32.0 + dot(
+        blocks_ref[:, 1, :].astype(BF16), spread_out
     )
     requested = jnp.sum(jnp.where(own, wide, 0.0), axis=0, keepdims=True).astype(I32)
     elements = cell_ref.shape[1]
@@ -661,19 +662,26 @@
                 column == iota((128, 128), 1) + other
             )
 
-    south, north = from_neighbours("gy", y_one[...].astype(F32), y_two[...].astype(F32))
-    for ref, line, step_y in ((whole_south, south, -1), (whole_north, north, 1)):
-        ref[...] = line
-        for step_x, row in ((-1, 0), (1, 63)):
+    lines_ref[0], lines_ref[1] = from_neighbours(
+        "gy", y_one[...].astype(F32), y_two[...].astype(F32)
+    )
+    for side, step_y in enumerate((-1, 1)):
+        for step_x, a, x in ((-1, 0, 0), (1, 3, EXD - 1)):
             block = diagonal(sizes, step_x, step_y)
-            for f in range(width // 128):
-                ref[row : row + 1, f * 128 : (f + 1) * 128] += blocks_ref[block, 1 + f : 2 + f]
-    lines = jnp.concatenate([whole_south[...], whole_north[...]], axis=0).astype(BF16)
-    west, east = from_neighbours("gx", x_one[...], x_two[...])
+            for i in range(2):
+                weight = float(HALVES[i, a] * ONE_D[a])
+                for f in range(width // 128):
+                    lines_ref[side, 16 * i + x : 16 * i + x + 1, f * 128 : (f + 1) * 128] += (
+                        weight * blocks_ref[block, 2 + f : 3 + f]
+                    )
+    lines = jnp.concatenate([lines_ref[0], lines_ref[1]], axis=0).astype(BF16)
+    west, east = from_neighbours("gx", x_one[...].astype(F32), x_two[...].astype(F32))
+    west, east = (
+        jnp.concatenate([float(HALVES[i, a] * ONE_D[a]) * line for i in range(2)], axis=0)
+        for line, a in ((west, 0), (east, 3))
+    )
     table_copy.wait()
-    west = dot_twice(table_ref[count : count + 64, 0:128], west)
-    east = dot_twice(table_ref[count + 64 : count + 128, 0:128], east)
-    add = dot_twice(table_ref[0:count], lines)
+    add = dot_twice(table_ref[...], lines)
     copy.wait()
     rounded[...] = (columns_ref[...] + add).astype(BF16)
     rounded[0:64] = (columns_ref[0:64] + add[0:64] + west).astype(BF16)
@@ -685,22 +693,20 @@
 
 def send_columns(columns, halos, blocks, cell, sizes):
     count, width = columns.shape
-    extra = np.concatenate(hi_lo_arrays(TABLES["col_x"]), axis=1)
     table = np.concatenate(hi_lo_arrays(TABLES["col_y"]), axis=1)
-    table = np.concatenate([table, np.pad(extra, ((0, 0), (0, 128)))], axis=0)
     return pl.pallas_call(
         functools.partial(send_kernel, sizes, EYD * sizes[1]),
         out_shape=(
             jax.ShapeDtypeStruct((count, width), BF16),
             jax.ShapeDtypeStruct((1, count), I32),
-            jax.ShapeDtypeStruct((64, width), F32),
-            jax.ShapeDtypeStruct((64, width), F32),
         ),
         in_specs=[ANY, ANY] + [VMEM] * 6,
-        out_specs=(VMEM,) * 4,
+        out_specs=(VMEM,) * 2,
         scratch_shapes=[
             pltpu.VMEM((count, width), F32),
             pltpu.VMEM(table.shape, BF16),
+            pltpu.VMEM((2, 32, width), F32),
+            pltpu.VMEM(blocks.shape, F32),
             pltpu.VMEM((count, width), BF16),
             pltpu.VMEM((count, count), BF16),
             pltpu.SemaphoreType.DMA((2,)),
@@ -708,7 +714,7 @@
         compiler_params=params(SEND_LIMIT),
         cost_estimate=cost(2e9, 5e6),
         name="send_columns",
-    )(columns, jnp.asarray(table), *halos, blocks, cell)
+    )(columns, jnp.asarray(table), halos[3], halos[1], halos[2], halos[0], blocks, cell)
 
 
 SEND_LIMIT = 60
@@ -780,6 +786,7 @@
 def unpack_kernel(
     received_ref,
     place_ref,
+    own_lines,
     lines_table,
     back_ref,
     x_one,
@@ -793,13 +800,24 @@
     for start in range(0, count, 128):
         pick[start : start + 128] = one_hot(place == iota((128, count), 0) + start)
     back_ref[...] = dot(pick[...], received_ref[...]).astype(BF16)
-    x_one[...], x_two[...] = by_parity("gx", back_ref[0:64], back_ref[count - 64 : count])
+    ends = []
+    for kind, (first, a) in enumerate(((0, 0), (count - 64, 3))):
+        rows = back_ref[first : first + 64].astype(F32)
+        half = [
+            sum(float(SPREAD[a, i]) * rows[32 * i + 16 * j : 32 * i + 16 * j + 16] for i in range(2))
+            for j in range(2)
+        ]
+        nodes = [sum(float(SPREAD[b, j]) * half[j] for j in range(2)) for b in range(4)]
+        ends.append(own_lines[kind] + jnp.concatenate(nodes, axis=0))
+    one, two = by_parity("gx", *ends)
+    x_one[...] = one.astype(BF16)
+    x_two[...] = two.astype(BF16)
     lines = dot(lines_table[...], back_ref[...])
-    south_ref[...] = lines[0:64] + lines[128:192]
-    north_ref[...] = lines[64:128] + lines[192:256]
-
-
-def unpack(received, place):
+    south_ref[...] = own_lines[2] + lines[0:64] + lines[128:192]
+    north_ref[...] = own_lines[3] + lines[64:128] + lines[192:256]
+
+
+def unpack(received, place, own_lines):
     count, width = received.shape
     table = jnp.asarray(np.concatenate(hi_lo_arrays(TABLES["lines"]), axis=0))
     return pl.pallas_call(
@@ -811,13 +829,13 @@
             jax.ShapeDtypeStruct((64, width), F32),
             jax.ShapeDtypeStruct((64, width), F32),
         ),
-        in_specs=[VMEM] * 3,
+        in_specs=[VMEM] * 4,
         out_specs=(VMEM,) * 5,
         scratch_shapes=[pltpu.VMEM((count, count), BF16)],
         compiler_params=params(16),
         cost_estimate=cost(2e9, 4e6),
         name="unpack",
-    )(received, place, table)
+    )(received, place, own_lines, table)
 
 
 def inner_kernel(dynamics_ref, back_ref, table_ref, total):
@@ -908,7 +926,7 @@
 
 
 def border_kernel(
-    fields, slot_ref, x_one, x_two, y_one, y_two, total_ref, table_ref, _, out_ref, buffer, sem
+    fields, slot_ref, y_two, y_one, x_two, x_one, total_ref, table_ref, _, out_ref, buffer, sem
 ):
     width = x_one.shape[1]
     levels = width // fields
@@ -917,11 +935,7 @@
     adds = []
     for kind, halo in enumerate(halos):
         table = table_ref[kind * 256 : kind * 256 + 256]
-        if kind < 2:
-            add = dot_twice(table, halo)
-        else:
-            add = dot(table[:, 0:64], halo)
-        adds.append(add.reshape(16, NP, width))
+        adds.append(dot(table, halo).reshape(16, NP, width))
     for kind in range(4):
         for k in range(16):
             if kind >= 2 and k in (0, 15):
@@ -956,7 +970,7 @@
         compiler_params=params(16),
         cost_estimate=cost(2e8, 4e6),
         name="border_sum",
-    )(slot, *halos, total, table, out)
+    )(slot, *halos[::-1], total, table, out)
 
 
 def regroup(blocks):
@@ -973,21 +987,21 @@
     columns, blocks, q, x_one, x_two, y_one, y_two = front(
         elem_cell, group_column.reshape(1, columns_dev), stiff, state_in, sizes
     )
+    hy = exchange("gy", y_one, y_two)
     hx = exchange("gx", x_one, x_two)
-    hy = exchange("gy", y_one, y_two)
     blocks = regroup(blocks)
 
-    outgoing, place, south, north = send_columns(
+    outgoing, place = send_columns(
         columns, (*hx, *hy), blocks, elem_cell.reshape(1, elements), sizes
     )
     incoming = regroup(outgoing)
-    dynamics = dynamics_rows(elem_cell, stiff, state_in, span_y, (*hx, south, north))
-    incoming, dynamics = lax.optimization_barrier((incoming, dynamics))
+    dynamics, own_lines = dynamics_rows(elem_cell, stiff, state_in, span_y)
+    incoming, dynamics, own_lines = lax.optimization_barrier((incoming, dynamics, own_lines))
     received = regroup(physics_step(incoming, q, group_inverse, fields))
 
-    back, x_one, x_two, south, north = unpack(received, place)
+    back, x_one, x_two, south, north = unpack(received, place, own_lines)
     bx = exchange("gx", x_one, x_two)
-    by = exchange("gy", *messages(*bx, south, north, hi_lo(TABLES["corner_col"])))
+    by = exchange("gy", *messages(*bx, south, north, bf16_table("corner_pt")))
     total = inner_sum(dynamics, back)
     inner, slot = to_slots(elem_cell, total, fields, span_y)
     return border_sum(slot, (*bx, *by), total, inner)

time: 116 us -> 114 us (0.983)
  starting transfers between devices: 22.1 us -> 20.6 us
    ppermute x8, starting transfers between devices: 12 us -> 10.5 us  [the longest x4 10.4 us: exchange(): second = lax.ppermute(two, axis, pairs(axis, False))]
where the time goes in v3:
time: 114 us; the launch traced here: 113 us
  Pallas kernels  49.4 us (43%)
  blocking collectives  29.3 us (26%)
  starting transfers between devices  20.6 us (18%)
  waiting for transfers between devices  13.2 us (12%)
    all_to_all x1, blocking collectives, regroup(): lax.all_to_all(blocks, ('gx', 'gy'), split_axis=0, concat_axis=0, tiled=T...  29.3 us
    pallas_call x1, Pallas kernels, dynamics_rows(): pl.pallas_call(functools.partial(dynamics_kernel, span_y), out_shape=(jax...  16.5 us
    pallas_call x1, Pallas kernels, front(): pl.pallas_call(functools.partial(front_kernel, sizes, EYD * sizes[1]), ou...  12 us
    ppermute x4, starting transfers between devices, exchange(): second = lax.ppermute(two, axis, pairs(axis, False))  10.4 us
    all_to_all x2, starting transfers between devices, regroup(): lax.all_to_all(blocks, ('gx', 'gy'), split_axis=0, concat_axis=0, tiled=T...  10.1 us
    all_to_all x2, waiting for transfers between devices, regroup(): lax.all_to_all(blocks, ('gx', 'gy'), split_axis=0, concat_axis=0, tiled=T...  8.57 us
    pallas_call x1, Pallas kernels, send_columns(): pl.pallas_call(functools.partial(send_kernel, sizes, EYD * sizes[1]), out...  4.93 us
    pallas_call x1, Pallas kernels, to_slots(): pl.pallas_call(functools.partial(to_slots_kernel, span_y), out_shape=(jax...  4.65 us
  transfers between devices with their start and end apart: 10, of which 5 were waited for; matrix products, arithmetic and copies ran while one was open for 0% of the time, Pallas kernels for 21%

profile of v3, /device:TPU:0, one launch (start us, length us, event | category | flops | bytes accessed | tf_op | source)
XLA Modules:
  0.0 113.4 jit_solution(5920877336976174204)
XLA Ops:
  0.0 12.0 %front.1 = (f32[1024,512]{1,0:T(8,128)}, bf16[32,8,128]{2,1,0:T(8,128)(2,1)}, s32[1,1024]{1,0:T(1,128)}, bf16[32,512]{1,0:T(8,128)(2,1)}, bf16[32,512]{1,0:T(8,1...) custom-call(s32[256]{0:T(256)} %cell_smem.5, s32[1,256]{1,0:T(1,128)} %bitcast.12, s32[1,1024]{1,0:T(1,128)} %bitcast.18, ...), custom_call_target="tpu_custom_call" | custom-call | flops 4000000000 | bytes 20000000 | tf_op jit(solution)/shard_map/front/pallas_call | solution.py:439
  12.0 7.3 %all-to-all-start = ((bf16[32,8,128]{2,1,0:T(8,128)(2,1)}), bf16[32,8,128]{2,1,0:T(8,128)(2,1)S(1)}, u32[]{:S(2)}, u32[]{:S(2)}) async-start(bf16[32,8,128]{2,1,0:T(8,128)(2,1)} %get-tuple-element.33), calls=%async_computation | async-start | bytes 131072 | tf_op jit(solution)/shard_map/all_to_all | solution.py:977
  19.3 3.7 %collective-permute-start = (bf16[32,512]{1,0:T(8,128)(2,1)}, bf16[32,512]{1,0:T(8,128)(2,1)S(1)}, u32[]{:S(2)}, u32[]{:S(2)}) collective-permute-start(bf16[32,512]{1,0:T(8,128)(2,1)} %get-tuple-element.29), channel_id=1, source_target_pairs={{1,2},{3,0},{2,1},{0,3},{5,6},{7,4},{6,5},{4,7},{9,10},{11,8},{10,... | collective-permute-start | bytes 98312 | tf_op jit(solution)/shard_map/ppermute | solution.py:601
  23.0 1.9 %collective-permute-start.1 = (bf16[32,512]{1,0:T(8,128)(2,1)}, bf16[32,512]{1,0:T(8,128)(2,1)S(1)}, u32[]{:S(2)}, u32[]{:S(2)}) collective-permute-start(bf16[32,512]{1,0:T(8,128)(2,1)} %get-tuple-element.30), channel_id=1, source_target_pairs={{4,8},{12,16},{20,24},{28,0},{8,4},{16,12},{24,20},{0,28},{5,9},{1... | collective-permute-start | bytes 98312 | tf_op jit(solution)/shard_map/ppermute | solution.py:601
  24.9 0.9 collective-permute-done.y_two
  25.8 2.0 %collective-permute-done.1.x_two = bf16[32,512]{1,0:T(8,128)(2,1)S(1)} collective-permute-done((bf16[32,512]{1,0:T(8,128)(2,1)}, bf16[32,512]{1,0:T(8,128)(2,1)S(1)}, u32[]{:S(2)}, u32[]{:S(2)}) %collective-permute-start.1) | collective-permute-done | bytes 32800 | tf_op jit(solution)/shard_map/ppermute | solution.py:601
  27.8 1.2 %collective-permute-done.2.y_one = bf16[32,512]{1,0:T(8,128)(2,1)S(1)} collective-permute-done((bf16[32,512]{1,0:T(8,128)(2,1)}, bf16[32,512]{1,0:T(8,128)(2,1)S(1)}, u32[]{:S(2)}, u32[]{:S(2)}) %collective-permute-start.2) | collective-permute-done | bytes 32800 | tf_op jit(solution)/shard_map/ppermute | solution.py:602
  29.1 0.6 copy-done.12
  29.6 0.0 copy-done.13
  29.6 0.0 copy-done.9
  29.7 4.9 %send_columns.1 = (bf16[1024,512]{1,0:T(8,128)(2,1)}, s32[1,1024]{1,0:T(1,128)}) custom-call(f32[1024,512]{1,0:T(8,128)} %get-tuple-element.28.columns_hbm, bf16[1024,128]{1,0:T(8,128)(2,1)} %constant.10.clone.table_hbm, bf16[32,512]{1,0:T(8,128)(2,1)} %copy-done.10, bf16[32,512]{1,0:T(8,128)(2,1)} %copy-done.11, bf16[32,512]{1,0:T(8,128)(2,1)} %copy-done.12, ...), custom_call_target="tpu_custom_call" | custom-call | flops 2000000000 | bytes 5000000 | tf_op jit(solution)/shard_map/send_columns/pallas_call | solution.py:697
  34.6 2.8 %all-to-all-start.1 = ((bf16[32,32,512]{2,1,0:T(8,128)(2,1)}), bf16[32,32,512]{2,1,0:T(8,128)(2,1)S(1)}, u32[]{:S(2)}, u32[]{:S(2)}) async-start(bf16[32,32,512]{2,1,0:T(8,128)(2,1)} %bitcast.15), calls=%async_computation.1 | async-start | bytes 2097152 | tf_op jit(solution)/shard_map/all_to_all | solution.py:977
  37.4 16.5 %dynamics_rows.1 = (f32[256,16,512]{2,1,0:T(8,128)}, f32[4,64,512]{2,1,0:T(8,128)}) custom-call(s32[256]{0:T(256)} %cell_smem.5, s32[1,256]{1,0:T(1,128)} %bitcast.14, f32[256,256]{1,0:T(8,128)} %bitcast.17, f32[4,256,16,128]{3,2,1,0:T(8,128)} %state_ref.3), custom_call_target="tpu_custom_call" | custom-call | flops 4000000000 | bytes 20000000 | tf_op jit(solution)/shard_map/dynamics_rows/pallas_call | solution.py:552
  53.9 8.6 %all-to-all-done.1 = bf16[32,32,512]{2,1,0:T(8,128)(2,1)S(1)} async-done(((bf16[32,32,512]{2,1,0:T(8,128)(2,1)}), bf16[32,32,512]{2,1,0:T(8,128)(2,1)S(1)}, u32[]{:S(2)}, u32[]{:S(2)}) %all-to-all-start.1) | async-done | bytes 1048608 | tf_op jit(solution)/shard_map/all_to_all | solution.py:977
  62.5 4.3 %physics.1 = bf16[1024,512]{1,0:T(8,128)(2,1)S(1)} custom-call(bf16[1024,512]{1,0:T(8,128)(2,1)S(1)} %bitcast.9, s32[1,1024]{1,0:T(1,128)S(1)} %copy-done.8, bf16[64,128,128]{2,1,0:T(8,128)(2,1)S(1)} %copy-done.3), custom_call_target="tpu_custom_call" | custom-call | flops 3000000000 | bytes 5000000 | tf_op jit(solution)/shard_map/physics/pallas_call | solution.py:766
  66.8 29.3 %all_to_all.28 = bf16[32,32,512]{2,1,0:T(8,128)(2,1)S(1)} all-to-all(bf16[32,32,512]{2,1,0:T(8,128)(2,1)S(1)} %bitcast.11), channel_id=1, replica_groups=mesh['gx'=8,'gy'=4] {'gx','gy'}, dimensions={0} | all-to-all | bytes 2097152 | tf_op jit(solution)/shard_map/all_to_all | solution.py:977
  96.1 1.5 %unpack.1 = (bf16[1024,512]{1,0:T(8,128)(2,1)S(1)}, bf16[64,512]{1,0:T(8,128)(2,1)S(1)}, bf16[64,512]{1,0:T(8,128)(2,1)S(1)}, f32[64,512]{1,0:T(8,128)S(1)}, f32[64,512]{1,0:T(8,128)S(1)}) custom-call(bf16[1024,512]{1,0:T(8,128)(2,1)S(1)} %bitcast.10, s32[1,1024]{1,0:T(1,128)S(1)} %copy-done.7, f32[4,64,512]{2,1,0:T(8,128)S(1)} %copy-done.6, ...), custom_call_target="tpu_custom_call" | custom-call | flops 2000000000 | bytes 4000000 | tf_op jit(solution)/shard_map/unpack/pallas_call | solution.py:823
  97.6 2.7 %collective-permute-start.4 = (bf16[64,512]{1,0:T(8,128)(2,1)S(1)}, bf16[64,512]{1,0:T(8,128)(2,1)S(1)}, u32[]{:S(2)}, u32[]{:S(2)}) collective-permute-start(bf16[64,512]{1,0:T(8,128)(2,1)S(1)} %get-tuple-element.44), channel_id=1, source_target_pairs={{4,8},{12,16},{20,24},{28,0},{8,4},{16,12},{24,20},{0,28},{5,9},{1... | collective-permute-start | bytes 196616 | tf_op jit(solution)/shard_map/ppermute | solution.py:601
  100.4 3.2 %inner_sum.1.total.total_ref = f32[256,16,512]{2,1,0:T(8,128)S(1)} custom-call(f32[256,16,512]{2,1,0:T(8,128)S(1)} %bitcast.8, bf16[1024,512]{1,0:T(8,128)(2,1)S(1)} %get-tuple-element.42.back_ref, bf16[1024,256]{1,0:T(8,128)(2,1)S(1)} %copy-done), custom_call_target="tpu_custom_call", output_to_operand_aliasing={{}: (0, {})} | custom-call | flops 4000000000 | bytes 20000000 | tf_op jit(solution)/shard_map/inner_sum/pallas_call | solution.py:868
  103.6 0.2 line_messages.1
  103.8 2.2 %collective-permute-start.6 = (bf16[64,512]{1,0:T(8,128)(2,1)S(1)}, bf16[64,512]{1,0:T(8,128)(2,1)S(1)}, u32[]{:S(2)}, u32[]{:S(2)}) collective-permute-start(bf16[64,512]{1,0:T(8,128)(2,1)S(1)} %get-tuple-element.48), channel_id=1, source_target_pairs={{1,2},{3,0},{2,1},{0,3},{5,6},{7,4},{6,5},{4,7},{9,10},{11,8},{10,... | collective-permute-start | bytes 196616 | tf_op jit(solution)/shard_map/ppermute | solution.py:601
  106.0 4.7 %to_slots.1 = (f32[4,256,16,128]{3,2,1,0:T(8,128)}, s32[1,256]{1,0:T(1,128)S(1)}) custom-call(s32[256]{0:T(256)S(1)} %copy-done.4, f32[256,16,512]{2,1,0:T(8,128)S(1)} %inner_sum.1.total.total_ref), custom_call_target="tpu_custom_call" | custom-call | flops 4000000000 | bytes 20000000 | tf_op jit(solution)/shard_map/to_slots/pallas_call | solution.py:910
  110.7 0.5 collective-permute-done.7.y_one
  111.2 2.1 %border_sum.1 = f32[4,256,16,128]{3,2,1,0:T(8,128)} custom-call(s32[1,256]{1,0:T(1,128)S(1)} %get-tuple-element.43.slot_ref, bf16[64,512]{1,0:T(8,128)(2,1)S(1)} %collective-permute-done.6.y_two, bf16[64,512]{1,0:T(8,128)(2,1)S(1)} %collective-permute-done.7.y_one, bf16[64,512]{1,0:T(8,128)(2,1)S(1)} %collective-permute-done.4.x_two, ...), custom_call_target="tpu_custom_call", output_to_operand_aliasing={{}: (7, {})} | custom-call | flops 200000000 | bytes 4000000 | tf_op jit(solution)/shard_map/border_sum/pallas_call | solution.py:960
  (39 shorter events, 0.1 us)
Async XLA Ops:
  12.0 17.0 %all-to-all-start = ((bf16[32,8,128]{2,1,0:T(8,128)(2,1)}), bf16[32,8,128]{2,1,0:T(8,128)(2,1)S(1)}, u32[]{:S(2)}, u32[]{:S(2)}) async-start(bf16[32,8,128]{2,1,0:T(8,128)(2,1)} %get-tuple-element.33), calls=%async_computation | async-start | bytes 131072 | tf_op jit(solution)/shard_map/all_to_all | solution.py:977
  19.3 6.5 %collective-permute-start = (bf16[32,512]{1,0:T(8,128)(2,1)}, bf16[32,512]{1,0:T(8,128)(2,1)S(1)}, u32[]{:S(2)}, u32[]{:S(2)}) collective-permute-start(bf16[32,512]{1,0:T(8,128)(2,1)} %get-tuple-element.29), channel_id=1, source_target_pairs={{1,2},{3,0},{2,1},{0,3},{5,6},{7,4},{6,5},{4,7},{9,10},{11,8},{10,... | collective-permute-start | bytes 98312 | tf_op jit(solution)/shard_map/ppermute | solution.py:601
  23.0 4.8 %collective-permute-start.1 = (bf16[32,512]{1,0:T(8,128)(2,1)}, bf16[32,512]{1,0:T(8,128)(2,1)S(1)}, u32[]{:S(2)}, u32[]{:S(2)}) collective-permute-start(bf16[32,512]{1,0:T(8,128)(2,1)} %get-tuple-element.30), channel_id=1, source_target_pairs={{4,8},{12,16},{20,24},{28,0},{8,4},{16,12},{24,20},{0,28},{5,9},{1... | collective-permute-start | bytes 98312 | tf_op jit(solution)/shard_map/ppermute | solution.py:601
  24.9 4.1 %collective-permute-start.2 = (bf16[32,512]{1,0:T(8,128)(2,1)}, bf16[32,512]{1,0:T(8,128)(2,1)S(1)}, u32[]{:S(2)}, u32[]{:S(2)}) collective-permute-start(bf16[32,512]{1,0:T(8,128)(2,1)} %get-tuple-element.31), channel_id=1, source_target_pairs={{0,1},{2,3},{1,0},{3,2},{4,5},{6,7},{5,4},{7,6},{8,9},{10,11},{9,8... | collective-permute-start | bytes 98312 | tf_op jit(solution)/shard_map/ppermute | solution.py:602
  24.9 4.1 %collective-permute-start.3 = (bf16[32,512]{1,0:T(8,128)(2,1)}, bf16[32,512]{1,0:T(8,128)(2,1)S(1)}, u32[]{:S(2)}, u32[]{:S(2)}) collective-permute-start(bf16[32,512]{1,0:T(8,128)(2,1)} %get-tuple-element.32), channel_id=1, source_target_pairs={{0,4},{8,12},{16,20},{24,28},{4,0},{12,8},{20,16},{28,24},{1,5},{9... | collective-permute-start | bytes 98312 | tf_op jit(solution)/shard_map/ppermute | solution.py:602
  25.8 3.2 %copy-start.10 = (bf16[32,512]{1,0:T(8,128)(2,1)}, bf16[32,512]{1,0:T(8,128)(2,1)S(1)}, u32[]{:S(2)}) copy-start(bf16[32,512]{1,0:T(8,128)(2,1)S(1)} %collective-permute-done.y_two) | copy-start | bytes 98308
  27.8 1.3 %copy-start.11 = (bf16[32,512]{1,0:T(8,128)(2,1)}, bf16[32,512]{1,0:T(8,128)(2,1)S(1)}, u32[]{:S(2)}) copy-start(bf16[32,512]{1,0:T(8,128)(2,1)S(1)} %collective-permute-done.1.x_two) | copy-start | bytes 98308
  29.0 0.6 copy-start.9
  34.6 27.9 %copy-start.3 = (bf16[64,128,128]{2,1,0:T(8,128)(2,1)S(1)}, bf16[64,128,128]{2,1,0:T(8,128)(2,1)}, u32[]{:S(2)}) copy-start(bf16[64,128,128]{2,1,0:T(8,128)(2,1)} %inverse_hbm.1) | copy-start | bytes 6291460
  34.6 27.9 %copy-start.8 = (s32[1,1024]{1,0:T(1,128)S(1)}, s32[1,1024]{1,0:T(1,128)}, u32[]{:S(2)}) copy-start(s32[1,1024]{1,0:T(1,128)} %get-tuple-element.39.q_ref) | copy-start | bytes 12292
  34.6 27.8 %all-to-all-start.1 = ((bf16[32,32,512]{2,1,0:T(8,128)(2,1)}), bf16[32,32,512]{2,1,0:T(8,128)(2,1)S(1)}, u32[]{:S(2)}, u32[]{:S(2)}) async-start(bf16[32,32,512]{2,1,0:T(8,128)(2,1)} %bitcast.15), calls=%async_computation.1 | async-start | bytes 2097152 | tf_op jit(solution)/shard_map/all_to_all | solution.py:977
  53.9 42.2 %copy-start.7 = (s32[1,1024]{1,0:T(1,128)S(1)}, s32[1,1024]{1,0:T(1,128)}, u32[]{:S(2)}) copy-start(s32[1,1024]{1,0:T(1,128)} %get-tuple-element.40.place_ref) | copy-start | bytes 12292
  62.5 33.6 %copy-start.5 = (bf16[256,1024]{1,0:T(8,128)(2,1)S(1)}, bf16[256,1024]{1,0:T(8,128)(2,1)}, u32[]{:S(2)}) copy-start(bf16[256,1024]{1,0:T(8,128)(2,1)} %constant.11.clone.lines_table) | copy-start | bytes 1572868
  62.5 33.6 %copy-start.6 = (f32[4,64,512]{2,1,0:T(8,128)S(1)}, f32[4,64,512]{2,1,0:T(8,128)}, u32[]{:S(2)}) copy-start(f32[4,64,512]{2,1,0:T(8,128)} %get-tuple-element.41.own_lines) | copy-start | bytes 1572868
  62.5 37.8 %slice-start = ((s8[8388608]{0:T(1024)(128)(4,1)}), s8[4194304]{0:T(1024)(128)(4,1)S(1)}, s32[]{:S(2)}) async-start(s8[8388608]{0:T(1024)(128)(4,1)} %bitcast.7), calls=%async_computation.3 | async-start | bytes 8388608
  62.5 37.8 %slice-start.1 = ((s8[8388608]{0:T(1024)(128)(4,1)}), s8[4194304]{0:T(1024)(128)(4,1)S(1)}, s32[]{:S(2)}) async-start(s8[8388608]{0:T(1024)(128)(4,1)} %bitcast.7), calls=%async_computation.4 | async-start | bytes 8388608
  62.5 37.8 %copy-start = (bf16[1024,256]{1,0:T(8,128)(2,1)S(1)}, bf16[1024,256]{1,0:T(8,128)(2,1)}, u32[]{:S(2)}) copy-start(bf16[1024,256]{1,0:T(8,128)(2,1)} %constant.13.clone.table_ref) | copy-start | bytes 1572868
  97.6 6.0 %collective-permute-start.4 = (bf16[64,512]{1,0:T(8,128)(2,1)S(1)}, bf16[64,512]{1,0:T(8,128)(2,1)S(1)}, u32[]{:S(2)}, u32[]{:S(2)}) collective-permute-start(bf16[64,512]{1,0:T(8,128)(2,1)S(1)} %get-tuple-element.44), channel_id=1, source_target_pairs={{4,8},{12,16},{20,24},{28,0},{8,4},{16,12},{24,20},{0,28},{5,9},{1... | collective-permute-start | bytes 196616 | tf_op jit(solution)/shard_map/ppermute | solution.py:601
  100.3 3.3 %collective-permute-start.5 = (bf16[64,512]{1,0:T(8,128)(2,1)S(1)}, bf16[64,512]{1,0:T(8,128)(2,1)S(1)}, u32[]{:S(2)}, u32[]{:S(2)}) collective-permute-start(bf16[64,512]{1,0:T(8,128)(2,1)S(1)} %get-tuple-element.45), channel_id=1, source_target_pairs={{0,4},{8,12},{16,20},{24,28},{4,0},{12,8},{20,16},{28,24},{1,5},{9... | collective-permute-start | bytes 196616 | tf_op jit(solution)/shard_map/ppermute | solution.py:602
  100.3 3.3 %copy-start.2 = (bf16[128,128]{1,0:T(8,128)(2,1)S(1)}, bf16[128,128]{1,0:T(8,128)(2,1)}, u32[]{:S(2)}) copy-start(bf16[128,128]{1,0:T(8,128)(2,1)} %constant.12.clone.table) | copy-start | bytes 98308
  100.3 5.7 %copy-start.4 = (s32[256]{0:T(256)S(1)}, s32[256]{0:T(256)}, u32[]{:S(2)}) copy-start(s32[256]{0:T(256)} %cell_smem.5) | copy-start | bytes 3076
  103.6 7.6 %copy-start.1 = (bf16[1024,64]{1,0:T(8,128)(2,1)S(1)}, bf16[1024,64]{1,0:T(8,128)(2,1)}, u32[]{:S(2)}) copy-start(bf16[1024,64]{1,0:T(8,128)(2,1)} %constant.14.clone.table_ref) | copy-start | bytes 393220
  103.8 6.9 %collective-permute-start.6 = (bf16[64,512]{1,0:T(8,128)(2,1)S(1)}, bf16[64,512]{1,0:T(8,128)(2,1)S(1)}, u32[]{:S(2)}, u32[]{:S(2)}) collective-permute-start(bf16[64,512]{1,0:T(8,128)(2,1)S(1)} %get-tuple-element.48), channel_id=1, source_target_pairs={{1,2},{3,0},{2,1},{0,3},{5,6},{7,4},{6,5},{4,7},{9,10},{11,8},{10,... | collective-permute-start | bytes 196616 | tf_op jit(solution)/shard_map/ppermute | solution.py:601
  106.0 5.1 %collective-permute-start.7 = (bf16[64,512]{1,0:T(8,128)(2,1)S(1)}, bf16[64,512]{1,0:T(8,128)(2,1)S(1)}, u32[]{:S(2)}, u32[]{:S(2)}) collective-permute-start(bf16[64,512]{1,0:T(8,128)(2,1)S(1)} %get-tuple-element.49), channel_id=1, source_target_pairs={{0,1},{2,3},{1,0},{3,2},{4,5},{6,7},{5,4},{7,6},{8,9},{10,11},{9,8... | collective-permute-start | bytes 196616 | tf_op jit(solution)/shard_map/ppermute | solution.py:602
  (2 other events, 1.2 us)

commit v4 on v3

--- a/solution.py
+++ b/solution.py
@@ -260,7 +260,7 @@
                     lo_ref[where, :, f * levels : (f + 1) * levels] = lo
             return 0
 
-        lax.fori_loop(0, per // 4, place_slots, 0)
+        lax.fori_loop(0, per // 4, place_slots, 0, unroll=2)
 
 
 def row_points(row, operators, hi_ref, lo_ref):
@@ -389,14 +389,16 @@
         return 0
 
     def send(part):
-        rows = pl.ds(part * (columns.shape[0] // 2), columns.shape[0] // 2)
+        rows = (pl.ds(0, 576), pl.ds(576, 256), pl.ds(832, 192))[part]
         return pltpu.make_async_copy(columns.at[rows], columns_out.at[rows], out_sem.at[part])
 
-    lax.fori_loop(0, EXD // 2 + 2, one_row, 0, unroll=2)
+    lax.fori_loop(0, 10, one_row, 0, unroll=5)
     send(0).start()
-    lax.fori_loop(EXD // 2 + 2, EXD, one_row, 0, unroll=2)
+    lax.fori_loop(10, 14, one_row, 0, unroll=4)
+    send(1).start()
+    lax.fori_loop(14, EXD, one_row, 0, unroll=2)
     emit(EXD - 1, None)
-    send(1).start()
+    send(2).start()
     for axis, low, high, one, two in (
         ("gx", ends[0, 0], ends[1, 1], x_one, x_two),
         ("gy", lines[0], lines[1], y_one, y_two),
@@ -413,6 +415,7 @@
     blocks_out[...] = blocks_ref[...].astype(BF16)
     send(0).wait()
     send(1).wait()
+    send(2).wait()
 
 
 def state_scratch(fields, elements, levels):
@@ -455,7 +458,7 @@
             pltpu.VMEM((2, 2, 64, width), F32),
             pltpu.VMEM((4 * elements, width), F32),
             pltpu.VMEM((devices, 8, 128), F32),
-            pltpu.SemaphoreType.DMA((2,)),
+            pltpu.SemaphoreType.DMA((3,)),
         ],
         compiler_params=params(FRONT_LIMIT),
         cost_estimate=cost(4e9, 2e7),
@@ -615,8 +618,8 @@
 def send_kernel(
     sizes,
     span_y,
-    columns_hbm,
-    table_hbm,
+    columns_ref,
+    table_ref,
     y_two,
     x_two,
     y_one,
@@ -625,21 +628,14 @@
     cell_ref,
     out_ref,
     place_ref,
-    columns_ref,
-    table_ref,
     lines_ref,
     blocks_ref,
     rounded,
     pick,
-    sems,
 ):
     count, width = columns_ref.shape
     devices = sizes[0] * sizes[1]
     per_peer = count // devices
-    table_copy = pltpu.make_async_copy(table_hbm, table_ref, sems.at[0])
-    table_copy.start()
-    copy = pltpu.make_async_copy(columns_hbm, columns_ref, sems.at[1])
-    copy.start()
     blocks_ref[...] = blocks_in[...].astype(F32)
     spread_out = one_hot((iota((128, count), 1) & (per_peer - 1)) == iota((128, count), 0))
     shift = per_peer.bit_length() - 1
@@ -680,9 +676,7 @@
         jnp.concatenate([float(HALVES[i, a] * ONE_D[a]) * line for i in range(2)], axis=0)
         for line, a in ((west, 0), (east, 3))
     )
-    table_copy.wait()
     add = dot_twice(table_ref[...], lines)
-    copy.wait()
     rounded[...] = (columns_ref[...] + add).astype(BF16)
     rounded[0:64] = (columns_ref[0:64] + add[0:64] + west).astype(BF16)
     rounded[count - 64 : count] = (
@@ -700,16 +694,13 @@
             jax.ShapeDtypeStruct((count, width), BF16),
             jax.ShapeDtypeStruct((1, count), I32),
         ),
-        in_specs=[ANY, ANY] + [VMEM] * 6,
+        in_specs=[VMEM] * 8,
         out_specs=(VMEM,) * 2,
         scratch_shapes=[
-            pltpu.VMEM((count, width), F32),
-            pltpu.VMEM(table.shape, BF16),
             pltpu.VMEM((2, 32, width), F32),
             pltpu.VMEM(blocks.shape, F32),
             pltpu.VMEM((count, width), BF16),
             pltpu.VMEM((count, count), BF16),
-            pltpu.SemaphoreType.DMA((2,)),
         ],
         compiler_params=params(SEND_LIMIT),
         cost_estimate=cost(2e9, 5e6),
@@ -717,7 +708,7 @@
     )(columns, jnp.asarray(table), halos[3], halos[1], halos[2], halos[0], blocks, cell)
 
 
-SEND_LIMIT = 60
+SEND_LIMIT = 16
 DYN_LIMIT = 56
 
 
@@ -856,7 +847,7 @@
         near_sum(pair * 2, pl.multiple_of(pair * 128 - 64, 64), 256, 0)
         return 0
 
-    lax.fori_loop(1, EXD // 2 - 1, middle, 0, unroll=2)
+    lax.fori_loop(1, EXD // 2 - 1, middle, 0, unroll=6)
 
 
 def inner_sum(dynamics, back):

time: 114 us -> 111 us (0.974)
  Pallas kernels: 49.4 us -> 45.7 us
    pallas_call x1, Pallas kernels: 4.93 us -> 3.09 us  [send_columns(): pl.pallas_call(functools.partial(send_kernel, sizes, EYD * sizes[1]), out...]
  transfers between devices with their start and end apart: 10 -> 10, of which waited for: 5 -> 4; matrix products, arithmetic and copies ran while one was open for 0% -> 0% of each run, Pallas kernels for 21% -> 21%
where the time goes in v4:
time: 111 us
  Pallas kernels  45.7 us (41%)
  blocking collectives  29.3 us (26%)
  starting transfers between devices  21.3 us (19%)
  waiting for transfers between devices  12.5 us (11%)
  local copies, waits for them, and re-layouts  1.65 us (1%)
    all_to_all x1, blocking collectives, regroup(): lax.all_to_all(blocks, ('gx', 'gy'), split_axis=0, concat_axis=0, tiled=T...  29.3 us
    pallas_call x1, Pallas kernels, dynamics_rows(): pl.pallas_call(functools.partial(dynamics_kernel, span_y), out_shape=(jax...  16.5 us
    pallas_call x1, Pallas kernels, front(): pl.pallas_call(functools.partial(front_kernel, sizes, EYD * sizes[1]), ou...  10.9 us
    ppermute x4, starting transfers between devices, exchange(): second = lax.ppermute(two, axis, pairs(axis, False))  10.9 us
    all_to_all x2, starting transfers between devices, regroup(): lax.all_to_all(blocks, ('gx', 'gy'), split_axis=0, concat_axis=0, tiled=T...  10.3 us
    all_to_all x2, waiting for transfers between devices, regroup(): lax.all_to_all(blocks, ('gx', 'gy'), split_axis=0, concat_axis=0, tiled=T...  8.38 us
    pallas_call x1, Pallas kernels, to_slots(): pl.pallas_call(functools.partial(to_slots_kernel, span_y), out_shape=(jax...  4.65 us
    pallas_call x1, Pallas kernels, physics_step(): pl.pallas_call(functools.partial(physics_kernel, fields), out_shape=jax.S...  4.27 us
  transfers between devices with their start and end apart: 10, of which 4 were waited for; matrix products, arithmetic and copies ran while one was open for 0% of the time, Pallas kernels for 21%

profile of v4, /device:TPU:0, one launch (start us, length us, event | category | flops | bytes accessed | tf_op | source)
XLA Modules:
  0.0 110.8 jit_solution(10837615850175960843)
XLA Ops:
  0.0 10.9 %front.1 = (f32[1024,512]{1,0:T(8,128)}, bf16[32,8,128]{2,1,0:T(8,128)(2,1)}, s32[1,1024]{1,0:T(1,128)}, bf16[32,512]{1,0:T(8,128)(2,1)}, bf16[32,512]{1,0:T(8,1...) custom-call(s32[256]{0:T(256)} %cell_smem.5, s32[1,256]{1,0:T(1,128)} %bitcast.12, s32[1,1024]{1,0:T(1,128)} %bitcast.17, ...), custom_call_target="tpu_custom_call" | custom-call | flops 4000000000 | bytes 20000000 | tf_op jit(solution)/shard_map/front/pallas_call | solution.py:442
  10.9 7.3 %all-to-all-start = ((bf16[32,8,128]{2,1,0:T(8,128)(2,1)}), bf16[32,8,128]{2,1,0:T(8,128)(2,1)S(1)}, u32[]{:S(2)}, u32[]{:S(2)}) async-start(bf16[32,8,128]{2,1,0:T(8,128)(2,1)} %get-tuple-element.33), calls=%async_computation | async-start | bytes 131072 | tf_op jit(solution)/shard_map/all_to_all | solution.py:968
  18.3 3.7 %collective-permute-start = (bf16[32,512]{1,0:T(8,128)(2,1)}, bf16[32,512]{1,0:T(8,128)(2,1)S(1)}, u32[]{:S(2)}, u32[]{:S(2)}) collective-permute-start(bf16[32,512]{1,0:T(8,128)(2,1)} %get-tuple-element.29), channel_id=1, source_target_pairs={{1,2},{3,0},{2,1},{0,3},{5,6},{7,4},{6,5},{4,7},{9,10},{11,8},{10,... | collective-permute-start | bytes 98312 | tf_op jit(solution)/shard_map/ppermute | solution.py:604
  21.9 1.9 %collective-permute-start.1 = (bf16[32,512]{1,0:T(8,128)(2,1)}, bf16[32,512]{1,0:T(8,128)(2,1)S(1)}, u32[]{:S(2)}, u32[]{:S(2)}) collective-permute-start(bf16[32,512]{1,0:T(8,128)(2,1)} %get-tuple-element.30), channel_id=1, source_target_pairs={{4,8},{12,16},{20,24},{28,0},{8,4},{16,12},{24,20},{0,28},{5,9},{1... | collective-permute-start | bytes 98312 | tf_op jit(solution)/shard_map/ppermute | solution.py:604
  23.8 0.9 collective-permute-done.y_two
  24.8 2.0 %collective-permute-done.1.x_two = bf16[32,512]{1,0:T(8,128)(2,1)S(1)} collective-permute-done((bf16[32,512]{1,0:T(8,128)(2,1)}, bf16[32,512]{1,0:T(8,128)(2,1)S(1)}, u32[]{:S(2)}, u32[]{:S(2)}) %collective-permute-start.1) | collective-permute-done | bytes 32800 | tf_op jit(solution)/shard_map/ppermute | solution.py:604
  26.7 1.2 %collective-permute-done.2.y_one = bf16[32,512]{1,0:T(8,128)(2,1)S(1)} collective-permute-done((bf16[32,512]{1,0:T(8,128)(2,1)}, bf16[32,512]{1,0:T(8,128)(2,1)S(1)}, u32[]{:S(2)}, u32[]{:S(2)}) %collective-permute-start.2) | collective-permute-done | bytes 32800 | tf_op jit(solution)/shard_map/ppermute | solution.py:605
  28.0 1.6 %copy-done.8 = f32[1024,512]{1,0:T(8,128)S(1)} copy-done((f32[1024,512]{1,0:T(8,128)S(1)}, f32[1024,512]{1,0:T(8,128)}, u32[]{:S(2)}) %copy-start.8) | copy-done | bytes 2097176
  29.6 3.1 %send_columns.1 = (bf16[1024,512]{1,0:T(8,128)(2,1)}, s32[1,1024]{1,0:T(1,128)S(1)}) custom-call(f32[1024,512]{1,0:T(8,128)S(1)} %copy-done.8, bf16[1024,128]{1,0:T(8,128)(2,1)S(1)} %copy-done.7, bf16[32,512]{1,0:T(8,128)(2,1)S(1)} %collective-permute-done.y_two, bf16[32,512]{1,0:T(8,128)(2,1)S(1)} %collective-permute-done.1.x_two, ...), custom_call_target="tpu_custom_call" | custom-call | flops 2000000000 | bytes 5000000 | tf_op jit(solution)/shard_map/send_columns/pallas_call | solution.py:691
  32.7 3.0 %all-to-all-start.1 = ((bf16[32,32,512]{2,1,0:T(8,128)(2,1)}), bf16[32,32,512]{2,1,0:T(8,128)(2,1)S(1)}, u32[]{:S(2)}, u32[]{:S(2)}) async-start(bf16[32,32,512]{2,1,0:T(8,128)(2,1)} %bitcast.3), calls=%async_computation.1 | async-start | bytes 2097152 | tf_op jit(solution)/shard_map/all_to_all | solution.py:968
  35.6 16.5 %dynamics_rows.1 = (f32[256,16,512]{2,1,0:T(8,128)}, f32[4,64,512]{2,1,0:T(8,128)}) custom-call(s32[256]{0:T(256)} %cell_smem.5, s32[1,256]{1,0:T(1,128)} %bitcast.13, f32[256,256]{1,0:T(8,128)} %bitcast.16, f32[4,256,16,128]{3,2,1,0:T(8,128)} %state_ref.3), custom_call_target="tpu_custom_call" | custom-call | flops 4000000000 | bytes 20000000 | tf_op jit(solution)/shard_map/dynamics_rows/pallas_call | solution.py:555
  52.1 8.4 %all-to-all-done.1 = bf16[32,32,512]{2,1,0:T(8,128)(2,1)S(1)} async-done(((bf16[32,32,512]{2,1,0:T(8,128)(2,1)}), bf16[32,32,512]{2,1,0:T(8,128)(2,1)S(1)}, u32[]{:S(2)}, u32[]{:S(2)}) %all-to-all-start.1) | async-done | bytes 1048608 | tf_op jit(solution)/shard_map/all_to_all | solution.py:968
  60.5 0.0 copy-start
  60.5 4.3 %physics.1 = bf16[1024,512]{1,0:T(8,128)(2,1)S(1)} custom-call(bf16[1024,512]{1,0:T(8,128)(2,1)S(1)} %bitcast.9, s32[1,1024]{1,0:T(1,128)S(1)} %copy-done.10, bf16[64,128,128]{2,1,0:T(8,128)(2,1)S(1)} %copy-done.3), custom_call_target="tpu_custom_call" | custom-call | flops 3000000000 | bytes 5000000 | tf_op jit(solution)/shard_map/physics/pallas_call | solution.py:757
  64.8 29.3 %all_to_all.28 = bf16[32,32,512]{2,1,0:T(8,128)(2,1)S(1)} all-to-all(bf16[32,32,512]{2,1,0:T(8,128)(2,1)S(1)} %bitcast.11), channel_id=1, replica_groups=mesh['gx'=8,'gy'=4] {'gx','gy'}, dimensions={0} | all-to-all | bytes 2097152 | tf_op jit(solution)/shard_map/all_to_all | solution.py:968
  94.1 1.5 %unpack.1 = (bf16[1024,512]{1,0:T(8,128)(2,1)S(1)}, bf16[64,512]{1,0:T(8,128)(2,1)S(1)}, bf16[64,512]{1,0:T(8,128)(2,1)S(1)}, f32[64,512]{1,0:T(8,128)S(1)}, f32[64,512]{1,0:T(8,128)S(1)}) custom-call(bf16[1024,512]{1,0:T(8,128)(2,1)S(1)} %bitcast.10, s32[1,1024]{1,0:T(1,128)S(1)} %get-tuple-element.40.place_ref, f32[4,64,512]{2,1,0:T(8,128)S(1)} %copy-done.9, ...), custom_call_target="tpu_custom_call" | custom-call | flops 2000000000 | bytes 4000000 | tf_op jit(solution)/shard_map/unpack/pallas_call | solution.py:814
  95.6 2.7 %collective-permute-start.4 = (bf16[64,512]{1,0:T(8,128)(2,1)S(1)}, bf16[64,512]{1,0:T(8,128)(2,1)S(1)}, u32[]{:S(2)}, u32[]{:S(2)}) collective-permute-start(bf16[64,512]{1,0:T(8,128)(2,1)S(1)} %get-tuple-element.44), channel_id=1, source_target_pairs={{4,8},{12,16},{20,24},{28,0},{8,4},{16,12},{24,20},{0,28},{5,9},{1... | collective-permute-start | bytes 196616 | tf_op jit(solution)/shard_map/ppermute | solution.py:604
  98.3 0.0 copy-start.2
  98.4 2.5 %inner_sum.1.total.total_ref = f32[256,16,512]{2,1,0:T(8,128)S(1)} custom-call(f32[256,16,512]{2,1,0:T(8,128)S(1)} %bitcast.8, bf16[1024,512]{1,0:T(8,128)(2,1)S(1)} %get-tuple-element.42.back_ref, bf16[1024,256]{1,0:T(8,128)(2,1)S(1)} %copy-done), custom_call_target="tpu_custom_call", output_to_operand_aliasing={{}: (0, {})} | custom-call | flops 4000000000 | bytes 20000000 | tf_op jit(solution)/shard_map/inner_sum/pallas_call | solution.py:859
  100.9 0.2 line_messages.1
  101.1 2.7 %collective-permute-start.6 = (bf16[64,512]{1,0:T(8,128)(2,1)S(1)}, bf16[64,512]{1,0:T(8,128)(2,1)S(1)}, u32[]{:S(2)}, u32[]{:S(2)}) collective-permute-start(bf16[64,512]{1,0:T(8,128)(2,1)S(1)} %get-tuple-element.48), channel_id=1, source_target_pairs={{1,2},{3,0},{2,1},{0,3},{5,6},{7,4},{6,5},{4,7},{9,10},{11,8},{10,... | collective-permute-start | bytes 196616 | tf_op jit(solution)/shard_map/ppermute | solution.py:604
  103.7 0.1 collective-permute-start.7
  103.8 4.7 %to_slots.1 = (f32[4,256,16,128]{3,2,1,0:T(8,128)}, s32[1,256]{1,0:T(1,128)S(1)}) custom-call(s32[256]{0:T(256)S(1)} %copy-done.5, f32[256,16,512]{2,1,0:T(8,128)S(1)} %inner_sum.1.total.total_ref), custom_call_target="tpu_custom_call" | custom-call | flops 4000000000 | bytes 20000000 | tf_op jit(solution)/shard_map/to_slots/pallas_call | solution.py:901
  108.5 2.1 %border_sum.1 = f32[4,256,16,128]{3,2,1,0:T(8,128)} custom-call(s32[1,256]{1,0:T(1,128)S(1)} %get-tuple-element.43.slot_ref, bf16[64,512]{1,0:T(8,128)(2,1)S(1)} %collective-permute-done.6.y_two, bf16[64,512]{1,0:T(8,128)(2,1)S(1)} %collective-permute-done.7.y_one, bf16[64,512]{1,0:T(8,128)(2,1)S(1)} %collective-permute-done.4.x_two, ...), custom_call_target="tpu_custom_call", output_to_operand_aliasing={{}: (7, {})} | custom-call | flops 200000000 | bytes 4000000 | tf_op jit(solution)/shard_map/border_sum/pallas_call | solution.py:951
  (33 shorter events, 0.1 us)
Async XLA Ops:
  0.0 28.0 %copy-start.7 = (bf16[1024,128]{1,0:T(8,128)(2,1)S(1)}, bf16[1024,128]{1,0:T(8,128)(2,1)}, u32[]{:S(2)}) copy-start(bf16[1024,128]{1,0:T(8,128)(2,1)} %constant.10.clone.table_ref) | copy-start | bytes 786436
  0.0 28.0 %copy-start.4 = (s32[256]{0:T(256)S(1)}, s32[256]{0:T(256)}, u32[]{:S(2)}) copy-start(s32[256]{0:T(256)} %cell_smem.5) | copy-start | bytes 3076
  10.9 17.0 %all-to-all-start = ((bf16[32,8,128]{2,1,0:T(8,128)(2,1)}), bf16[32,8,128]{2,1,0:T(8,128)(2,1)S(1)}, u32[]{:S(2)}, u32[]{:S(2)}) async-start(bf16[32,8,128]{2,1,0:T(8,128)(2,1)} %get-tuple-element.33), calls=%async_computation | async-start | bytes 131072 | tf_op jit(solution)/shard_map/all_to_all | solution.py:968
  18.3 6.5 %collective-permute-start = (bf16[32,512]{1,0:T(8,128)(2,1)}, bf16[32,512]{1,0:T(8,128)(2,1)S(1)}, u32[]{:S(2)}, u32[]{:S(2)}) collective-permute-start(bf16[32,512]{1,0:T(8,128)(2,1)} %get-tuple-element.29), channel_id=1, source_target_pairs={{1,2},{3,0},{2,1},{0,3},{5,6},{7,4},{6,5},{4,7},{9,10},{11,8},{10,... | collective-permute-start | bytes 98312 | tf_op jit(solution)/shard_map/ppermute | solution.py:604
  21.9 4.8 %collective-permute-start.1 = (bf16[32,512]{1,0:T(8,128)(2,1)}, bf16[32,512]{1,0:T(8,128)(2,1)S(1)}, u32[]{:S(2)}, u32[]{:S(2)}) collective-permute-start(bf16[32,512]{1,0:T(8,128)(2,1)} %get-tuple-element.30), channel_id=1, source_target_pairs={{4,8},{12,16},{20,24},{28,0},{8,4},{16,12},{24,20},{0,28},{5,9},{1... | collective-permute-start | bytes 98312 | tf_op jit(solution)/shard_map/ppermute | solution.py:604
  23.8 4.1 %collective-permute-start.2 = (bf16[32,512]{1,0:T(8,128)(2,1)}, bf16[32,512]{1,0:T(8,128)(2,1)S(1)}, u32[]{:S(2)}, u32[]{:S(2)}) collective-permute-start(bf16[32,512]{1,0:T(8,128)(2,1)} %get-tuple-element.31), channel_id=1, source_target_pairs={{0,1},{2,3},{1,0},{3,2},{4,5},{6,7},{5,4},{7,6},{8,9},{10,11},{9,8... | collective-permute-start | bytes 98312 | tf_op jit(solution)/shard_map/ppermute | solution.py:605
  23.8 4.1 %collective-permute-start.3 = (bf16[32,512]{1,0:T(8,128)(2,1)}, bf16[32,512]{1,0:T(8,128)(2,1)S(1)}, u32[]{:S(2)}, u32[]{:S(2)}) collective-permute-start(bf16[32,512]{1,0:T(8,128)(2,1)} %get-tuple-element.32), channel_id=1, source_target_pairs={{0,4},{8,12},{16,20},{24,28},{4,0},{12,8},{20,16},{28,24},{1,5},{9... | collective-permute-start | bytes 98312 | tf_op jit(solution)/shard_map/ppermute | solution.py:605
  28.0 1.6 %copy-start.8 = (f32[1024,512]{1,0:T(8,128)S(1)}, f32[1024,512]{1,0:T(8,128)}, u32[]{:S(2)}) copy-start(f32[1024,512]{1,0:T(8,128)} %get-tuple-element.28.columns_ref) | copy-start | bytes 6291460
  32.7 27.8 %copy-start.3 = (bf16[64,128,128]{2,1,0:T(8,128)(2,1)S(1)}, bf16[64,128,128]{2,1,0:T(8,128)(2,1)}, u32[]{:S(2)}) copy-start(bf16[64,128,128]{2,1,0:T(8,128)(2,1)} %inverse_hbm.1) | copy-start | bytes 6291460
  32.7 27.8 %copy-start.10 = (s32[1,1024]{1,0:T(1,128)S(1)}, s32[1,1024]{1,0:T(1,128)}, u32[]{:S(2)}) copy-start(s32[1,1024]{1,0:T(1,128)} %get-tuple-element.39.q_ref) | copy-start | bytes 12292
  32.7 27.8 %all-to-all-start.1 = ((bf16[32,32,512]{2,1,0:T(8,128)(2,1)}), bf16[32,32,512]{2,1,0:T(8,128)(2,1)S(1)}, u32[]{:S(2)}, u32[]{:S(2)}) async-start(bf16[32,32,512]{2,1,0:T(8,128)(2,1)} %bitcast.3), calls=%async_computation.1 | async-start | bytes 2097152 | tf_op jit(solution)/shard_map/all_to_all | solution.py:968
  60.5 33.6 %copy-start.6 = (bf16[256,1024]{1,0:T(8,128)(2,1)S(1)}, bf16[256,1024]{1,0:T(8,128)(2,1)}, u32[]{:S(2)}) copy-start(bf16[256,1024]{1,0:T(8,128)(2,1)} %constant.11.clone.lines_table) | copy-start | bytes 1572868
  60.5 33.6 %copy-start.9 = (f32[4,64,512]{2,1,0:T(8,128)S(1)}, f32[4,64,512]{2,1,0:T(8,128)}, u32[]{:S(2)}) copy-start(f32[4,64,512]{2,1,0:T(8,128)} %get-tuple-element.41.own_lines) | copy-start | bytes 1572868
  60.5 37.8 %slice-start = ((s8[8388608]{0:T(1024)(128)(4,1)}), s8[4194304]{0:T(1024)(128)(4,1)S(1)}, s32[]{:S(2)}) async-start(s8[8388608]{0:T(1024)(128)(4,1)} %bitcast.7), calls=%async_computation.3 | async-start | bytes 8388608
  60.5 37.8 %slice-start.1 = ((s8[8388608]{0:T(1024)(128)(4,1)}), s8[4194304]{0:T(1024)(128)(4,1)S(1)}, s32[]{:S(2)}) async-start(s8[8388608]{0:T(1024)(128)(4,1)} %bitcast.7), calls=%async_computation.4 | async-start | bytes 8388608
  60.5 37.8 %copy-start = (bf16[1024,256]{1,0:T(8,128)(2,1)S(1)}, bf16[1024,256]{1,0:T(8,128)(2,1)}, u32[]{:S(2)}) copy-start(bf16[1024,256]{1,0:T(8,128)(2,1)} %constant.13.clone.table_ref) | copy-start | bytes 1572868
  95.6 5.2 %collective-permute-start.4 = (bf16[64,512]{1,0:T(8,128)(2,1)S(1)}, bf16[64,512]{1,0:T(8,128)(2,1)S(1)}, u32[]{:S(2)}, u32[]{:S(2)}) collective-permute-start(bf16[64,512]{1,0:T(8,128)(2,1)S(1)} %get-tuple-element.44), channel_id=1, source_target_pairs={{4,8},{12,16},{20,24},{28,0},{8,4},{16,12},{24,20},{0,28},{5,9},{1... | collective-permute-start | bytes 196616 | tf_op jit(solution)/shard_map/ppermute | solution.py:604
  98.3 2.5 %collective-permute-start.5 = (bf16[64,512]{1,0:T(8,128)(2,1)S(1)}, bf16[64,512]{1,0:T(8,128)(2,1)S(1)}, u32[]{:S(2)}, u32[]{:S(2)}) collective-permute-start(bf16[64,512]{1,0:T(8,128)(2,1)S(1)} %get-tuple-element.45), channel_id=1, source_target_pairs={{0,4},{8,12},{16,20},{24,28},{4,0},{12,8},{20,16},{28,24},{1,5},{9... | collective-permute-start | bytes 196616 | tf_op jit(solution)/shard_map/ppermute | solution.py:605
  98.3 2.5 %copy-start.2 = (bf16[128,128]{1,0:T(8,128)(2,1)S(1)}, bf16[128,128]{1,0:T(8,128)(2,1)}, u32[]{:S(2)}) copy-start(bf16[128,128]{1,0:T(8,128)(2,1)} %constant.12.clone.table) | copy-start | bytes 98308
  98.3 5.5 %copy-start.5 = (s32[256]{0:T(256)S(1)}, s32[256]{0:T(256)}, u32[]{:S(2)}) copy-start(s32[256]{0:T(256)} %cell_smem.5) | copy-start | bytes 3076
  100.8 7.7 %copy-start.1 = (bf16[1024,64]{1,0:T(8,128)(2,1)S(1)}, bf16[1024,64]{1,0:T(8,128)(2,1)}, u32[]{:S(2)}) copy-start(bf16[1024,64]{1,0:T(8,128)(2,1)} %constant.14.clone.table_ref) | copy-start | bytes 393220
  101.1 7.4 %collective-permute-start.6 = (bf16[64,512]{1,0:T(8,128)(2,1)S(1)}, bf16[64,512]{1,0:T(8,128)(2,1)S(1)}, u32[]{:S(2)}, u32[]{:S(2)}) collective-permute-start(bf16[64,512]{1,0:T(8,128)(2,1)S(1)} %get-tuple-element.48), channel_id=1, source_target_pairs={{1,2},{3,0},{2,1},{0,3},{5,6},{7,4},{6,5},{4,7},{9,10},{11,8},{10,... | collective-permute-start | bytes 196616 | tf_op jit(solution)/shard_map/ppermute | solution.py:604
  103.7 4.8 %collective-permute-start.7 = (bf16[64,512]{1,0:T(8,128)(2,1)S(1)}, bf16[64,512]{1,0:T(8,128)(2,1)S(1)}, u32[]{:S(2)}, u32[]{:S(2)}) collective-permute-start(bf16[64,512]{1,0:T(8,128)(2,1)S(1)} %get-tuple-element.49), channel_id=1, source_target_pairs={{0,1},{2,3},{1,0},{3,2},{4,5},{6,7},{5,4},{7,6},{8,9},{10,11},{9,8... | collective-permute-start | bytes 196616 | tf_op jit(solution)/shard_map/ppermute | solution.py:605

commit v5 on v4

--- a/solution.py
+++ b/solution.py
@@ -260,7 +260,7 @@
                     lo_ref[where, :, f * levels : (f + 1) * levels] = lo
             return 0
 
-        lax.fori_loop(0, per // 4, place_slots, 0, unroll=2)
+        lax.fori_loop(0, per // 4, place_slots, 0, unroll=4)
 
 
 def row_points(row, operators, hi_ref, lo_ref):
@@ -392,7 +392,7 @@
         rows = (pl.ds(0, 576), pl.ds(576, 256), pl.ds(832, 192))[part]
         return pltpu.make_async_copy(columns.at[rows], columns_out.at[rows], out_sem.at[part])
 
-    lax.fori_loop(0, 10, one_row, 0, unroll=5)
+    lax.fori_loop(0, 10, one_row, 0, unroll=10)
     send(0).start()
     lax.fori_loop(10, 14, one_row, 0, unroll=4)
     send(1).start()
@@ -615,25 +615,18 @@
     return jnp.where(even, two, one), jnp.where(even, one, two)
 
 
-def send_kernel(
+def places_kernel(
     sizes,
     span_y,
-    columns_ref,
-    table_ref,
-    y_two,
-    x_two,
-    y_one,
-    x_one,
+    columns_in,
     blocks_in,
     cell_ref,
-    out_ref,
+    columns_ref,
+    pick,
     place_ref,
-    lines_ref,
     blocks_ref,
-    rounded,
-    pick,
 ):
-    count, width = columns_ref.shape
+    count = pick.shape[0]
     devices = sizes[0] * sizes[1]
     per_peer = count // devices
     blocks_ref[...] = blocks_in[...].astype(F32)
@@ -658,6 +651,41 @@
                 column == iota((128, 128), 1) + other
             )
 
+
+def send_places(columns, blocks, cell, sizes):
+    count, width = columns.shape
+    return pl.pallas_call(
+        functools.partial(places_kernel, sizes, EYD * sizes[1]),
+        out_shape=(
+            jax.ShapeDtypeStruct((count, width), F32),
+            jax.ShapeDtypeStruct((count, count), BF16),
+            jax.ShapeDtypeStruct((1, count), I32),
+            jax.ShapeDtypeStruct(blocks.shape, F32),
+        ),
+        in_specs=[VMEM] * 3,
+        out_specs=(VMEM,) * 4,
+        input_output_aliases={0: 0},
+        compiler_params=params(16),
+        cost_estimate=cost(4e9, 2e7),
+        name="send_places",
+    )(columns, blocks, cell)
+
+
+def send_kernel(
+    sizes,
+    columns_ref,
+    pick,
+    blocks_ref,
+    table_ref,
+    y_two,
+    y_one,
+    x_two,
+    x_one,
+    out_ref,
+    lines_ref,
+    rounded,
+):
+    count, width = columns_ref.shape
     lines_ref[0], lines_ref[1] = from_neighbours(
         "gy", y_one[...].astype(F32), y_two[...].astype(F32)
     )
@@ -685,27 +713,22 @@
     out_ref[...] = dot(pick[...], rounded[...]).astype(BF16)
 
 
-def send_columns(columns, halos, blocks, cell, sizes):
+def send_columns(columns, pick, blocks, halos, sizes):
     count, width = columns.shape
     table = np.concatenate(hi_lo_arrays(TABLES["col_y"]), axis=1)
     return pl.pallas_call(
-        functools.partial(send_kernel, sizes, EYD * sizes[1]),
-        out_shape=(
-            jax.ShapeDtypeStruct((count, width), BF16),
-            jax.ShapeDtypeStruct((1, count), I32),
-        ),
+        functools.partial(send_kernel, sizes),
+        out_shape=jax.ShapeDtypeStruct((count, width), BF16),
         in_specs=[VMEM] * 8,
-        out_specs=(VMEM,) * 2,
+        out_specs=VMEM,
         scratch_shapes=[
             pltpu.VMEM((2, 32, width), F32),
-            pltpu.VMEM(blocks.shape, F32),
             pltpu.VMEM((count, width), BF16),
-            pltpu.VMEM((count, count), BF16),
         ],
         compiler_params=params(SEND_LIMIT),
         cost_estimate=cost(2e9, 5e6),
         name="send_columns",
-    )(columns, jnp.asarray(table), halos[3], halos[1], halos[2], halos[0], blocks, cell)
+    )(columns, pick, blocks, jnp.asarray(table), halos[3], halos[2], halos[1], halos[0])
 
 
 SEND_LIMIT = 16
@@ -889,7 +912,7 @@
                     buffer[chunk, f, k] = total[tile, :, f * levels : (f + 1) * levels]
             return 0
 
-        lax.fori_loop(0, per // 4, take_slots, 0)
+        lax.fori_loop(0, per // 4, take_slots, 0, unroll=4)
         copy(chunk).start()
     for chunk in range(CHUNKS):
         copy(chunk).wait()
@@ -982,9 +1005,10 @@
     hx = exchange("gx", x_one, x_two)
     blocks = regroup(blocks)
 
-    outgoing, place = send_columns(
-        columns, (*hx, *hy), blocks, elem_cell.reshape(1, elements), sizes
-    )
+    columns, pick, place, blocks = send_places(
+        columns, blocks, elem_cell.reshape(1, elements), sizes
+    )
+    outgoing = send_columns(columns, pick, blocks, (*hx, *hy), sizes)
     incoming = regroup(outgoing)
     dynamics, own_lines = dynamics_rows(elem_cell, stiff, state_in, span_y)
     incoming, dynamics, own_lines = lax.optimization_barrier((incoming, dynamics, own_lines))

time: 111 us -> 109 us (0.982)
  waiting for transfers between devices: 12.5 us -> 10.6 us
    ppermute x4, waiting for transfers between devices: 2.9 us -> 0.01 us  [exchange(): second = lax.ppermute(two, axis, pairs(axis, False))]
    all_to_all x2, waiting for transfers between devices: 8.38 us -> 10.6 us  [regroup(): lax.all_to_all(blocks, ('gx', 'gy'), split_axis=0, concat_axis=0, tiled=T...]
    ppermute x4, waiting for transfers between devices: 1.24 us -> 0.01 us  [exchange(): return (lax.ppermute(one, axis, pairs(axis, True)), second)]
    pallas_call x1 -> x2, Pallas kernels: 3.09 us -> 3.55 us  [the longest x1 2.53 us: send_columns(): pl.pallas_call(functools.partial(send_kernel, sizes), out_shape=jax.Shape...]
  transfers between devices with their start and end apart: 10 -> 10, of which waited for: 4 -> 2; matrix products, arithmetic and copies ran while one was open for 0% -> 0% of each run, Pallas kernels for 21% -> 23%
where the time goes in v5:
time: 109 us
  Pallas kernels  45.9 us (42%)
  blocking collectives  29.3 us (27%)
  starting transfers between devices  21.3 us (20%)
  waiting for transfers between devices  10.6 us (10%)
  local copies, waits for them, and re-layouts  1.65 us (2%)
    all_to_all x1, blocking collectives, regroup(): lax.all_to_all(blocks, ('gx', 'gy'), split_axis=0, concat_axis=0, tiled=T...  29.3 us
    pallas_call x1, Pallas kernels, dynamics_rows(): pl.pallas_call(functools.partial(dynamics_kernel, span_y), out_shape=(jax...  16.5 us
    ppermute x4, starting transfers between devices, exchange(): second = lax.ppermute(two, axis, pairs(axis, False))  10.9 us
    pallas_call x1, Pallas kernels, front(): pl.pallas_call(functools.partial(front_kernel, sizes, EYD * sizes[1]), ou...  10.7 us
    all_to_all x2, waiting for transfers between devices, regroup(): lax.all_to_all(blocks, ('gx', 'gy'), split_axis=0, concat_axis=0, tiled=T...  10.6 us
    all_to_all x2, starting transfers between devices, regroup(): lax.all_to_all(blocks, ('gx', 'gy'), split_axis=0, concat_axis=0, tiled=T...  10.3 us
    pallas_call x1, Pallas kernels, to_slots(): pl.pallas_call(functools.partial(to_slots_kernel, span_y), out_shape=(jax...  4.61 us
    pallas_call x1, Pallas kernels, physics_step(): pl.pallas_call(functools.partial(physics_kernel, fields), out_shape=jax.S...  4.27 us
  transfers between devices with their start and end apart: 10, of which 2 were waited for; matrix products, arithmetic and copies ran while one was open for 0% of the time, Pallas kernels for 23%

profile of v5, /device:TPU:0, one launch (start us, length us, event | category | flops | bytes accessed | tf_op | source)
XLA Modules:
  0.0 109.2 jit_solution(9040642376815949083)
XLA Ops:
  0.0 10.7 %front.1 = (f32[1024,512]{1,0:T(8,128)}, bf16[32,8,128]{2,1,0:T(8,128)(2,1)}, s32[1,1024]{1,0:T(1,128)}, bf16[32,512]{1,0:T(8,128)(2,1)}, bf16[32,512]{1,0:T(8,1...) custom-call(s32[256]{0:T(256)} %cell_smem.5, s32[1,256]{1,0:T(1,128)} %bitcast.12, s32[1,1024]{1,0:T(1,128)} %bitcast.17, ...), custom_call_target="tpu_custom_call" | custom-call | flops 4000000000 | bytes 20000000 | tf_op jit(solution)/shard_map/front/pallas_call | solution.py:442
  10.7 0.0 copy-start.7
  10.7 7.3 %all-to-all-start = ((bf16[32,8,128]{2,1,0:T(8,128)(2,1)}), bf16[32,8,128]{2,1,0:T(8,128)(2,1)S(1)}, u32[]{:S(2)}, u32[]{:S(2)}) async-start(bf16[32,8,128]{2,1,0:T(8,128)(2,1)} %get-tuple-element.31), calls=%async_computation | async-start | bytes 131072 | tf_op jit(solution)/shard_map/all_to_all | solution.py:991
  18.0 3.7 %collective-permute-start = (bf16[32,512]{1,0:T(8,128)(2,1)}, bf16[32,512]{1,0:T(8,128)(2,1)S(1)}, u32[]{:S(2)}, u32[]{:S(2)}) collective-permute-start(bf16[32,512]{1,0:T(8,128)(2,1)} %get-tuple-element.35), channel_id=1, source_target_pairs={{1,2},{3,0},{2,1},{0,3},{5,6},{7,4},{6,5},{4,7},{9,10},{11,8},{10,... | collective-permute-start | bytes 98312 | tf_op jit(solution)/shard_map/ppermute | solution.py:604
  21.7 1.9 %collective-permute-start.2 = (bf16[32,512]{1,0:T(8,128)(2,1)}, bf16[32,512]{1,0:T(8,128)(2,1)S(1)}, u32[]{:S(2)}, u32[]{:S(2)}) collective-permute-start(bf16[32,512]{1,0:T(8,128)(2,1)} %get-tuple-element.37), channel_id=1, source_target_pairs={{4,8},{12,16},{20,24},{28,0},{8,4},{16,12},{24,20},{0,28},{5,9},{1... | collective-permute-start | bytes 98312 | tf_op jit(solution)/shard_map/ppermute | solution.py:604
  23.6 2.3 %all-to-all-done.blocks_in = bf16[32,8,128]{2,1,0:T(8,128)(2,1)S(1)} async-done(((bf16[32,8,128]{2,1,0:T(8,128)(2,1)}), bf16[32,8,128]{2,1,0:T(8,128)(2,1)S(1)}, u32[]{:S(2)}, u32[]{:S(2)}) %all-to-all-start) | async-done | bytes 65568 | tf_op jit(solution)/shard_map/all_to_all | solution.py:991
  25.8 1.6 %copy-done.8 = f32[1024,512]{1,0:T(8,128)S(1)} copy-done((f32[1024,512]{1,0:T(8,128)S(1)}, f32[1024,512]{1,0:T(8,128)}, u32[]{:S(2)}) %copy-start.8) | copy-done | bytes 2097176
  27.4 1.0 send_places.1
  28.5 2.5 %send_columns.1 = bf16[1024,512]{1,0:T(8,128)(2,1)} custom-call(f32[1024,512]{1,0:T(8,128)S(1)} %get-tuple-element.32.columns_ref, bf16[1024,1024]{1,0:T(8,128)(2,1)S(1)} %get-tuple-element.33.pick, f32[32,8,128]{2,1,0:T(8,128)S(1)} %get-tuple-element.34.blocks_ref, bf16[1024,128]{1,0:T(8,128)(2,1)S(1)} %copy-done.7, ...), custom_call_target="tpu_custom_call" | custom-call | flops 2000000000 | bytes 5000000 | tf_op jit(solution)/shard_map/send_columns/pallas_call | solution.py:719
  31.0 3.0 %all-to-all-start.1 = ((bf16[32,32,512]{2,1,0:T(8,128)(2,1)}), bf16[32,32,512]{2,1,0:T(8,128)(2,1)S(1)}, u32[]{:S(2)}, u32[]{:S(2)}) async-start(bf16[32,32,512]{2,1,0:T(8,128)(2,1)} %bitcast.3), calls=%async_computation.1 | async-start | bytes 2097152 | tf_op jit(solution)/shard_map/all_to_all | solution.py:991
  34.0 16.5 %dynamics_rows.1 = (f32[256,16,512]{2,1,0:T(8,128)}, f32[4,64,512]{2,1,0:T(8,128)}) custom-call(s32[256]{0:T(256)} %cell_smem.5, s32[1,256]{1,0:T(1,128)} %bitcast.13, f32[256,256]{1,0:T(8,128)} %bitcast.16, f32[4,256,16,128]{3,2,1,0:T(8,128)} %state_ref.3), custom_call_target="tpu_custom_call" | custom-call | flops 4000000000 | bytes 20000000 | tf_op jit(solution)/shard_map/dynamics_rows/pallas_call | solution.py:555
  50.5 8.4 %all-to-all-done.1 = bf16[32,32,512]{2,1,0:T(8,128)(2,1)S(1)} async-done(((bf16[32,32,512]{2,1,0:T(8,128)(2,1)}), bf16[32,32,512]{2,1,0:T(8,128)(2,1)S(1)}, u32[]{:S(2)}, u32[]{:S(2)}) %all-to-all-start.1) | async-done | bytes 1048608 | tf_op jit(solution)/shard_map/all_to_all | solution.py:991
  58.9 0.0 slice-start.1
  58.9 0.0 copy-start
  58.9 4.3 %physics.1 = bf16[1024,512]{1,0:T(8,128)(2,1)S(1)} custom-call(bf16[1024,512]{1,0:T(8,128)(2,1)S(1)} %bitcast.9, s32[1,1024]{1,0:T(1,128)S(1)} %copy-done.10, bf16[64,128,128]{2,1,0:T(8,128)(2,1)S(1)} %copy-done.3), custom_call_target="tpu_custom_call" | custom-call | flops 3000000000 | bytes 5000000 | tf_op jit(solution)/shard_map/physics/pallas_call | solution.py:780
  63.2 29.3 %all_to_all.28 = bf16[32,32,512]{2,1,0:T(8,128)(2,1)S(1)} all-to-all(bf16[32,32,512]{2,1,0:T(8,128)(2,1)S(1)} %bitcast.11), channel_id=1, replica_groups=mesh['gx'=8,'gy'=4] {'gx','gy'}, dimensions={0} | all-to-all | bytes 2097152 | tf_op jit(solution)/shard_map/all_to_all | solution.py:991
  92.5 1.5 %unpack.1 = (bf16[1024,512]{1,0:T(8,128)(2,1)S(1)}, bf16[64,512]{1,0:T(8,128)(2,1)S(1)}, bf16[64,512]{1,0:T(8,128)(2,1)S(1)}, f32[64,512]{1,0:T(8,128)S(1)}, f32[64,512]{1,0:T(8,128)S(1)}) custom-call(bf16[1024,512]{1,0:T(8,128)(2,1)S(1)} %bitcast.10, s32[1,1024]{1,0:T(1,128)S(1)} %get-tuple-element.44.place_ref, f32[4,64,512]{2,1,0:T(8,128)S(1)} %copy-done.9, ...), custom_call_target="tpu_custom_call" | custom-call | flops 2000000000 | bytes 4000000 | tf_op jit(solution)/shard_map/unpack/pallas_call | solution.py:837
  94.0 2.7 %collective-permute-start.4 = (bf16[64,512]{1,0:T(8,128)(2,1)S(1)}, bf16[64,512]{1,0:T(8,128)(2,1)S(1)}, u32[]{:S(2)}, u32[]{:S(2)}) collective-permute-start(bf16[64,512]{1,0:T(8,128)(2,1)S(1)} %get-tuple-element.48), channel_id=1, source_target_pairs={{4,8},{12,16},{20,24},{28,0},{8,4},{16,12},{24,20},{0,28},{5,9},{1... | collective-permute-start | bytes 196616 | tf_op jit(solution)/shard_map/ppermute | solution.py:604
  96.7 2.5 %inner_sum.1.total.total_ref = f32[256,16,512]{2,1,0:T(8,128)S(1)} custom-call(f32[256,16,512]{2,1,0:T(8,128)S(1)} %bitcast.8, bf16[1024,512]{1,0:T(8,128)(2,1)S(1)} %get-tuple-element.46.back_ref, bf16[1024,256]{1,0:T(8,128)(2,1)S(1)} %copy-done), custom_call_target="tpu_custom_call", output_to_operand_aliasing={{}: (0, {})} | custom-call | flops 4000000000 | bytes 20000000 | tf_op jit(solution)/shard_map/inner_sum/pallas_call | solution.py:882
  99.3 0.2 line_messages.1
  99.5 2.6 %collective-permute-start.6 = (bf16[64,512]{1,0:T(8,128)(2,1)S(1)}, bf16[64,512]{1,0:T(8,128)(2,1)S(1)}, u32[]{:S(2)}, u32[]{:S(2)}) collective-permute-start(bf16[64,512]{1,0:T(8,128)(2,1)S(1)} %get-tuple-element.52), channel_id=1, source_target_pairs={{1,2},{3,0},{2,1},{0,3},{5,6},{7,4},{6,5},{4,7},{9,10},{11,8},{10,... | collective-permute-start | bytes 196616 | tf_op jit(solution)/shard_map/ppermute | solution.py:604
  102.1 0.1 collective-permute-start.7
  102.2 4.6 %to_slots.1 = (f32[4,256,16,128]{3,2,1,0:T(8,128)}, s32[1,256]{1,0:T(1,128)S(1)}) custom-call(s32[256]{0:T(256)S(1)} %copy-done.5, f32[256,16,512]{2,1,0:T(8,128)S(1)} %inner_sum.1.total.total_ref), custom_call_target="tpu_custom_call" | custom-call | flops 4000000000 | bytes 20000000 | tf_op jit(solution)/shard_map/to_slots/pallas_call | solution.py:924
  106.9 2.1 %border_sum.1 = f32[4,256,16,128]{3,2,1,0:T(8,128)} custom-call(s32[1,256]{1,0:T(1,128)S(1)} %get-tuple-element.47.slot_ref, bf16[64,512]{1,0:T(8,128)(2,1)S(1)} %collective-permute-done.6.y_two, bf16[64,512]{1,0:T(8,128)(2,1)S(1)} %collective-permute-done.7.y_one, bf16[64,512]{1,0:T(8,128)(2,1)S(1)} %collective-permute-done.4.x_two, ...), custom_call_target="tpu_custom_call", output_to_operand_aliasing={{}: (7, {})} | custom-call | flops 200000000 | bytes 4000000 | tf_op jit(solution)/shard_map/border_sum/pallas_call | solution.py:974
  (34 shorter events, 0.1 us)
Async XLA Ops:
  0.0 25.8 %copy-start.4 = (s32[256]{0:T(256)S(1)}, s32[256]{0:T(256)}, u32[]{:S(2)}) copy-start(s32[256]{0:T(256)} %cell_smem.5) | copy-start | bytes 3076
  10.7 17.8 %copy-start.7 = (bf16[1024,128]{1,0:T(8,128)(2,1)S(1)}, bf16[1024,128]{1,0:T(8,128)(2,1)}, u32[]{:S(2)}) copy-start(bf16[1024,128]{1,0:T(8,128)(2,1)} %constant.10.clone.table_ref) | copy-start | bytes 786436
  10.7 15.2 %all-to-all-start = ((bf16[32,8,128]{2,1,0:T(8,128)(2,1)}), bf16[32,8,128]{2,1,0:T(8,128)(2,1)S(1)}, u32[]{:S(2)}, u32[]{:S(2)}) async-start(bf16[32,8,128]{2,1,0:T(8,128)(2,1)} %get-tuple-element.31), calls=%async_computation | async-start | bytes 131072 | tf_op jit(solution)/shard_map/all_to_all | solution.py:991
  18.0 10.5 %collective-permute-start = (bf16[32,512]{1,0:T(8,128)(2,1)}, bf16[32,512]{1,0:T(8,128)(2,1)S(1)}, u32[]{:S(2)}, u32[]{:S(2)}) collective-permute-start(bf16[32,512]{1,0:T(8,128)(2,1)} %get-tuple-element.35), channel_id=1, source_target_pairs={{1,2},{3,0},{2,1},{0,3},{5,6},{7,4},{6,5},{4,7},{9,10},{11,8},{10,... | collective-permute-start | bytes 98312 | tf_op jit(solution)/shard_map/ppermute | solution.py:604
  21.7 6.8 %collective-permute-start.1 = (bf16[32,512]{1,0:T(8,128)(2,1)}, bf16[32,512]{1,0:T(8,128)(2,1)S(1)}, u32[]{:S(2)}, u32[]{:S(2)}) collective-permute-start(bf16[32,512]{1,0:T(8,128)(2,1)} %get-tuple-element.36), channel_id=1, source_target_pairs={{0,1},{2,3},{1,0},{3,2},{4,5},{6,7},{5,4},{7,6},{8,9},{10,11},{9,8... | collective-permute-start | bytes 98312 | tf_op jit(solution)/shard_map/ppermute | solution.py:605
  21.7 6.8 %collective-permute-start.2 = (bf16[32,512]{1,0:T(8,128)(2,1)}, bf16[32,512]{1,0:T(8,128)(2,1)S(1)}, u32[]{:S(2)}, u32[]{:S(2)}) collective-permute-start(bf16[32,512]{1,0:T(8,128)(2,1)} %get-tuple-element.37), channel_id=1, source_target_pairs={{4,8},{12,16},{20,24},{28,0},{8,4},{16,12},{24,20},{0,28},{5,9},{1... | collective-permute-start | bytes 98312 | tf_op jit(solution)/shard_map/ppermute | solution.py:604
  23.6 4.9 %collective-permute-start.3 = (bf16[32,512]{1,0:T(8,128)(2,1)}, bf16[32,512]{1,0:T(8,128)(2,1)S(1)}, u32[]{:S(2)}, u32[]{:S(2)}) collective-permute-start(bf16[32,512]{1,0:T(8,128)(2,1)} %get-tuple-element.38), channel_id=1, source_target_pairs={{0,4},{8,12},{16,20},{24,28},{4,0},{12,8},{20,16},{28,24},{1,5},{9... | collective-permute-start | bytes 98312 | tf_op jit(solution)/shard_map/ppermute | solution.py:605
  25.8 1.6 %copy-start.8 = (f32[1024,512]{1,0:T(8,128)S(1)}, f32[1024,512]{1,0:T(8,128)}, u32[]{:S(2)}) copy-start(f32[1024,512]{1,0:T(8,128)} %get-tuple-element.30.columns_in) | copy-start | bytes 6291460
  31.0 27.8 %copy-start.3 = (bf16[64,128,128]{2,1,0:T(8,128)(2,1)S(1)}, bf16[64,128,128]{2,1,0:T(8,128)(2,1)}, u32[]{:S(2)}) copy-start(bf16[64,128,128]{2,1,0:T(8,128)(2,1)} %inverse_hbm.1) | copy-start | bytes 6291460
  31.0 27.8 %copy-start.10 = (s32[1,1024]{1,0:T(1,128)S(1)}, s32[1,1024]{1,0:T(1,128)}, u32[]{:S(2)}) copy-start(s32[1,1024]{1,0:T(1,128)} %get-tuple-element.43.q_ref) | copy-start | bytes 12292
  31.0 27.8 %all-to-all-start.1 = ((bf16[32,32,512]{2,1,0:T(8,128)(2,1)}), bf16[32,32,512]{2,1,0:T(8,128)(2,1)S(1)}, u32[]{:S(2)}, u32[]{:S(2)}) async-start(bf16[32,32,512]{2,1,0:T(8,128)(2,1)} %bitcast.3), calls=%async_computation.1 | async-start | bytes 2097152 | tf_op jit(solution)/shard_map/all_to_all | solution.py:991
  58.9 33.6 %copy-start.6 = (bf16[256,1024]{1,0:T(8,128)(2,1)S(1)}, bf16[256,1024]{1,0:T(8,128)(2,1)}, u32[]{:S(2)}) copy-start(bf16[256,1024]{1,0:T(8,128)(2,1)} %constant.11.clone.lines_table) | copy-start | bytes 1572868
  58.9 33.6 %copy-start.9 = (f32[4,64,512]{2,1,0:T(8,128)S(1)}, f32[4,64,512]{2,1,0:T(8,128)}, u32[]{:S(2)}) copy-start(f32[4,64,512]{2,1,0:T(8,128)} %get-tuple-element.45.own_lines) | copy-start | bytes 1572868
  58.9 37.8 %slice-start = ((s8[8388608]{0:T(1024)(128)(4,1)}), s8[4194304]{0:T(1024)(128)(4,1)S(1)}, s32[]{:S(2)}) async-start(s8[8388608]{0:T(1024)(128)(4,1)} %bitcast.7), calls=%async_computation.3 | async-start | bytes 8388608
  58.9 37.8 %slice-start.1 = ((s8[8388608]{0:T(1024)(128)(4,1)}), s8[4194304]{0:T(1024)(128)(4,1)S(1)}, s32[]{:S(2)}) async-start(s8[8388608]{0:T(1024)(128)(4,1)} %bitcast.7), calls=%async_computation.4 | async-start | bytes 8388608
  58.9 37.8 %copy-start = (bf16[1024,256]{1,0:T(8,128)(2,1)S(1)}, bf16[1024,256]{1,0:T(8,128)(2,1)}, u32[]{:S(2)}) copy-start(bf16[1024,256]{1,0:T(8,128)(2,1)} %constant.13.clone.table_ref) | copy-start | bytes 1572868
  94.0 5.2 %collective-permute-start.4 = (bf16[64,512]{1,0:T(8,128)(2,1)S(1)}, bf16[64,512]{1,0:T(8,128)(2,1)S(1)}, u32[]{:S(2)}, u32[]{:S(2)}) collective-permute-start(bf16[64,512]{1,0:T(8,128)(2,1)S(1)} %get-tuple-element.48), channel_id=1, source_target_pairs={{4,8},{12,16},{20,24},{28,0},{8,4},{16,12},{24,20},{0,28},{5,9},{1... | collective-permute-start | bytes 196616 | tf_op jit(solution)/shard_map/ppermute | solution.py:604
  96.7 2.6 %collective-permute-start.5 = (bf16[64,512]{1,0:T(8,128)(2,1)S(1)}, bf16[64,512]{1,0:T(8,128)(2,1)S(1)}, u32[]{:S(2)}, u32[]{:S(2)}) collective-permute-start(bf16[64,512]{1,0:T(8,128)(2,1)S(1)} %get-tuple-element.49), channel_id=1, source_target_pairs={{0,4},{8,12},{16,20},{24,28},{4,0},{12,8},{20,16},{28,24},{1,5},{9... | collective-permute-start | bytes 196616 | tf_op jit(solution)/shard_map/ppermute | solution.py:605
  96.7 2.5 %copy-start.2 = (bf16[128,128]{1,0:T(8,128)(2,1)S(1)}, bf16[128,128]{1,0:T(8,128)(2,1)}, u32[]{:S(2)}) copy-start(bf16[128,128]{1,0:T(8,128)(2,1)} %constant.12.clone.table) | copy-start | bytes 98308
  96.7 5.5 %copy-start.5 = (s32[256]{0:T(256)S(1)}, s32[256]{0:T(256)}, u32[]{:S(2)}) copy-start(s32[256]{0:T(256)} %cell_smem.5) | copy-start | bytes 3076
  99.2 7.6 %copy-start.1 = (bf16[1024,64]{1,0:T(8,128)(2,1)S(1)}, bf16[1024,64]{1,0:T(8,128)(2,1)}, u32[]{:S(2)}) copy-start(bf16[1024,64]{1,0:T(8,128)(2,1)} %constant.14.clone.table_ref) | copy-start | bytes 393220
  99.5 7.4 %collective-permute-start.6 = (bf16[64,512]{1,0:T(8,128)(2,1)S(1)}, bf16[64,512]{1,0:T(8,128)(2,1)S(1)}, u32[]{:S(2)}, u32[]{:S(2)}) collective-permute-start(bf16[64,512]{1,0:T(8,128)(2,1)S(1)} %get-tuple-element.52), channel_id=1, source_target_pairs={{1,2},{3,0},{2,1},{0,3},{5,6},{7,4},{6,5},{4,7},{9,10},{11,8},{10,... | collective-permute-start | bytes 196616 | tf_op jit(solution)/shard_map/ppermute | solution.py:604
  102.1 4.8 %collective-permute-start.7 = (bf16[64,512]{1,0:T(8,128)(2,1)S(1)}, bf16[64,512]{1,0:T(8,128)(2,1)S(1)}, u32[]{:S(2)}, u32[]{:S(2)}) collective-permute-start(bf16[64,512]{1,0:T(8,128)(2,1)S(1)} %get-tuple-element.53), channel_id=1, source_target_pairs={{0,1},{2,3},{1,0},{3,2},{4,5},{6,7},{5,4},{7,6},{8,9},{10,11},{9,8... | collective-permute-start | bytes 196616 | tf_op jit(solution)/shard_map/ppermute | solution.py:605
